TPU v7x, 256 devices: a whole 4x4x8 slice. The times are simulated.
256 devices in a mesh: layer: 64 (over y, x, z_lo, core), batch: 4 (over z_hi).
Axes of the slice: x: 4, y: 4, z: 8 (z_hi: 4, z_lo: 2; z = z_hi * 2 + z_lo), core: 2. Of those that a mesh axis runs over, the one named last changes fastest.
Arguments:
- images: bfloat16 [32, 4, 4, 512], P('batch'), parts along dimension 0, may hold values from -6 to 6
- weights: bfloat16 [128, 4608, 512], P('layer'), may hold values from -0.25 to 0.25
- biases: float32 [128, 512], P('layer'), may hold values from -3 to 3
Outputs:
- states: float32 [128, 32, 4, 4, 512], P('layer', 'batch'), parts along dimension 1
There are 4 independent parts, one for each index of `batch`. A program takes and returns all parts, laid end to end along the dimension named above; an argument that names none is the same for every part. Nothing has to cross between parts.
All inputs are finite; a program needn't handle non-finite values.
Results may differ from a plain program's by a relative error of at most 0.015.
Values sent between devices are 32-bit elements; how exact they have to be, the bound alone decides.
No kernel may reach another device: no remote copies, remote signals or barrier semaphores. Data moves between devices by JAX's collectives and lax.ppermute only.
A program may use at most 64 MiB of HBM per device.

v0:
```python
import jax
import jax.numpy as jnp
from jax import lax
from jax.sharding import PartitionSpec as P

step_size = 0.25


def shifted_2(block, axis, distance):
    devices = range(lax.axis_size(axis))
    route = [(i - distance, i) for i in devices if i - distance in devices]
    return lax.ppermute(block, axis, route)


def fine_step(field, weight, bias):
    channels = field.shape[-1]
    height = field.shape[1]
    breadth = field.shape[2]
    lowered = field.astype(jnp.bfloat16)
    padded = jnp.pad(lowered, ((0, 0), (1, 1), (1, 1), (0, 0)))
    pieces = [
        padded[:, row_shift : row_shift + height, col_shift : col_shift + breadth, :]
        for row_shift in range(3)
        for col_shift in range(3)
    ]
    stacked = jnp.concatenate(pieces, axis=-1).reshape(-1, 9 * channels)
    mixed = jnp.dot(stacked, weight, preferred_element_type=jnp.float32).reshape(field.shape) + bias
    return field + step_size * jnp.tanh(mixed)


def coarse_step(field, weight, bias):
    channels = field.shape[-1]
    lowered = field.astype(jnp.bfloat16).reshape(-1, channels)
    centre = weight[4 * channels : 5 * channels]
    mixed = jnp.dot(lowered, centre, preferred_element_type=jnp.float32).reshape(field.shape) + bias
    return field + 2.0 * step_size * jnp.tanh(mixed)


def shards(images, weights, biases):
    initial = images.astype(jnp.float32)
    position = lax.axis_index("layer")
    is_head = position == 0
    guessed = fine_step(fine_step(initial, weights[0], biases[0]), weights[1], biases[1])
    incoming = shifted_2(guessed, "layer", 1)
    shifted = jnp.where(is_head, initial, incoming)
    relaxed = fine_step(shifted, weights[0], biases[0])
    forcing = fine_step(relaxed, weights[1], biases[1]) - coarse_step(
        shifted, weights[0], biases[0]
    )
    group_count = 1
    group_rows = initial.shape[0] // group_count
    blocks = lax.axis_size("layer")

    def advance(turn_index, state_tuple):
        outgoing, solved, received = state_tuple
        arrived = shifted_2(outgoing, "layer", 1)
        group_index = turn_index - position
        in_range = (group_index >= 0) & (group_index < group_count)
        entry = jnp.where(is_head, initial, arrived)

        def update(entry_state):
            solved_rows = coarse_step(entry_state, weights[0], biases[0]) + forcing
            return (solved_rows, solved_rows, entry_state)

        def hold(entry_state):
            return (outgoing, solved, received)

        return lax.cond(in_range, update, hold, entry)

    empty_rows = jnp.zeros((group_rows,) + initial.shape[1:], jnp.float32)
    empty_all = jnp.zeros_like(initial)
    _, solved, received = lax.fori_loop(
        0, blocks + group_count - 1, advance, (empty_rows, empty_all, empty_all)
    )
    arrived_starts = shifted_2(solved, "layer", 1)
    predecessors = jnp.where(is_head, initial, arrived_starts)
    finished = fine_step(predecessors, weights[0], biases[0])
    return jnp.stack([finished, solved], axis=0)


def solution(mesh):
    return jax.shard_map(
        shards,
        mesh=mesh,
        in_specs=(P("batch", None, None, None), P("layer", None, None), P("layer", None)),
        out_specs=P("layer", "batch", None, None, None),
        check_vma=False,
    )
```

profile of v0, /device:TPU:16, one launch (start us, length us, event | category | flops | bytes accessed | tf_op | source)
XLA Modules:
  0.0 743.1 jit_solution(13190608354636995868)
XLA Ops:
  27.2 700.6 %while.15 = (s32[]{:T(128)}, f32[8,4,4,512]{3,0,2,1:T(8,128)}, f32[8,4,4,512]{3,0,2,1:T(8,128)S(1)}, s32[]{:T(128)}, pred[]{:T(512)}, /*index=5*/f32[8,4,4,512]{...) while((s32[]{:T(128)}, f32[8,4,4,512]{3,0,2,1:T(8,128)}, ...), condition=%wide.region_3.4_spmd, body=%wide.region_0.3_spmd.sunk | while | flops 67567624 | bytes 3677459 | solution.py:72
  29.2 9.0 %collective-permute-done = f32[8,4,4,512]{3,0,2,1:T(8,128)S(1)} collective-permute-done((f32[8,4,4,512]{3,0,2,1:T(8,128)}, f32[8,4,4,512]{3,0,2,1:T(8,128)S(1)}, u32[]{:S(2)}, u32[]{:S(2)}) %collective-permute-start) | collective-permute-done | bytes 262176 | tf_op jit(solution)/shard_map/while/body/eval_jaxpr/ppermute | solution.py:12
  40.1 9.0 %collective-permute-done = f32[8,4,4,512]{3,0,2,1:T(8,128)S(1)} collective-permute-done((f32[8,4,4,512]{3,0,2,1:T(8,128)}, f32[8,4,4,512]{3,0,2,1:T(8,128)S(1)}, u32[]{:S(2)}, u32[]{:S(2)}) %collective-permute-start) | collective-permute-done | bytes 262176 | tf_op jit(solution)/shard_map/while/body/eval_jaxpr/ppermute | solution.py:12
  51.0 9.0 %collective-permute-done = f32[8,4,4,512]{3,0,2,1:T(8,128)S(1)} collective-permute-done((f32[8,4,4,512]{3,0,2,1:T(8,128)}, f32[8,4,4,512]{3,0,2,1:T(8,128)S(1)}, u32[]{:S(2)}, u32[]{:S(2)}) %collective-permute-start) | collective-permute-done | bytes 262176 | tf_op jit(solution)/shard_map/while/body/eval_jaxpr/ppermute | solution.py:12
  61.9 9.0 %collective-permute-done = f32[8,4,4,512]{3,0,2,1:T(8,128)S(1)} collective-permute-done((f32[8,4,4,512]{3,0,2,1:T(8,128)}, f32[8,4,4,512]{3,0,2,1:T(8,128)S(1)}, u32[]{:S(2)}, u32[]{:S(2)}) %collective-permute-start) | collective-permute-done | bytes 262176 | tf_op jit(solution)/shard_map/while/body/eval_jaxpr/ppermute | solution.py:12
  72.8 9.0 %collective-permute-done = f32[8,4,4,512]{3,0,2,1:T(8,128)S(1)} collective-permute-done((f32[8,4,4,512]{3,0,2,1:T(8,128)}, f32[8,4,4,512]{3,0,2,1:T(8,128)S(1)}, u32[]{:S(2)}, u32[]{:S(2)}) %collective-permute-start) | collective-permute-done | bytes 262176 | tf_op jit(solution)/shard_map/while/body/eval_jaxpr/ppermute | solution.py:12
  83.7 9.0 %collective-permute-done = f32[8,4,4,512]{3,0,2,1:T(8,128)S(1)} collective-permute-done((f32[8,4,4,512]{3,0,2,1:T(8,128)}, f32[8,4,4,512]{3,0,2,1:T(8,128)S(1)}, u32[]{:S(2)}, u32[]{:S(2)}) %collective-permute-start) | collective-permute-done | bytes 262176 | tf_op jit(solution)/shard_map/while/body/eval_jaxpr/ppermute | solution.py:12
  94.6 9.0 %collective-permute-done = f32[8,4,4,512]{3,0,2,1:T(8,128)S(1)} collective-permute-done((f32[8,4,4,512]{3,0,2,1:T(8,128)}, f32[8,4,4,512]{3,0,2,1:T(8,128)S(1)}, u32[]{:S(2)}, u32[]{:S(2)}) %collective-permute-start) | collective-permute-done | bytes 262176 | tf_op jit(solution)/shard_map/while/body/eval_jaxpr/ppermute | solution.py:12
  105.5 9.0 %collective-permute-done = f32[8,4,4,512]{3,0,2,1:T(8,128)S(1)} collective-permute-done((f32[8,4,4,512]{3,0,2,1:T(8,128)}, f32[8,4,4,512]{3,0,2,1:T(8,128)S(1)}, u32[]{:S(2)}, u32[]{:S(2)}) %collective-permute-start) | collective-permute-done | bytes 262176 | tf_op jit(solution)/shard_map/while/body/eval_jaxpr/ppermute | solution.py:12
  127.3 9.0 %collective-permute-done = f32[8,4,4,512]{3,0,2,1:T(8,128)S(1)} collective-permute-done((f32[8,4,4,512]{3,0,2,1:T(8,128)}, f32[8,4,4,512]{3,0,2,1:T(8,128)S(1)}, u32[]{:S(2)}, u32[]{:S(2)}) %collective-permute-start) | collective-permute-done | bytes 262176 | tf_op jit(solution)/shard_map/while/body/eval_jaxpr/ppermute | solution.py:12
  138.2 9.0 %collective-permute-done = f32[8,4,4,512]{3,0,2,1:T(8,128)S(1)} collective-permute-done((f32[8,4,4,512]{3,0,2,1:T(8,128)}, f32[8,4,4,512]{3,0,2,1:T(8,128)S(1)}, u32[]{:S(2)}, u32[]{:S(2)}) %collective-permute-start) | collective-permute-done | bytes 262176 | tf_op jit(solution)/shard_map/while/body/eval_jaxpr/ppermute | solution.py:12
  149.1 9.0 %collective-permute-done = f32[8,4,4,512]{3,0,2,1:T(8,128)S(1)} collective-permute-done((f32[8,4,4,512]{3,0,2,1:T(8,128)}, f32[8,4,4,512]{3,0,2,1:T(8,128)S(1)}, u32[]{:S(2)}, u32[]{:S(2)}) %collective-permute-start) | collective-permute-done | bytes 262176 | tf_op jit(solution)/shard_map/while/body/eval_jaxpr/ppermute | solution.py:12
  160.0 9.0 %collective-permute-done = f32[8,4,4,512]{3,0,2,1:T(8,128)S(1)} collective-permute-done((f32[8,4,4,512]{3,0,2,1:T(8,128)}, f32[8,4,4,512]{3,0,2,1:T(8,128)S(1)}, u32[]{:S(2)}, u32[]{:S(2)}) %collective-permute-start) | collective-permute-done | bytes 262176 | tf_op jit(solution)/shard_map/while/body/eval_jaxpr/ppermute | solution.py:12
  170.9 9.0 %collective-permute-done = f32[8,4,4,512]{3,0,2,1:T(8,128)S(1)} collective-permute-done((f32[8,4,4,512]{3,0,2,1:T(8,128)}, f32[8,4,4,512]{3,0,2,1:T(8,128)S(1)}, u32[]{:S(2)}, u32[]{:S(2)}) %collective-permute-start) | collective-permute-done | bytes 262176 | tf_op jit(solution)/shard_map/while/body/eval_jaxpr/ppermute | solution.py:12
  181.8 9.0 %collective-permute-done = f32[8,4,4,512]{3,0,2,1:T(8,128)S(1)} collective-permute-done((f32[8,4,4,512]{3,0,2,1:T(8,128)}, f32[8,4,4,512]{3,0,2,1:T(8,128)S(1)}, u32[]{:S(2)}, u32[]{:S(2)}) %collective-permute-start) | collective-permute-done | bytes 262176 | tf_op jit(solution)/shard_map/while/body/eval_jaxpr/ppermute | solution.py:12
  192.7 9.0 %collective-permute-done = f32[8,4,4,512]{3,0,2,1:T(8,128)S(1)} collective-permute-done((f32[8,4,4,512]{3,0,2,1:T(8,128)}, f32[8,4,4,512]{3,0,2,1:T(8,128)S(1)}, u32[]{:S(2)}, u32[]{:S(2)}) %collective-permute-start) | collective-permute-done | bytes 262176 | tf_op jit(solution)/shard_map/while/body/eval_jaxpr/ppermute | solution.py:12
  203.6 9.0 %collective-permute-done = f32[8,4,4,512]{3,0,2,1:T(8,128)S(1)} collective-permute-done((f32[8,4,4,512]{3,0,2,1:T(8,128)}, f32[8,4,4,512]{3,0,2,1:T(8,128)S(1)}, u32[]{:S(2)}, u32[]{:S(2)}) %collective-permute-start) | collective-permute-done | bytes 262176 | tf_op jit(solution)/shard_map/while/body/eval_jaxpr/ppermute | solution.py:12
  214.5 9.0 %collective-permute-done = f32[8,4,4,512]{3,0,2,1:T(8,128)S(1)} collective-permute-done((f32[8,4,4,512]{3,0,2,1:T(8,128)}, f32[8,4,4,512]{3,0,2,1:T(8,128)S(1)}, u32[]{:S(2)}, u32[]{:S(2)}) %collective-permute-start) | collective-permute-done | bytes 262176 | tf_op jit(solution)/shard_map/while/body/eval_jaxpr/ppermute | solution.py:12
  225.4 9.0 %collective-permute-done = f32[8,4,4,512]{3,0,2,1:T(8,128)S(1)} collective-permute-done((f32[8,4,4,512]{3,0,2,1:T(8,128)}, f32[8,4,4,512]{3,0,2,1:T(8,128)S(1)}, u32[]{:S(2)}, u32[]{:S(2)}) %collective-permute-start) | collective-permute-done | bytes 262176 | tf_op jit(solution)/shard_map/while/body/eval_jaxpr/ppermute | solution.py:12
  236.3 9.0 %collective-permute-done = f32[8,4,4,512]{3,0,2,1:T(8,128)S(1)} collective-permute-done((f32[8,4,4,512]{3,0,2,1:T(8,128)}, f32[8,4,4,512]{3,0,2,1:T(8,128)S(1)}, u32[]{:S(2)}, u32[]{:S(2)}) %collective-permute-start) | collective-permute-done | bytes 262176 | tf_op jit(solution)/shard_map/while/body/eval_jaxpr/ppermute | solution.py:12
  247.2 9.0 %collective-permute-done = f32[8,4,4,512]{3,0,2,1:T(8,128)S(1)} collective-permute-done((f32[8,4,4,512]{3,0,2,1:T(8,128)}, f32[8,4,4,512]{3,0,2,1:T(8,128)S(1)}, u32[]{:S(2)}, u32[]{:S(2)}) %collective-permute-start) | collective-permute-done | bytes 262176 | tf_op jit(solution)/shard_map/while/body/eval_jaxpr/ppermute | solution.py:12
  258.1 9.0 %collective-permute-done = f32[8,4,4,512]{3,0,2,1:T(8,128)S(1)} collective-permute-done((f32[8,4,4,512]{3,0,2,1:T(8,128)}, f32[8,4,4,512]{3,0,2,1:T(8,128)S(1)}, u32[]{:S(2)}, u32[]{:S(2)}) %collective-permute-start) | collective-permute-done | bytes 262176 | tf_op jit(solution)/shard_map/while/body/eval_jaxpr/ppermute | solution.py:12
  269.0 9.0 %collective-permute-done = f32[8,4,4,512]{3,0,2,1:T(8,128)S(1)} collective-permute-done((f32[8,4,4,512]{3,0,2,1:T(8,128)}, f32[8,4,4,512]{3,0,2,1:T(8,128)S(1)}, u32[]{:S(2)}, u32[]{:S(2)}) %collective-permute-start) | collective-permute-done | bytes 262176 | tf_op jit(solution)/shard_map/while/body/eval_jaxpr/ppermute | solution.py:12
  279.9 9.0 %collective-permute-done = f32[8,4,4,512]{3,0,2,1:T(8,128)S(1)} collective-permute-done((f32[8,4,4,512]{3,0,2,1:T(8,128)}, f32[8,4,4,512]{3,0,2,1:T(8,128)S(1)}, u32[]{:S(2)}, u32[]{:S(2)}) %collective-permute-start) | collective-permute-done | bytes 262176 | tf_op jit(solution)/shard_map/while/body/eval_jaxpr/ppermute | solution.py:12
  290.8 9.0 %collective-permute-done = f32[8,4,4,512]{3,0,2,1:T(8,128)S(1)} collective-permute-done((f32[8,4,4,512]{3,0,2,1:T(8,128)}, f32[8,4,4,512]{3,0,2,1:T(8,128)S(1)}, u32[]{:S(2)}, u32[]{:S(2)}) %collective-permute-start) | collective-permute-done | bytes 262176 | tf_op jit(solution)/shard_map/while/body/eval_jaxpr/ppermute | solution.py:12
  301.7 9.0 %collective-permute-done = f32[8,4,4,512]{3,0,2,1:T(8,128)S(1)} collective-permute-done((f32[8,4,4,512]{3,0,2,1:T(8,128)}, f32[8,4,4,512]{3,0,2,1:T(8,128)S(1)}, u32[]{:S(2)}, u32[]{:S(2)}) %collective-permute-start) | collective-permute-done | bytes 262176 | tf_op jit(solution)/shard_map/while/body/eval_jaxpr/ppermute | solution.py:12
  312.6 9.0 %collective-permute-done = f32[8,4,4,512]{3,0,2,1:T(8,128)S(1)} collective-permute-done((f32[8,4,4,512]{3,0,2,1:T(8,128)}, f32[8,4,4,512]{3,0,2,1:T(8,128)S(1)}, u32[]{:S(2)}, u32[]{:S(2)}) %collective-permute-start) | collective-permute-done | bytes 262176 | tf_op jit(solution)/shard_map/while/body/eval_jaxpr/ppermute | solution.py:12
  334.4 9.0 %collective-permute-done = f32[8,4,4,512]{3,0,2,1:T(8,128)S(1)} collective-permute-done((f32[8,4,4,512]{3,0,2,1:T(8,128)}, f32[8,4,4,512]{3,0,2,1:T(8,128)S(1)}, u32[]{:S(2)}, u32[]{:S(2)}) %collective-permute-start) | collective-permute-done | bytes 262176 | tf_op jit(solution)/shard_map/while/body/eval_jaxpr/ppermute | solution.py:12
  345.3 9.0 %collective-permute-done = f32[8,4,4,512]{3,0,2,1:T(8,128)S(1)} collective-permute-done((f32[8,4,4,512]{3,0,2,1:T(8,128)}, f32[8,4,4,512]{3,0,2,1:T(8,128)S(1)}, u32[]{:S(2)}, u32[]{:S(2)}) %collective-permute-start) | collective-permute-done | bytes 262176 | tf_op jit(solution)/shard_map/while/body/eval_jaxpr/ppermute | solution.py:12
  356.2 9.0 %collective-permute-done = f32[8,4,4,512]{3,0,2,1:T(8,128)S(1)} collective-permute-done((f32[8,4,4,512]{3,0,2,1:T(8,128)}, f32[8,4,4,512]{3,0,2,1:T(8,128)S(1)}, u32[]{:S(2)}, u32[]{:S(2)}) %collective-permute-start) | collective-permute-done | bytes 262176 | tf_op jit(solution)/shard_map/while/body/eval_jaxpr/ppermute | solution.py:12
  367.1 9.0 %collective-permute-done = f32[8,4,4,512]{3,0,2,1:T(8,128)S(1)} collective-permute-done((f32[8,4,4,512]{3,0,2,1:T(8,128)}, f32[8,4,4,512]{3,0,2,1:T(8,128)S(1)}, u32[]{:S(2)}, u32[]{:S(2)}) %collective-permute-start) | collective-permute-done | bytes 262176 | tf_op jit(solution)/shard_map/while/body/eval_jaxpr/ppermute | solution.py:12
  378.0 9.0 %collective-permute-done = f32[8,4,4,512]{3,0,2,1:T(8,128)S(1)} collective-permute-done((f32[8,4,4,512]{3,0,2,1:T(8,128)}, f32[8,4,4,512]{3,0,2,1:T(8,128)S(1)}, u32[]{:S(2)}, u32[]{:S(2)}) %collective-permute-start) | collective-permute-done | bytes 262176 | tf_op jit(solution)/shard_map/while/body/eval_jaxpr/ppermute | solution.py:12
  391.8 9.0 %collective-permute-done = f32[8,4,4,512]{3,0,2,1:T(8,128)S(1)} collective-permute-done((f32[8,4,4,512]{3,0,2,1:T(8,128)}, f32[8,4,4,512]{3,0,2,1:T(8,128)S(1)}, u32[]{:S(2)}, u32[]{:S(2)}) %collective-permute-start) | collective-permute-done | bytes 262176 | tf_op jit(solution)/shard_map/while/body/eval_jaxpr/ppermute | solution.py:12
  402.7 9.0 %collective-permute-done = f32[8,4,4,512]{3,0,2,1:T(8,128)S(1)} collective-permute-done((f32[8,4,4,512]{3,0,2,1:T(8,128)}, f32[8,4,4,512]{3,0,2,1:T(8,128)S(1)}, u32[]{:S(2)}, u32[]{:S(2)}) %collective-permute-start) | collective-permute-done | bytes 262176 | tf_op jit(solution)/shard_map/while/body/eval_jaxpr/ppermute | solution.py:12
  413.6 9.0 %collective-permute-done = f32[8,4,4,512]{3,0,2,1:T(8,128)S(1)} collective-permute-done((f32[8,4,4,512]{3,0,2,1:T(8,128)}, f32[8,4,4,512]{3,0,2,1:T(8,128)S(1)}, u32[]{:S(2)}, u32[]{:S(2)}) %collective-permute-start) | collective-permute-done | bytes 262176 | tf_op jit(solution)/shard_map/while/body/eval_jaxpr/ppermute | solution.py:12
  424.5 9.0 %collective-permute-done = f32[8,4,4,512]{3,0,2,1:T(8,128)S(1)} collective-permute-done((f32[8,4,4,512]{3,0,2,1:T(8,128)}, f32[8,4,4,512]{3,0,2,1:T(8,128)S(1)}, u32[]{:S(2)}, u32[]{:S(2)}) %collective-permute-start) | collective-permute-done | bytes 262176 | tf_op jit(solution)/shard_map/while/body/eval_jaxpr/ppermute | solution.py:12
  435.4 9.0 %collective-permute-done = f32[8,4,4,512]{3,0,2,1:T(8,128)S(1)} collective-permute-done((f32[8,4,4,512]{3,0,2,1:T(8,128)}, f32[8,4,4,512]{3,0,2,1:T(8,128)S(1)}, u32[]{:S(2)}, u32[]{:S(2)}) %collective-permute-start) | collective-permute-done | bytes 262176 | tf_op jit(solution)/shard_map/while/body/eval_jaxpr/ppermute | solution.py:12
  446.3 9.0 %collective-permute-done = f32[8,4,4,512]{3,0,2,1:T(8,128)S(1)} collective-permute-done((f32[8,4,4,512]{3,0,2,1:T(8,128)}, f32[8,4,4,512]{3,0,2,1:T(8,128)S(1)}, u32[]{:S(2)}, u32[]{:S(2)}) %collective-permute-start) | collective-permute-done | bytes 262176 | tf_op jit(solution)/shard_map/while/body/eval_jaxpr/ppermute | solution.py:12
  457.2 9.0 %collective-permute-done = f32[8,4,4,512]{3,0,2,1:T(8,128)S(1)} collective-permute-done((f32[8,4,4,512]{3,0,2,1:T(8,128)}, f32[8,4,4,512]{3,0,2,1:T(8,128)S(1)}, u32[]{:S(2)}, u32[]{:S(2)}) %collective-permute-start) | collective-permute-done | bytes 262176 | tf_op jit(solution)/shard_map/while/body/eval_jaxpr/ppermute | solution.py:12
  468.1 9.0 %collective-permute-done = f32[8,4,4,512]{3,0,2,1:T(8,128)S(1)} collective-permute-done((f32[8,4,4,512]{3,0,2,1:T(8,128)}, f32[8,4,4,512]{3,0,2,1:T(8,128)S(1)}, u32[]{:S(2)}, u32[]{:S(2)}) %collective-permute-start) | collective-permute-done | bytes 262176 | tf_op jit(solution)/shard_map/while/body/eval_jaxpr/ppermute | solution.py:12
  479.0 9.0 %collective-permute-done = f32[8,4,4,512]{3,0,2,1:T(8,128)S(1)} collective-permute-done((f32[8,4,4,512]{3,0,2,1:T(8,128)}, f32[8,4,4,512]{3,0,2,1:T(8,128)S(1)}, u32[]{:S(2)}, u32[]{:S(2)}) %collective-permute-start) | collective-permute-done | bytes 262176 | tf_op jit(solution)/shard_map/while/body/eval_jaxpr/ppermute | solution.py:12
  500.8 9.0 %collective-permute-done = f32[8,4,4,512]{3,0,2,1:T(8,128)S(1)} collective-permute-done((f32[8,4,4,512]{3,0,2,1:T(8,128)}, f32[8,4,4,512]{3,0,2,1:T(8,128)S(1)}, u32[]{:S(2)}, u32[]{:S(2)}) %collective-permute-start) | collective-permute-done | bytes 262176 | tf_op jit(solution)/shard_map/while/body/eval_jaxpr/ppermute | solution.py:12
  511.7 9.0 %collective-permute-done = f32[8,4,4,512]{3,0,2,1:T(8,128)S(1)} collective-permute-done((f32[8,4,4,512]{3,0,2,1:T(8,128)}, f32[8,4,4,512]{3,0,2,1:T(8,128)S(1)}, u32[]{:S(2)}, u32[]{:S(2)}) %collective-permute-start) | collective-permute-done | bytes 262176 | tf_op jit(solution)/shard_map/while/body/eval_jaxpr/ppermute | solution.py:12
  522.6 9.0 %collective-permute-done = f32[8,4,4,512]{3,0,2,1:T(8,128)S(1)} collective-permute-done((f32[8,4,4,512]{3,0,2,1:T(8,128)}, f32[8,4,4,512]{3,0,2,1:T(8,128)S(1)}, u32[]{:S(2)}, u32[]{:S(2)}) %collective-permute-start) | collective-permute-done | bytes 262176 | tf_op jit(solution)/shard_map/while/body/eval_jaxpr/ppermute | solution.py:12
  533.5 9.0 %collective-permute-done = f32[8,4,4,512]{3,0,2,1:T(8,128)S(1)} collective-permute-done((f32[8,4,4,512]{3,0,2,1:T(8,128)}, f32[8,4,4,512]{3,0,2,1:T(8,128)S(1)}, u32[]{:S(2)}, u32[]{:S(2)}) %collective-permute-start) | collective-permute-done | bytes 262176 | tf_op jit(solution)/shard_map/while/body/eval_jaxpr/ppermute | solution.py:12
  544.4 9.0 %collective-permute-done = f32[8,4,4,512]{3,0,2,1:T(8,128)S(1)} collective-permute-done((f32[8,4,4,512]{3,0,2,1:T(8,128)}, f32[8,4,4,512]{3,0,2,1:T(8,128)S(1)}, u32[]{:S(2)}, u32[]{:S(2)}) %collective-permute-start) | collective-permute-done | bytes 262176 | tf_op jit(solution)/shard_map/while/body/eval_jaxpr/ppermute | solution.py:12
  555.3 9.0 %collective-permute-done = f32[8,4,4,512]{3,0,2,1:T(8,128)S(1)} collective-permute-done((f32[8,4,4,512]{3,0,2,1:T(8,128)}, f32[8,4,4,512]{3,0,2,1:T(8,128)S(1)}, u32[]{:S(2)}, u32[]{:S(2)}) %collective-permute-start) | collective-permute-done | bytes 262176 | tf_op jit(solution)/shard_map/while/body/eval_jaxpr/ppermute | solution.py:12
  566.2 9.0 %collective-permute-done = f32[8,4,4,512]{3,0,2,1:T(8,128)S(1)} collective-permute-done((f32[8,4,4,512]{3,0,2,1:T(8,128)}, f32[8,4,4,512]{3,0,2,1:T(8,128)S(1)}, u32[]{:S(2)}, u32[]{:S(2)}) %collective-permute-start) | collective-permute-done | bytes 262176 | tf_op jit(solution)/shard_map/while/body/eval_jaxpr/ppermute | solution.py:12
  (217 shorter events, 322.7 us)
Async XLA Ops:
  27.2 10.9 %collective-permute-start = (f32[8,4,4,512]{3,0,2,1:T(8,128)}, f32[8,4,4,512]{3,0,2,1:T(8,128)S(1)}, u32[]{:S(2)}, u32[]{:S(2)}) collective-permute-start(f32[8,4,4,512]{3,0,2,1:T(8,128)} %get-tuple-element.291), channel_id=1, source_target_pairs={{0,4},{4,8},{8,12},{12,16},{16,20},{20,24},{24,28},{28,32},{32,36}... | collective-permute-start | bytes 786440 | tf_op jit(solution)/shard_map/while/body/eval_jaxpr/ppermute | solution.py:12
  38.1 10.9 %collective-permute-start = (f32[8,4,4,512]{3,0,2,1:T(8,128)}, f32[8,4,4,512]{3,0,2,1:T(8,128)S(1)}, u32[]{:S(2)}, u32[]{:S(2)}) collective-permute-start(f32[8,4,4,512]{3,0,2,1:T(8,128)} %get-tuple-element.291), channel_id=1, source_target_pairs={{0,4},{4,8},{8,12},{12,16},{16,20},{20,24},{24,28},{28,32},{32,36}... | collective-permute-start | bytes 786440 | tf_op jit(solution)/shard_map/while/body/eval_jaxpr/ppermute | solution.py:12
  49.0 10.9 %collective-permute-start = (f32[8,4,4,512]{3,0,2,1:T(8,128)}, f32[8,4,4,512]{3,0,2,1:T(8,128)S(1)}, u32[]{:S(2)}, u32[]{:S(2)}) collective-permute-start(f32[8,4,4,512]{3,0,2,1:T(8,128)} %get-tuple-element.291), channel_id=1, source_target_pairs={{0,4},{4,8},{8,12},{12,16},{16,20},{20,24},{24,28},{28,32},{32,36}... | collective-permute-start | bytes 786440 | tf_op jit(solution)/shard_map/while/body/eval_jaxpr/ppermute | solution.py:12
  59.9 10.9 %collective-permute-start = (f32[8,4,4,512]{3,0,2,1:T(8,128)}, f32[8,4,4,512]{3,0,2,1:T(8,128)S(1)}, u32[]{:S(2)}, u32[]{:S(2)}) collective-permute-start(f32[8,4,4,512]{3,0,2,1:T(8,128)} %get-tuple-element.291), channel_id=1, source_target_pairs={{0,4},{4,8},{8,12},{12,16},{16,20},{20,24},{24,28},{28,32},{32,36}... | collective-permute-start | bytes 786440 | tf_op jit(solution)/shard_map/while/body/eval_jaxpr/ppermute | solution.py:12
  70.8 10.9 %collective-permute-start = (f32[8,4,4,512]{3,0,2,1:T(8,128)}, f32[8,4,4,512]{3,0,2,1:T(8,128)S(1)}, u32[]{:S(2)}, u32[]{:S(2)}) collective-permute-start(f32[8,4,4,512]{3,0,2,1:T(8,128)} %get-tuple-element.291), channel_id=1, source_target_pairs={{0,4},{4,8},{8,12},{12,16},{16,20},{20,24},{24,28},{28,32},{32,36}... | collective-permute-start | bytes 786440 | tf_op jit(solution)/shard_map/while/body/eval_jaxpr/ppermute | solution.py:12
  92.6 10.9 %collective-permute-start = (f32[8,4,4,512]{3,0,2,1:T(8,128)}, f32[8,4,4,512]{3,0,2,1:T(8,128)S(1)}, u32[]{:S(2)}, u32[]{:S(2)}) collective-permute-start(f32[8,4,4,512]{3,0,2,1:T(8,128)} %get-tuple-element.291), channel_id=1, source_target_pairs={{0,4},{4,8},{8,12},{12,16},{16,20},{20,24},{24,28},{28,32},{32,36}... | collective-permute-start | bytes 786440 | tf_op jit(solution)/shard_map/while/body/eval_jaxpr/ppermute | solution.py:12
  103.5 10.9 %collective-permute-start = (f32[8,4,4,512]{3,0,2,1:T(8,128)}, f32[8,4,4,512]{3,0,2,1:T(8,128)S(1)}, u32[]{:S(2)}, u32[]{:S(2)}) collective-permute-start(f32[8,4,4,512]{3,0,2,1:T(8,128)} %get-tuple-element.291), channel_id=1, source_target_pairs={{0,4},{4,8},{8,12},{12,16},{16,20},{20,24},{24,28},{28,32},{32,36}... | collective-permute-start | bytes 786440 | tf_op jit(solution)/shard_map/while/body/eval_jaxpr/ppermute | solution.py:12
  125.3 10.9 %collective-permute-start = (f32[8,4,4,512]{3,0,2,1:T(8,128)}, f32[8,4,4,512]{3,0,2,1:T(8,128)S(1)}, u32[]{:S(2)}, u32[]{:S(2)}) collective-permute-start(f32[8,4,4,512]{3,0,2,1:T(8,128)} %get-tuple-element.291), channel_id=1, source_target_pairs={{0,4},{4,8},{8,12},{12,16},{16,20},{20,24},{24,28},{28,32},{32,36}... | collective-permute-start | bytes 786440 | tf_op jit(solution)/shard_map/while/body/eval_jaxpr/ppermute | solution.py:12
  136.2 10.9 %collective-permute-start = (f32[8,4,4,512]{3,0,2,1:T(8,128)}, f32[8,4,4,512]{3,0,2,1:T(8,128)S(1)}, u32[]{:S(2)}, u32[]{:S(2)}) collective-permute-start(f32[8,4,4,512]{3,0,2,1:T(8,128)} %get-tuple-element.291), channel_id=1, source_target_pairs={{0,4},{4,8},{8,12},{12,16},{16,20},{20,24},{24,28},{28,32},{32,36}... | collective-permute-start | bytes 786440 | tf_op jit(solution)/shard_map/while/body/eval_jaxpr/ppermute | solution.py:12
  147.1 10.9 %collective-permute-start = (f32[8,4,4,512]{3,0,2,1:T(8,128)}, f32[8,4,4,512]{3,0,2,1:T(8,128)S(1)}, u32[]{:S(2)}, u32[]{:S(2)}) collective-permute-start(f32[8,4,4,512]{3,0,2,1:T(8,128)} %get-tuple-element.291), channel_id=1, source_target_pairs={{0,4},{4,8},{8,12},{12,16},{16,20},{20,24},{24,28},{28,32},{32,36}... | collective-permute-start | bytes 786440 | tf_op jit(solution)/shard_map/while/body/eval_jaxpr/ppermute | solution.py:12
  158.0 10.9 %collective-permute-start = (f32[8,4,4,512]{3,0,2,1:T(8,128)}, f32[8,4,4,512]{3,0,2,1:T(8,128)S(1)}, u32[]{:S(2)}, u32[]{:S(2)}) collective-permute-start(f32[8,4,4,512]{3,0,2,1:T(8,128)} %get-tuple-element.291), channel_id=1, source_target_pairs={{0,4},{4,8},{8,12},{12,16},{16,20},{20,24},{24,28},{28,32},{32,36}... | collective-permute-start | bytes 786440 | tf_op jit(solution)/shard_map/while/body/eval_jaxpr/ppermute | solution.py:12
  168.9 10.9 %collective-permute-start = (f32[8,4,4,512]{3,0,2,1:T(8,128)}, f32[8,4,4,512]{3,0,2,1:T(8,128)S(1)}, u32[]{:S(2)}, u32[]{:S(2)}) collective-permute-start(f32[8,4,4,512]{3,0,2,1:T(8,128)} %get-tuple-element.291), channel_id=1, source_target_pairs={{0,4},{4,8},{8,12},{12,16},{16,20},{20,24},{24,28},{28,32},{32,36}... | collective-permute-start | bytes 786440 | tf_op jit(solution)/shard_map/while/body/eval_jaxpr/ppermute | solution.py:12
  179.8 10.9 %collective-permute-start = (f32[8,4,4,512]{3,0,2,1:T(8,128)}, f32[8,4,4,512]{3,0,2,1:T(8,128)S(1)}, u32[]{:S(2)}, u32[]{:S(2)}) collective-permute-start(f32[8,4,4,512]{3,0,2,1:T(8,128)} %get-tuple-element.291), channel_id=1, source_target_pairs={{0,4},{4,8},{8,12},{12,16},{16,20},{20,24},{24,28},{28,32},{32,36}... | collective-permute-start | bytes 786440 | tf_op jit(solution)/shard_map/while/body/eval_jaxpr/ppermute | solution.py:12
  201.6 10.9 %collective-permute-start = (f32[8,4,4,512]{3,0,2,1:T(8,128)}, f32[8,4,4,512]{3,0,2,1:T(8,128)S(1)}, u32[]{:S(2)}, u32[]{:S(2)}) collective-permute-start(f32[8,4,4,512]{3,0,2,1:T(8,128)} %get-tuple-element.291), channel_id=1, source_target_pairs={{0,4},{4,8},{8,12},{12,16},{16,20},{20,24},{24,28},{28,32},{32,36}... | collective-permute-start | bytes 786440 | tf_op jit(solution)/shard_map/while/body/eval_jaxpr/ppermute | solution.py:12
  212.5 10.9 %collective-permute-start = (f32[8,4,4,512]{3,0,2,1:T(8,128)}, f32[8,4,4,512]{3,0,2,1:T(8,128)S(1)}, u32[]{:S(2)}, u32[]{:S(2)}) collective-permute-start(f32[8,4,4,512]{3,0,2,1:T(8,128)} %get-tuple-element.291), channel_id=1, source_target_pairs={{0,4},{4,8},{8,12},{12,16},{16,20},{20,24},{24,28},{28,32},{32,36}... | collective-permute-start | bytes 786440 | tf_op jit(solution)/shard_map/while/body/eval_jaxpr/ppermute | solution.py:12
  234.3 10.9 %collective-permute-start = (f32[8,4,4,512]{3,0,2,1:T(8,128)}, f32[8,4,4,512]{3,0,2,1:T(8,128)S(1)}, u32[]{:S(2)}, u32[]{:S(2)}) collective-permute-start(f32[8,4,4,512]{3,0,2,1:T(8,128)} %get-tuple-element.291), channel_id=1, source_target_pairs={{0,4},{4,8},{8,12},{12,16},{16,20},{20,24},{24,28},{28,32},{32,36}... | collective-permute-start | bytes 786440 | tf_op jit(solution)/shard_map/while/body/eval_jaxpr/ppermute | solution.py:12
  245.2 10.9 %collective-permute-start = (f32[8,4,4,512]{3,0,2,1:T(8,128)}, f32[8,4,4,512]{3,0,2,1:T(8,128)S(1)}, u32[]{:S(2)}, u32[]{:S(2)}) collective-permute-start(f32[8,4,4,512]{3,0,2,1:T(8,128)} %get-tuple-element.291), channel_id=1, source_target_pairs={{0,4},{4,8},{8,12},{12,16},{16,20},{20,24},{24,28},{28,32},{32,36}... | collective-permute-start | bytes 786440 | tf_op jit(solution)/shard_map/while/body/eval_jaxpr/ppermute | solution.py:12
  267.0 10.9 %collective-permute-start = (f32[8,4,4,512]{3,0,2,1:T(8,128)}, f32[8,4,4,512]{3,0,2,1:T(8,128)S(1)}, u32[]{:S(2)}, u32[]{:S(2)}) collective-permute-start(f32[8,4,4,512]{3,0,2,1:T(8,128)} %get-tuple-element.291), channel_id=1, source_target_pairs={{0,4},{4,8},{8,12},{12,16},{16,20},{20,24},{24,28},{28,32},{32,36}... | collective-permute-start | bytes 786440 | tf_op jit(solution)/shard_map/while/body/eval_jaxpr/ppermute | solution.py:12
  277.9 10.9 %collective-permute-start = (f32[8,4,4,512]{3,0,2,1:T(8,128)}, f32[8,4,4,512]{3,0,2,1:T(8,128)S(1)}, u32[]{:S(2)}, u32[]{:S(2)}) collective-permute-start(f32[8,4,4,512]{3,0,2,1:T(8,128)} %get-tuple-element.291), channel_id=1, source_target_pairs={{0,4},{4,8},{8,12},{12,16},{16,20},{20,24},{24,28},{28,32},{32,36}... | collective-permute-start | bytes 786440 | tf_op jit(solution)/shard_map/while/body/eval_jaxpr/ppermute | solution.py:12
  299.7 10.9 %collective-permute-start = (f32[8,4,4,512]{3,0,2,1:T(8,128)}, f32[8,4,4,512]{3,0,2,1:T(8,128)S(1)}, u32[]{:S(2)}, u32[]{:S(2)}) collective-permute-start(f32[8,4,4,512]{3,0,2,1:T(8,128)} %get-tuple-element.291), channel_id=1, source_target_pairs={{0,4},{4,8},{8,12},{12,16},{16,20},{20,24},{24,28},{28,32},{32,36}... | collective-permute-start | bytes 786440 | tf_op jit(solution)/shard_map/while/body/eval_jaxpr/ppermute | solution.py:12
  310.6 10.9 %collective-permute-start = (f32[8,4,4,512]{3,0,2,1:T(8,128)}, f32[8,4,4,512]{3,0,2,1:T(8,128)S(1)}, u32[]{:S(2)}, u32[]{:S(2)}) collective-permute-start(f32[8,4,4,512]{3,0,2,1:T(8,128)} %get-tuple-element.291), channel_id=1, source_target_pairs={{0,4},{4,8},{8,12},{12,16},{16,20},{20,24},{24,28},{28,32},{32,36}... | collective-permute-start | bytes 786440 | tf_op jit(solution)/shard_map/while/body/eval_jaxpr/ppermute | solution.py:12
  332.4 10.9 %collective-permute-start = (f32[8,4,4,512]{3,0,2,1:T(8,128)}, f32[8,4,4,512]{3,0,2,1:T(8,128)S(1)}, u32[]{:S(2)}, u32[]{:S(2)}) collective-permute-start(f32[8,4,4,512]{3,0,2,1:T(8,128)} %get-tuple-element.291), channel_id=1, source_target_pairs={{0,4},{4,8},{8,12},{12,16},{16,20},{20,24},{24,28},{28,32},{32,36}... | collective-permute-start | bytes 786440 | tf_op jit(solution)/shard_map/while/body/eval_jaxpr/ppermute | solution.py:12
  343.3 10.9 %collective-permute-start = (f32[8,4,4,512]{3,0,2,1:T(8,128)}, f32[8,4,4,512]{3,0,2,1:T(8,128)S(1)}, u32[]{:S(2)}, u32[]{:S(2)}) collective-permute-start(f32[8,4,4,512]{3,0,2,1:T(8,128)} %get-tuple-element.291), channel_id=1, source_target_pairs={{0,4},{4,8},{8,12},{12,16},{16,20},{20,24},{24,28},{28,32},{32,36}... | collective-permute-start | bytes 786440 | tf_op jit(solution)/shard_map/while/body/eval_jaxpr/ppermute | solution.py:12
  354.2 10.9 %collective-permute-start = (f32[8,4,4,512]{3,0,2,1:T(8,128)}, f32[8,4,4,512]{3,0,2,1:T(8,128)S(1)}, u32[]{:S(2)}, u32[]{:S(2)}) collective-permute-start(f32[8,4,4,512]{3,0,2,1:T(8,128)} %get-tuple-element.291), channel_id=1, source_target_pairs={{0,4},{4,8},{8,12},{12,16},{16,20},{20,24},{24,28},{28,32},{32,36}... | collective-permute-start | bytes 786440 | tf_op jit(solution)/shard_map/while/body/eval_jaxpr/ppermute | solution.py:12
  365.1 10.9 %collective-permute-start = (f32[8,4,4,512]{3,0,2,1:T(8,128)}, f32[8,4,4,512]{3,0,2,1:T(8,128)S(1)}, u32[]{:S(2)}, u32[]{:S(2)}) collective-permute-start(f32[8,4,4,512]{3,0,2,1:T(8,128)} %get-tuple-element.291), channel_id=1, source_target_pairs={{0,4},{4,8},{8,12},{12,16},{16,20},{20,24},{24,28},{28,32},{32,36}... | collective-permute-start | bytes 786440 | tf_op jit(solution)/shard_map/while/body/eval_jaxpr/ppermute | solution.py:12
  376.0 10.9 %collective-permute-start = (f32[8,4,4,512]{3,0,2,1:T(8,128)}, f32[8,4,4,512]{3,0,2,1:T(8,128)S(1)}, u32[]{:S(2)}, u32[]{:S(2)}) collective-permute-start(f32[8,4,4,512]{3,0,2,1:T(8,128)} %get-tuple-element.291), channel_id=1, source_target_pairs={{0,4},{4,8},{8,12},{12,16},{16,20},{20,24},{24,28},{28,32},{32,36}... | collective-permute-start | bytes 786440 | tf_op jit(solution)/shard_map/while/body/eval_jaxpr/ppermute | solution.py:12
  400.8 10.9 %collective-permute-start = (f32[8,4,4,512]{3,0,2,1:T(8,128)}, f32[8,4,4,512]{3,0,2,1:T(8,128)S(1)}, u32[]{:S(2)}, u32[]{:S(2)}) collective-permute-start(f32[8,4,4,512]{3,0,2,1:T(8,128)} %get-tuple-element.291), channel_id=1, source_target_pairs={{0,4},{4,8},{8,12},{12,16},{16,20},{20,24},{24,28},{28,32},{32,36}... | collective-permute-start | bytes 786440 | tf_op jit(solution)/shard_map/while/body/eval_jaxpr/ppermute | solution.py:12
  411.7 10.9 %collective-permute-start = (f32[8,4,4,512]{3,0,2,1:T(8,128)}, f32[8,4,4,512]{3,0,2,1:T(8,128)S(1)}, u32[]{:S(2)}, u32[]{:S(2)}) collective-permute-start(f32[8,4,4,512]{3,0,2,1:T(8,128)} %get-tuple-element.291), channel_id=1, source_target_pairs={{0,4},{4,8},{8,12},{12,16},{16,20},{20,24},{24,28},{28,32},{32,36}... | collective-permute-start | bytes 786440 | tf_op jit(solution)/shard_map/while/body/eval_jaxpr/ppermute | solution.py:12
  433.5 10.9 %collective-permute-start = (f32[8,4,4,512]{3,0,2,1:T(8,128)}, f32[8,4,4,512]{3,0,2,1:T(8,128)S(1)}, u32[]{:S(2)}, u32[]{:S(2)}) collective-permute-start(f32[8,4,4,512]{3,0,2,1:T(8,128)} %get-tuple-element.291), channel_id=1, source_target_pairs={{0,4},{4,8},{8,12},{12,16},{16,20},{20,24},{24,28},{28,32},{32,36}... | collective-permute-start | bytes 786440 | tf_op jit(solution)/shard_map/while/body/eval_jaxpr/ppermute | solution.py:12
  444.4 10.9 %collective-permute-start = (f32[8,4,4,512]{3,0,2,1:T(8,128)}, f32[8,4,4,512]{3,0,2,1:T(8,128)S(1)}, u32[]{:S(2)}, u32[]{:S(2)}) collective-permute-start(f32[8,4,4,512]{3,0,2,1:T(8,128)} %get-tuple-element.291), channel_id=1, source_target_pairs={{0,4},{4,8},{8,12},{12,16},{16,20},{20,24},{24,28},{28,32},{32,36}... | collective-permute-start | bytes 786440 | tf_op jit(solution)/shard_map/while/body/eval_jaxpr/ppermute | solution.py:12
  466.2 10.9 %collective-permute-start = (f32[8,4,4,512]{3,0,2,1:T(8,128)}, f32[8,4,4,512]{3,0,2,1:T(8,128)S(1)}, u32[]{:S(2)}, u32[]{:S(2)}) collective-permute-start(f32[8,4,4,512]{3,0,2,1:T(8,128)} %get-tuple-element.291), channel_id=1, source_target_pairs={{0,4},{4,8},{8,12},{12,16},{16,20},{20,24},{24,28},{28,32},{32,36}... | collective-permute-start | bytes 786440 | tf_op jit(solution)/shard_map/while/body/eval_jaxpr/ppermute | solution.py:12
  477.1 10.9 %collective-permute-start = (f32[8,4,4,512]{3,0,2,1:T(8,128)}, f32[8,4,4,512]{3,0,2,1:T(8,128)S(1)}, u32[]{:S(2)}, u32[]{:S(2)}) collective-permute-start(f32[8,4,4,512]{3,0,2,1:T(8,128)} %get-tuple-element.291), channel_id=1, source_target_pairs={{0,4},{4,8},{8,12},{12,16},{16,20},{20,24},{24,28},{28,32},{32,36}... | collective-permute-start | bytes 786440 | tf_op jit(solution)/shard_map/while/body/eval_jaxpr/ppermute | solution.py:12
  498.9 10.9 %collective-permute-start = (f32[8,4,4,512]{3,0,2,1:T(8,128)}, f32[8,4,4,512]{3,0,2,1:T(8,128)S(1)}, u32[]{:S(2)}, u32[]{:S(2)}) collective-permute-start(f32[8,4,4,512]{3,0,2,1:T(8,128)} %get-tuple-element.291), channel_id=1, source_target_pairs={{0,4},{4,8},{8,12},{12,16},{16,20},{20,24},{24,28},{28,32},{32,36}... | collective-permute-start | bytes 786440 | tf_op jit(solution)/shard_map/while/body/eval_jaxpr/ppermute | solution.py:12
  509.8 10.9 %collective-permute-start = (f32[8,4,4,512]{3,0,2,1:T(8,128)}, f32[8,4,4,512]{3,0,2,1:T(8,128)S(1)}, u32[]{:S(2)}, u32[]{:S(2)}) collective-permute-start(f32[8,4,4,512]{3,0,2,1:T(8,128)} %get-tuple-element.291), channel_id=1, source_target_pairs={{0,4},{4,8},{8,12},{12,16},{16,20},{20,24},{24,28},{28,32},{32,36}... | collective-permute-start | bytes 786440 | tf_op jit(solution)/shard_map/while/body/eval_jaxpr/ppermute | solution.py:12
  520.7 10.9 %collective-permute-start = (f32[8,4,4,512]{3,0,2,1:T(8,128)}, f32[8,4,4,512]{3,0,2,1:T(8,128)S(1)}, u32[]{:S(2)}, u32[]{:S(2)}) collective-permute-start(f32[8,4,4,512]{3,0,2,1:T(8,128)} %get-tuple-element.291), channel_id=1, source_target_pairs={{0,4},{4,8},{8,12},{12,16},{16,20},{20,24},{24,28},{28,32},{32,36}... | collective-permute-start | bytes 786440 | tf_op jit(solution)/shard_map/while/body/eval_jaxpr/ppermute | solution.py:12
  531.6 10.9 %collective-permute-start = (f32[8,4,4,512]{3,0,2,1:T(8,128)}, f32[8,4,4,512]{3,0,2,1:T(8,128)S(1)}, u32[]{:S(2)}, u32[]{:S(2)}) collective-permute-start(f32[8,4,4,512]{3,0,2,1:T(8,128)} %get-tuple-element.291), channel_id=1, source_target_pairs={{0,4},{4,8},{8,12},{12,16},{16,20},{20,24},{24,28},{28,32},{32,36}... | collective-permute-start | bytes 786440 | tf_op jit(solution)/shard_map/while/body/eval_jaxpr/ppermute | solution.py:12
  542.5 10.9 %collective-permute-start = (f32[8,4,4,512]{3,0,2,1:T(8,128)}, f32[8,4,4,512]{3,0,2,1:T(8,128)S(1)}, u32[]{:S(2)}, u32[]{:S(2)}) collective-permute-start(f32[8,4,4,512]{3,0,2,1:T(8,128)} %get-tuple-element.291), channel_id=1, source_target_pairs={{0,4},{4,8},{8,12},{12,16},{16,20},{20,24},{24,28},{28,32},{32,36}... | collective-permute-start | bytes 786440 | tf_op jit(solution)/shard_map/while/body/eval_jaxpr/ppermute | solution.py:12
  553.4 10.9 %collective-permute-start = (f32[8,4,4,512]{3,0,2,1:T(8,128)}, f32[8,4,4,512]{3,0,2,1:T(8,128)S(1)}, u32[]{:S(2)}, u32[]{:S(2)}) collective-permute-start(f32[8,4,4,512]{3,0,2,1:T(8,128)} %get-tuple-element.291), channel_id=1, source_target_pairs={{0,4},{4,8},{8,12},{12,16},{16,20},{20,24},{24,28},{28,32},{32,36}... | collective-permute-start | bytes 786440 | tf_op jit(solution)/shard_map/while/body/eval_jaxpr/ppermute | solution.py:12
  575.2 10.9 %collective-permute-start = (f32[8,4,4,512]{3,0,2,1:T(8,128)}, f32[8,4,4,512]{3,0,2,1:T(8,128)S(1)}, u32[]{:S(2)}, u32[]{:S(2)}) collective-permute-start(f32[8,4,4,512]{3,0,2,1:T(8,128)} %get-tuple-element.291), channel_id=1, source_target_pairs={{0,4},{4,8},{8,12},{12,16},{16,20},{20,24},{24,28},{28,32},{32,36}... | collective-permute-start | bytes 786440 | tf_op jit(solution)/shard_map/while/body/eval_jaxpr/ppermute | solution.py:12
  586.1 10.9 %collective-permute-start = (f32[8,4,4,512]{3,0,2,1:T(8,128)}, f32[8,4,4,512]{3,0,2,1:T(8,128)S(1)}, u32[]{:S(2)}, u32[]{:S(2)}) collective-permute-start(f32[8,4,4,512]{3,0,2,1:T(8,128)} %get-tuple-element.291), channel_id=1, source_target_pairs={{0,4},{4,8},{8,12},{12,16},{16,20},{20,24},{24,28},{28,32},{32,36}... | collective-permute-start | bytes 786440 | tf_op jit(solution)/shard_map/while/body/eval_jaxpr/ppermute | solution.py:12
  607.9 10.9 %collective-permute-start = (f32[8,4,4,512]{3,0,2,1:T(8,128)}, f32[8,4,4,512]{3,0,2,1:T(8,128)S(1)}, u32[]{:S(2)}, u32[]{:S(2)}) collective-permute-start(f32[8,4,4,512]{3,0,2,1:T(8,128)} %get-tuple-element.291), channel_id=1, source_target_pairs={{0,4},{4,8},{8,12},{12,16},{16,20},{20,24},{24,28},{28,32},{32,36}... | collective-permute-start | bytes 786440 | tf_op jit(solution)/shard_map/while/body/eval_jaxpr/ppermute | solution.py:12
  618.8 10.9 %collective-permute-start = (f32[8,4,4,512]{3,0,2,1:T(8,128)}, f32[8,4,4,512]{3,0,2,1:T(8,128)S(1)}, u32[]{:S(2)}, u32[]{:S(2)}) collective-permute-start(f32[8,4,4,512]{3,0,2,1:T(8,128)} %get-tuple-element.291), channel_id=1, source_target_pairs={{0,4},{4,8},{8,12},{12,16},{16,20},{20,24},{24,28},{28,32},{32,36}... | collective-permute-start | bytes 786440 | tf_op jit(solution)/shard_map/while/body/eval_jaxpr/ppermute | solution.py:12
  640.6 10.9 %collective-permute-start = (f32[8,4,4,512]{3,0,2,1:T(8,128)}, f32[8,4,4,512]{3,0,2,1:T(8,128)S(1)}, u32[]{:S(2)}, u32[]{:S(2)}) collective-permute-start(f32[8,4,4,512]{3,0,2,1:T(8,128)} %get-tuple-element.291), channel_id=1, source_target_pairs={{0,4},{4,8},{8,12},{12,16},{16,20},{20,24},{24,28},{28,32},{32,36}... | collective-permute-start | bytes 786440 | tf_op jit(solution)/shard_map/while/body/eval_jaxpr/ppermute | solution.py:12
  651.5 10.9 %collective-permute-start = (f32[8,4,4,512]{3,0,2,1:T(8,128)}, f32[8,4,4,512]{3,0,2,1:T(8,128)S(1)}, u32[]{:S(2)}, u32[]{:S(2)}) collective-permute-start(f32[8,4,4,512]{3,0,2,1:T(8,128)} %get-tuple-element.291), channel_id=1, source_target_pairs={{0,4},{4,8},{8,12},{12,16},{16,20},{20,24},{24,28},{28,32},{32,36}... | collective-permute-start | bytes 786440 | tf_op jit(solution)/shard_map/while/body/eval_jaxpr/ppermute | solution.py:12
  673.3 10.9 %collective-permute-start = (f32[8,4,4,512]{3,0,2,1:T(8,128)}, f32[8,4,4,512]{3,0,2,1:T(8,128)S(1)}, u32[]{:S(2)}, u32[]{:S(2)}) collective-permute-start(f32[8,4,4,512]{3,0,2,1:T(8,128)} %get-tuple-element.291), channel_id=1, source_target_pairs={{0,4},{4,8},{8,12},{12,16},{16,20},{20,24},{24,28},{28,32},{32,36}... | collective-permute-start | bytes 786440 | tf_op jit(solution)/shard_map/while/body/eval_jaxpr/ppermute | solution.py:12
  684.2 10.9 %collective-permute-start = (f32[8,4,4,512]{3,0,2,1:T(8,128)}, f32[8,4,4,512]{3,0,2,1:T(8,128)S(1)}, u32[]{:S(2)}, u32[]{:S(2)}) collective-permute-start(f32[8,4,4,512]{3,0,2,1:T(8,128)} %get-tuple-element.291), channel_id=1, source_target_pairs={{0,4},{4,8},{8,12},{12,16},{16,20},{20,24},{24,28},{28,32},{32,36}... | collective-permute-start | bytes 786440 | tf_op jit(solution)/shard_map/while/body/eval_jaxpr/ppermute | solution.py:12
  706.0 10.9 %collective-permute-start = (f32[8,4,4,512]{3,0,2,1:T(8,128)}, f32[8,4,4,512]{3,0,2,1:T(8,128)S(1)}, u32[]{:S(2)}, u32[]{:S(2)}) collective-permute-start(f32[8,4,4,512]{3,0,2,1:T(8,128)} %get-tuple-element.291), channel_id=1, source_target_pairs={{0,4},{4,8},{8,12},{12,16},{16,20},{20,24},{24,28},{28,32},{32,36}... | collective-permute-start | bytes 786440 | tf_op jit(solution)/shard_map/while/body/eval_jaxpr/ppermute | solution.py:12
  716.9 10.9 %collective-permute-start = (f32[8,4,4,512]{3,0,2,1:T(8,128)}, f32[8,4,4,512]{3,0,2,1:T(8,128)S(1)}, u32[]{:S(2)}, u32[]{:S(2)}) collective-permute-start(f32[8,4,4,512]{3,0,2,1:T(8,128)} %get-tuple-element.291), channel_id=1, source_target_pairs={{0,4},{4,8},{8,12},{12,16},{16,20},{20,24},{24,28},{28,32},{32,36}... | collective-permute-start | bytes 786440 | tf_op jit(solution)/shard_map/while/body/eval_jaxpr/ppermute | solution.py:12
  (21 other events, 202.7 us)
where the time goes:
time: 745 us; the launch traced here: 743 us
  waiting for transfers between devices  592 us (79%)
  starting transfers between devices  126 us (17%)
  matrix products  16.9 us (2%)
    ppermute x66, waiting for transfers between devices, shifted_2(): return lax.ppermute(block, axis, route)  592 us
    ppermute x66, starting transfers between devices, shifted_2(): return lax.ppermute(block, axis, route)  126 us
  transfers between devices with their start and end apart: 66, of which 66 were waited for; matrix products, arithmetic and copies ran while one was open for 0% of the time, Pallas kernels for 0%

commit v1 on v0

v1 whole, which is shorter than its diff:
```python
import functools

import jax
import jax.numpy as jnp
from jax import lax
from jax.experimental import pallas as pl
from jax.experimental.pallas import tpu as pltpu
from jax.sharding import PartitionSpec as P

step_size = 0.25
GROUP = 8
PAD = 8


def fine_step(field, weight, bias):
    channels = field.shape[-1]
    height = field.shape[1]
    breadth = field.shape[2]
    lowered = field.astype(jnp.bfloat16)
    padded = jnp.pad(lowered, ((0, 0), (1, 1), (1, 1), (0, 0)))
    pieces = [
        padded[:, row_shift : row_shift + height, col_shift : col_shift + breadth, :]
        for row_shift in range(3)
        for col_shift in range(3)
    ]
    stacked = jnp.concatenate(pieces, axis=-1).reshape(-1, 9 * channels)
    mixed = jnp.dot(stacked, weight, preferred_element_type=jnp.float32).reshape(field.shape) + bias
    return field + step_size * jnp.tanh(mixed)


def coarse_step(field, weight, bias):
    channels = field.shape[-1]
    lowered = field.astype(jnp.bfloat16).reshape(-1, channels)
    centre = weight[4 * channels : 5 * channels]
    mixed = jnp.dot(lowered, centre, preferred_element_type=jnp.float32).reshape(field.shape) + bias
    return field + 2.0 * step_size * jnp.tanh(mixed)


def lower_kernel(*refs):
    out = refs[-1]
    halves = refs[:-1]
    for n, ref in enumerate(halves):
        rows = ref.shape[0]
        slot, part = divmod(n * rows, out.shape[1])
        out[slot, part : part + rows] = ref[...].astype(jnp.bfloat16)


def chain_kernel(turn, spots, state, centres, extras, starts_in, starts, end):
    del starts_in
    rows = state.shape[0]

    @pl.when(spots[0] == turn)
    def _():
        mine = spots[1]
        current = state[...]
        for at in range(GROUP):
            starts[at] = current
            mixed = jnp.dot(
                current.astype(jnp.bfloat16),
                centres[lax.bitwise_xor(mine, at)],
                preferred_element_type=jnp.float32,
            )
            bias = extras[at, rows : rows + 1]
            current = current + 2.0 * step_size * jnp.tanh(mixed + bias) + extras[at, :rows]
        end[...] = current


def solution(mesh):
    blocks = mesh.shape["layer"]
    parts = mesh.shape["batch"]
    groups = blocks // GROUP
    both = ("layer", "batch")

    def route(step):
        pairs = []
        for block in range(blocks):
            for part in range(parts):
                there, other = step(block, part)
                pairs.append((block * parts + part, there * parts + other))
        return pairs

    def upward(block, part):
        return block ^ 2, (part + ((block >> 1) & 1)) % parts

    def downward(block, part):
        return block ^ 2, (part + ((block >> 1) & 1) - 1) % parts

    up, down = route(upward), route(downward)
    beside = route(lambda block, part: (block ^ 4, part))
    twin = route(lambda block, part: (block ^ 1, part))

    def across(pair_of_halves):
        top, bottom = pair_of_halves
        return lax.ppermute(top, both, up), lax.ppermute(bottom, both, down)

    def swap(pair_of_halves, pairs):
        return tuple(lax.ppermute(half, both, pairs) for half in pair_of_halves)

    def shards(images, weights, biases):
        channels = images.shape[-1]
        position = lax.axis_index("layer")
        is_head = position == 0
        mine = position % GROUP
        spots = jnp.stack([position // GROUP, mine]).astype(jnp.int32)
        initial = images.astype(jnp.float32)
        cells = initial.shape[0] * initial.shape[1] * initial.shape[2]
        rows = cells // GROUP

        centre = weights[0, 4 * channels : 5 * channels].astype(jnp.float32)
        slots = [None] * GROUP
        slots[0] = (centre[: channels // 2], centre[channels // 2 :])
        slots[2] = across(slots[0])
        slots[4] = swap(slots[0], beside)
        slots[6] = across(slots[4])
        for at in range(0, GROUP, 2):
            slots[at + 1] = swap(slots[at], twin)

        guessed = fine_step(fine_step(initial, weights[0], biases[0]), weights[1], biases[1])
        incoming = lax.ppermute(guessed, "layer", [(i, i + 1) for i in range(blocks - 1)])
        shifted = jnp.where(is_head, initial, incoming)
        relaxed = fine_step(shifted, weights[0], biases[0])
        forcing = fine_step(relaxed, weights[1], biases[1]) - coarse_step(
            shifted, weights[0], biases[0]
        )
        teams = [[g * GROUP + i for i in range(GROUP)] for g in range(groups)]
        packed = jnp.concatenate(
            [
                forcing.reshape(GROUP, rows, channels),
                jnp.broadcast_to(biases[0], (GROUP, PAD, channels)),
            ],
            axis=1,
        )
        extras = lax.all_to_all(packed, "layer", 0, 0, axis_index_groups=teams)

        vmem = pl.BlockSpec(memory_space=pltpu.VMEM)
        smem = pl.BlockSpec(memory_space=pltpu.SMEM)
        centres = pl.pallas_call(
            lower_kernel,
            out_shape=jax.ShapeDtypeStruct((GROUP, channels, channels), jnp.bfloat16),
            in_specs=[vmem] * (2 * GROUP),
            out_specs=vmem,
            compiler_params=pltpu.CompilerParams(vmem_limit_bytes=32 << 20),
        )(*[half for slot in slots for half in slot])

        starts = jnp.zeros((GROUP, rows, channels), jnp.float32)
        state = lax.dynamic_slice_in_dim(initial.reshape(cells, channels), mine * rows, rows)
        for turn in range(groups):
            if turn:
                pairs = [((turn - 1) * GROUP + i, turn * GROUP + i) for i in range(GROUP)]
                state = lax.ppermute(state, "layer", pairs)
            starts, state = pl.pallas_call(
                functools.partial(chain_kernel, turn),
                out_shape=(
                    jax.ShapeDtypeStruct((GROUP, rows, channels), jnp.float32),
                    jax.ShapeDtypeStruct((rows, channels), jnp.float32),
                ),
                in_specs=[smem] + [vmem] * 4,
                out_specs=(vmem, vmem),
                input_output_aliases={4: 0},
                compiler_params=pltpu.CompilerParams(vmem_limit_bytes=32 << 20),
            )(spots, state, centres, extras, starts)

        predecessors = lax.all_to_all(starts, "layer", 0, 0, axis_index_groups=teams)
        predecessors = predecessors.reshape(initial.shape)
        solved = coarse_step(predecessors, weights[0], biases[0]) + forcing
        finished = fine_step(predecessors, weights[0], biases[0])
        return jnp.stack([finished, solved], axis=0)

    return jax.shard_map(
        shards,
        mesh=mesh,
        in_specs=(P("batch", None, None, None), P("layer", None, None), P("layer", None)),
        out_specs=P("layer", "batch", None, None, None),
        check_vma=False,
    )
```

time: 745 us -> 134 us (0.18)
  the two profiles are of different devices: /device:TPU:16 before, /device:TPU:92 now
where the time goes in v1:
time: 134 us
  waiting for transfers between devices  56.6 us (42%)
  starting transfers between devices  23.8 us (18%)
  local copies, waits for them, and re-layouts  16 us (12%)
  matrix products  13.6 us (10%)
  blocking collectives  11.8 us (9%)
  Pallas kernels  9.22 us (7%)
  other arithmetic  1.96 us (1%)
    ppermute x7, waiting for transfers between devices, shards(): state = lax.ppermute(state, 'layer', pairs)  39.1 us
    dot_general x5, matrix products, fine_step(): jnp.dot(stacked, weight, preferred_element_type=jnp.float32)  12.1 us
    all_to_all x1, blocking collectives, shards(): lax.all_to_all(starts, 'layer', 0, 0, axis_index_groups=teams)  11.8 us
    unnamed x59, local copies, waits for them, and re-layouts  8.58 us
    ppermute x10, waiting for transfers between devices, swap(): return tuple((lax.ppermute(half, both, pairs) for half in pair_of_halves))  7.92 us
    ppermute x4, starting transfers between devices, across(): return (lax.ppermute(top, both, up), lax.ppermute(bottom, both, down))  6.62 us
    pallas_call x8, Pallas kernels, shards(): pl.pallas_call(functools.partial(chain_kernel, turn), out_shape=(jax.Shap...  6.34 us
    ppermute x4, waiting for transfers between devices, across(): return (lax.ppermute(top, both, up), lax.ppermute(bottom, both, down))  6.23 us
  transfers between devices with their start and end apart: 23, of which 6 were waited for; matrix products, arithmetic and copies ran while one was open for 11% of the time, Pallas kernels for 2%

profile of v1, /device:TPU:92, one launch (start us, length us, event | category | flops | bytes accessed | tf_op | source)
XLA Modules:
  0.0 133.8 jit_solution(18336856820033780918)
XLA Ops:
  0.0 0.8 fusion.135
  0.8 1.0 copy.12
  1.8 0.8 copy_convert_fusion
  2.7 3.4 %fusion.136 = (bf16[8,4,4,512]{3,0,2,1:T(8,128)(2,1)S(1)}, f32[8,4,4,512]{3,0,2,1:T(8,128)S(1)}) fusion(f32[512]{0:T(512)S(1)} %bitcast.104, bf16[8,4,4,4608]{3,0,2,1:T(8,128)(2,1)S(1)} %fusion.100, bf16[2,4608,512]{2,1,0:T(8,128)(2,1)} %param.4, bf16[8,4,4,512]{3,2,1,0:T(4,128)(2,1)S(1)} %copy-done.3), kind=kOutput, calls=%fused_computation.146 | convolution fusion | flops 604307456 | bytes 6424576 | tf_op jit(solution)/shard_map/dot_general | solution.py:27
  6.2 1.6 %copy-done.6 = bf16[2,4608,512]{2,1,0:T(8,128)(2,1)S(1)} copy-done((bf16[2,4608,512]{2,1,0:T(8,128)(2,1)S(1)}, bf16[2,4608,512]{2,1,0:T(8,128)(2,1)}, u32[]{:S(2)}) %copy-start.6) | copy-done | bytes 9437208
  7.8 1.5 %fusion.56 = f32[8,4,4,512]{3,0,2,1:T(8,128)} fusion(f32[8,4,4,512]{3,0,2,1:T(8,128)S(1)} %get-tuple-element.42, bf16[8,4,4,4608]{3,0,2,1:T(8,128)(2,1)S(1)} %fusion.108, bf16[2,4608,512]{2,1,0:T(8,128)(2,1)S(1)} %copy-done.6, f32[512]{0:T(512)S(1)} %bitcast.110), kind=kOutput, calls=%fused_computation.36 | convolution fusion | flops 604176384 | bytes 6424576 | tf_op jit(solution)/shard_map/dot_general | solution.py:27
  9.3 1.9 %collective-permute-start.14 = (f32[8,4,4,512]{3,0,2,1:T(8,128)}, f32[8,4,4,512]{3,0,2,1:T(8,128)S(1)}, u32[]{:S(2)}, u32[]{:S(2)}) collective-permute-start(f32[8,4,4,512]{3,0,2,1:T(8,128)} %fusion.56), channel_id=1, source_target_pairs={{0,4},{4,8},{8,12},{12,16},{16,20},{20,24},{24,28},{28,32},{32,36}... | collective-permute-start | bytes 786440 | tf_op jit(solution)/shard_map/ppermute | solution.py:119
  11.4 2.1 %collective-permute-start = (f32[256,512]{1,0:T(8,128)S(1)}, f32[256,512]{1,0:T(8,128)S(1)}, u32[]{:S(2)}, u32[]{:S(2)}) collective-permute-start(f32[256,512]{1,0:T(8,128)S(1)} %get-tuple-element.36.refs_0_), channel_id=1, source_target_pairs={{0,4},{1,5},{2,6},{3,7},{4,0},{5,1},{6,2},{7,3},{8,12},{9,13},{10,... | collective-permute-start | bytes 1572872 | tf_op jit(solution)/shard_map/ppermute | solution.py:97
  13.5 0.7 collective-permute-start.2
  14.7 3.4 %collective-permute-done.14 = f32[8,4,4,512]{3,0,2,1:T(8,128)S(1)} collective-permute-done((f32[8,4,4,512]{3,0,2,1:T(8,128)}, f32[8,4,4,512]{3,0,2,1:T(8,128)S(1)}, u32[]{:S(2)}, u32[]{:S(2)}) %collective-permute-start.14) | collective-permute-done | bytes 262176 | tf_op jit(solution)/shard_map/ppermute | solution.py:119
  18.1 1.3 collective-permute-start.7
  19.7 3.1 %fusion.137 = (bf16[8,4,4,512]{3,0,2,1:T(8,128)(2,1)S(1)}, f32[8,4,4,512]{3,0,2,1:T(8,128)S(1)}) fusion(f32[512]{0:T(512)S(1)} %bitcast.105, bf16[8,4,4,4608]{3,0,2,1:T(8,128)(2,1)S(1)} %fusion.116, bf16[2,4608,512]{2,1,0:T(8,128)(2,1)} %param.4, f32[8,4,4,512]{3,0,2,1:T(8,128)S(1)} %collective-permute-done.14, bf16[8,4,4,512]{3,2,1,0:T(4,128)(2,1)S(1)} %copy-done.3, ...), kind=kOutput, calls=%fused_computation.147 | convolution fusion | flops 604372992 | bytes 6686721 | tf_op jit(solution)/shard_map/dot_general | solution.py:27
  23.0 1.3 fusion.22
  24.3 1.2 collective-permute-start.3
  25.5 1.9 %collective-permute-done.2.refs_4_ = f32[256,512]{1,0:T(8,128)S(1)} collective-permute-done((f32[256,512]{1,0:T(8,128)S(1)}, f32[256,512]{1,0:T(8,128)S(1)}, u32[]{:S(2)}, u32[]{:S(2)}) %collective-permute-start.2) | collective-permute-done | bytes 524320 | tf_op jit(solution)/shard_map/ppermute | solution.py:94
  28.0 1.1 collective-permute-done.6.refs_8_
  29.1 3.4 %collective-permute-start.10 = (f32[256,512]{1,0:T(8,128)S(1)}, f32[256,512]{1,0:T(8,128)}, u32[]{:S(2)}, u32[]{:S(2)}) collective-permute-start(f32[256,512]{1,0:T(8,128)S(1)} %collective-permute-done.6.refs_8_), channel_id=1, source_target_pairs={{0,8},{1,9},{2,10},{3,11},{4,12},{5,13},{6,14},{7,15},{8,1},{9,2},... | collective-permute-start | bytes 1572872 | tf_op jit(solution)/shard_map/ppermute | solution.py:94
  32.5 6.8 %collective-permute-done.7.refs_9_ = f32[256,512]{1,0:T(8,128)} collective-permute-done((f32[256,512]{1,0:T(8,128)S(1)}, f32[256,512]{1,0:T(8,128)}, u32[]{:S(2)}, u32[]{:S(2)}) %collective-permute-start.7) | collective-permute-done | bytes 524320 | tf_op jit(solution)/shard_map/ppermute | solution.py:97
  39.3 1.2 collective-permute-start.11
  40.5 3.2 %fusion.47 = f32[8,4,4,512]{3,0,2,1:T(8,128)S(1)} fusion(f32[8,4,4,512]{3,0,2,1:T(8,128)S(1)} %fusion.22, f32[8,4,4,512]{3,0,2,1:T(8,128)S(1)} %get-tuple-element.44, bf16[8,4,4,4608]{3,0,2,1:T(8,128)(2,1)S(1)} %fusion.124, bf16[2,4608,512]{2,1,0:T(8,128)(2,1)} %param.4, f32[512]{0:T(512)S(1)} %bitcast.111), kind=kOutput, calls=%fused_computation.33 | convolution fusion | flops 604241920 | bytes 6686720 | tf_op jit(solution)/shard_map/dot_general | solution.py:27
  43.8 0.7 copy-done.4
  44.6 0.8 pad_maximum_fusion.1
  45.4 4.1 %all-to-all-start = ((f32[8,24,512]{2,1,0:T(8,128)}), f32[8,24,512]{2,1,0:T(8,128)S(1)}, u32[]{:S(2)}, u32[]{:S(2)}) async-start(f32[8,24,512]{2,1,0:T(8,128)} %pad_maximum_fusion.1), calls=%async_computation | async-start | bytes 786432 | tf_op jit(solution)/shard_map/all_to_all | solution.py:133
  50.8 4.3 %collective-permute-done.11.refs_13_ = f32[256,512]{1,0:T(8,128)} collective-permute-done((f32[256,512]{1,0:T(8,128)}, f32[256,512]{1,0:T(8,128)}, u32[]{:S(2)}, u32[]{:S(2)}) %collective-permute-start.11) | collective-permute-done | bytes 524320 | tf_op jit(solution)/shard_map/ppermute | solution.py:94
  55.1 1.8 %copy.13 = f32[8,4,4,512]{3,2,1,0:T(4,128)} copy(f32[8,4,4,512]{3,0,2,1:T(8,128)} %get-tuple-element.37) | data formatting | bytes 524288 | tf_op jit(solution)/shard_map/convert_element_type | solution.py:105
  56.9 1.8 %reshape.42 = f32[128,512]{1,0:T(8,128)} reshape(f32[8,4,4,512]{3,2,1,0:T(4,128)} %copy.13) | data formatting | bytes 524288 | tf_op jit(solution)/shard_map/reshape | solution.py:146
  58.8 1.4 %constant_dynamic-slice_fusion.state = f32[16,512]{1,0:T(8,128)} fusion(f32[128,512]{1,0:T(8,128)} %reshape.42, s32[]{:T(128)S(6)} %select_n.24), kind=kLoop, calls=%fused_computation.142 | loop fusion | bytes 65540 | tf_op jit(solution)/shard_map/dynamic_slice | solution.py:146
  60.2 2.9 %shard_map.37.centres = bf16[8,512,512]{2,1,0:T(8,128)(2,1)S(1)} custom-call(f32[256,512]{1,0:T(8,128)S(1)} %get-tuple-element.36.refs_0_, f32[256,512]{1,0:T(8,128)S(1)} %get-tuple-element.35.refs_1_, f32[256,512]{1,0:T(8,128)S(1)} %collective-permute-done.refs_2_, f32[256,512]{1,0:T(8,128)S(1)} %collective-permute-done.1.refs_3_, ...), custom_call_target="tpu_custom_call" | custom-call | tf_op jit(solution)/shard_map/pallas_call | solution.py:137
  63.0 1.9 %copy-done = bf16[8,512,512]{2,1,0:T(8,128)(2,1)} copy-done((bf16[8,512,512]{2,1,0:T(8,128)(2,1)}, bf16[8,512,512]{2,1,0:T(8,128)(2,1)S(1)}, u32[]{:S(2)}) %copy-start) | copy-done | bytes 4194328
  65.0 2.2 %copy-done.1 = bf16[8,512,512]{2,1,0:T(8,128)(2,1)S(1)} copy-done((bf16[8,512,512]{2,1,0:T(8,128)(2,1)S(1)}, bf16[8,512,512]{2,1,0:T(8,128)(2,1)}, u32[]{:S(2)}) %copy-start.1) | copy-done | bytes 4194328
  67.2 0.8 copy-done.2
  68.5 0.7 collective-permute-start.15
  69.2 0.6 shard_map.39
  69.8 0.7 collective-permute-start.16
  70.5 0.6 shard_map.40
  71.0 0.7 collective-permute-start.17
  71.7 0.6 shard_map.41
  72.2 0.7 collective-permute-start.18
  72.9 0.6 shard_map.42
  73.5 0.8 collective-permute-start.19
  74.9 0.8 collective-permute-start.20
  75.7 0.6 shard_map.44
  76.3 1.3 collective-permute-start.21
  77.6 39.1 %collective-permute-done.21.state = f32[16,512]{1,0:T(8,128)S(1)} collective-permute-done((f32[16,512]{1,0:T(8,128)S(1)}, f32[16,512]{1,0:T(8,128)S(1)}, u32[]{:S(2)}, u32[]{:S(2)}) %collective-permute-start.21) | collective-permute-done | bytes 32800 | tf_op jit(solution)/shard_map/ppermute | solution.py:150
  116.7 2.5 %shard_map.45 = (f32[8,16,512]{2,1,0:T(8,128)S(1)}, f32[16,512]{1,0:T(8,128)}) custom-call(s32[2]{0:T(128)S(1)} %pad_add_fusion.spots, f32[16,512]{1,0:T(8,128)S(1)} %collective-permute-done.21.state, bf16[8,512,512]{2,1,0:T(8,128)(2,1)S(1)} %copy-done.1, f32[8,24,512]{2,1,0:T(8,128)S(1)} %all-to-all-done.extras, ...), custom_call_target="tpu_custom_call", output_to_operand_aliasing={{0}: (4, {})} | custom-call | tf_op jit(solution)/shard_map/pallas_call | solution.py:151
  119.2 11.8 %all_to_all.10 = f32[8,16,512]{2,1,0:T(8,128)S(1)} all-to-all(f32[8,16,512]{2,1,0:T(8,128)S(1)} %get-tuple-element.34), channel_id=1, replica_groups={{0,4,8,12,16,20,24,28},{32,36,40,44,48,52,56,60},{64,68,72,76,80,84,88,..., dimensions={0} | all-to-all | bytes 524288 | tf_op jit(solution)/shard_map/all_to_all | solution.py:163
  131.8 0.9 fusion.68
  132.7 1.1 copy.21
  (100 shorter events, 5.0 us)
Async XLA Ops:
  0.0 1.8 %copy-start.3 = (bf16[8,4,4,512]{3,2,1,0:T(4,128)(2,1)S(1)}, bf16[8,4,4,512]{3,2,1,0:T(4,128)(2,1)}, u32[]{:S(2)}) copy-start(bf16[8,4,4,512]{3,2,1,0:T(4,128)(2,1)} %param.3) | copy-start | bytes 393220
  2.7 5.1 %copy-start.6 = (bf16[2,4608,512]{2,1,0:T(8,128)(2,1)S(1)}, bf16[2,4608,512]{2,1,0:T(8,128)(2,1)}, u32[]{:S(2)}) copy-start(bf16[2,4608,512]{2,1,0:T(8,128)(2,1)} %param.4) | copy-start | bytes 28311556
  9.3 8.8 %collective-permute-start.14 = (f32[8,4,4,512]{3,0,2,1:T(8,128)}, f32[8,4,4,512]{3,0,2,1:T(8,128)S(1)}, u32[]{:S(2)}, u32[]{:S(2)}) collective-permute-start(f32[8,4,4,512]{3,0,2,1:T(8,128)} %fusion.56), channel_id=1, source_target_pairs={{0,4},{4,8},{8,12},{12,16},{16,20},{20,24},{24,28},{28,32},{32,36}... | collective-permute-start | bytes 786440 | tf_op jit(solution)/shard_map/ppermute | solution.py:119
  11.4 12.9 %collective-permute-start = (f32[256,512]{1,0:T(8,128)S(1)}, f32[256,512]{1,0:T(8,128)S(1)}, u32[]{:S(2)}, u32[]{:S(2)}) collective-permute-start(f32[256,512]{1,0:T(8,128)S(1)} %get-tuple-element.36.refs_0_), channel_id=1, source_target_pairs={{0,4},{1,5},{2,6},{3,7},{4,0},{5,1},{6,2},{7,3},{8,12},{9,13},{10,... | collective-permute-start | bytes 1572872 | tf_op jit(solution)/shard_map/ppermute | solution.py:97
  13.5 13.9 %collective-permute-start.2 = (f32[256,512]{1,0:T(8,128)S(1)}, f32[256,512]{1,0:T(8,128)S(1)}, u32[]{:S(2)}, u32[]{:S(2)}) collective-permute-start(f32[256,512]{1,0:T(8,128)S(1)} %get-tuple-element.36.refs_0_), channel_id=1, source_target_pairs={{0,8},{1,9},{2,10},{3,11},{4,12},{5,13},{6,14},{7,15},{8,1},{9,2},... | collective-permute-start | bytes 1572872 | tf_op jit(solution)/shard_map/ppermute | solution.py:94
  14.3 14.8 %collective-permute-start.6 = (f32[256,512]{1,0:T(8,128)S(1)}, f32[256,512]{1,0:T(8,128)S(1)}, u32[]{:S(2)}, u32[]{:S(2)}) collective-permute-start(f32[256,512]{1,0:T(8,128)S(1)} %get-tuple-element.36.refs_0_), channel_id=1, source_target_pairs={{0,16},{1,17},{2,18},{3,19},{4,20},{5,21},{6,22},{7,23},{8,24},{9,... | collective-permute-start | bytes 1572872 | tf_op jit(solution)/shard_map/ppermute | solution.py:97
  14.7 34.8 %collective-permute-start.1 = (f32[256,512]{1,0:T(8,128)S(1)}, f32[256,512]{1,0:T(8,128)S(1)}, u32[]{:S(2)}, u32[]{:S(2)}) collective-permute-start(f32[256,512]{1,0:T(8,128)S(1)} %get-tuple-element.35.refs_1_), channel_id=1, source_target_pairs={{0,4},{1,5},{2,6},{3,7},{4,0},{5,1},{6,2},{7,3},{8,12},{9,13},{10,... | collective-permute-start | bytes 1572872 | tf_op jit(solution)/shard_map/ppermute | solution.py:97
  18.1 21.2 %collective-permute-start.7 = (f32[256,512]{1,0:T(8,128)S(1)}, f32[256,512]{1,0:T(8,128)}, u32[]{:S(2)}, u32[]{:S(2)}) collective-permute-start(f32[256,512]{1,0:T(8,128)S(1)} %get-tuple-element.35.refs_1_), channel_id=1, source_target_pairs={{0,16},{1,17},{2,18},{3,19},{4,20},{5,21},{6,22},{7,23},{8,24},{9,... | collective-permute-start | bytes 1572872 | tf_op jit(solution)/shard_map/ppermute | solution.py:97
  24.3 25.7 %collective-permute-start.3 = (f32[256,512]{1,0:T(8,128)S(1)}, f32[256,512]{1,0:T(8,128)}, u32[]{:S(2)}, u32[]{:S(2)}) collective-permute-start(f32[256,512]{1,0:T(8,128)S(1)} %get-tuple-element.35.refs_1_), channel_id=1, source_target_pairs={{0,11},{1,8},{2,9},{3,10},{4,15},{5,12},{6,13},{7,14},{8,0},{9,1},... | collective-permute-start | bytes 1572872 | tf_op jit(solution)/shard_map/ppermute | solution.py:94
  27.5 22.7 %collective-permute-start.4 = (f32[256,512]{1,0:T(8,128)S(1)}, f32[256,512]{1,0:T(8,128)}, u32[]{:S(2)}, u32[]{:S(2)}) collective-permute-start(f32[256,512]{1,0:T(8,128)S(1)} %collective-permute-done.2.refs_4_), channel_id=1, source_target_pairs={{0,4},{1,5},{2,6},{3,7},{4,0},{5,1},{6,2},{7,3},{8,12},{9,13},{10,... | collective-permute-start | bytes 1572872 | tf_op jit(solution)/shard_map/ppermute | solution.py:97
  29.1 21.4 %collective-permute-start.10 = (f32[256,512]{1,0:T(8,128)S(1)}, f32[256,512]{1,0:T(8,128)}, u32[]{:S(2)}, u32[]{:S(2)}) collective-permute-start(f32[256,512]{1,0:T(8,128)S(1)} %collective-permute-done.6.refs_8_), channel_id=1, source_target_pairs={{0,8},{1,9},{2,10},{3,11},{4,12},{5,13},{6,14},{7,15},{8,1},{9,2},... | collective-permute-start | bytes 1572872 | tf_op jit(solution)/shard_map/ppermute | solution.py:94
  39.3 15.8 %collective-permute-start.11 = (f32[256,512]{1,0:T(8,128)}, f32[256,512]{1,0:T(8,128)}, u32[]{:S(2)}, u32[]{:S(2)}) collective-permute-start(f32[256,512]{1,0:T(8,128)} %collective-permute-done.7.refs_9_), channel_id=1, source_target_pairs={{0,11},{1,8},{2,9},{3,10},{4,15},{5,12},{6,13},{7,14},{8,0},{9,1},... | collective-permute-start | bytes 1572872 | tf_op jit(solution)/shard_map/ppermute | solution.py:94
  43.8 0.7 copy-start.4
  45.4 19.6 %all-to-all-start = ((f32[8,24,512]{2,1,0:T(8,128)}), f32[8,24,512]{2,1,0:T(8,128)S(1)}, u32[]{:S(2)}, u32[]{:S(2)}) async-start(f32[8,24,512]{2,1,0:T(8,128)} %pad_maximum_fusion.1), calls=%async_computation | async-start | bytes 786432 | tf_op jit(solution)/shard_map/all_to_all | solution.py:133
  49.5 10.6 %collective-permute-start.8 = (f32[256,512]{1,0:T(8,128)S(1)}, f32[256,512]{1,0:T(8,128)}, u32[]{:S(2)}, u32[]{:S(2)}) collective-permute-start(f32[256,512]{1,0:T(8,128)S(1)} %collective-permute-done.6.refs_8_), channel_id=1, source_target_pairs={{0,4},{1,5},{2,6},{3,7},{4,0},{5,1},{6,2},{7,3},{8,12},{9,13},{10,... | collective-permute-start | bytes 1572872 | tf_op jit(solution)/shard_map/ppermute | solution.py:97
  50.0 10.1 %collective-permute-start.9 = (f32[256,512]{1,0:T(8,128)}, f32[256,512]{1,0:T(8,128)}, u32[]{:S(2)}, u32[]{:S(2)}) collective-permute-start(f32[256,512]{1,0:T(8,128)} %collective-permute-done.7.refs_9_), channel_id=1, source_target_pairs={{0,4},{1,5},{2,6},{3,7},{4,0},{5,1},{6,2},{7,3},{8,12},{9,13},{10,... | collective-permute-start | bytes 1572872 | tf_op jit(solution)/shard_map/ppermute | solution.py:97
  50.1 10.0 %collective-permute-start.5 = (f32[256,512]{1,0:T(8,128)}, f32[256,512]{1,0:T(8,128)}, u32[]{:S(2)}, u32[]{:S(2)}) collective-permute-start(f32[256,512]{1,0:T(8,128)} %collective-permute-done.3.refs_5_), channel_id=1, source_target_pairs={{0,4},{1,5},{2,6},{3,7},{4,0},{5,1},{6,2},{7,3},{8,12},{9,13},{10,... | collective-permute-start | bytes 1572872 | tf_op jit(solution)/shard_map/ppermute | solution.py:97
  50.5 9.6 %collective-permute-start.12 = (f32[256,512]{1,0:T(8,128)}, f32[256,512]{1,0:T(8,128)}, u32[]{:S(2)}, u32[]{:S(2)}) collective-permute-start(f32[256,512]{1,0:T(8,128)} %collective-permute-done.10.refs_12_), channel_id=1, source_target_pairs={{0,4},{1,5},{2,6},{3,7},{4,0},{5,1},{6,2},{7,3},{8,12},{9,13},{10,... | collective-permute-start | bytes 1572872 | tf_op jit(solution)/shard_map/ppermute | solution.py:97
  55.1 5.0 %collective-permute-start.13 = (f32[256,512]{1,0:T(8,128)}, f32[256,512]{1,0:T(8,128)}, u32[]{:S(2)}, u32[]{:S(2)}) collective-permute-start(f32[256,512]{1,0:T(8,128)} %collective-permute-done.11.refs_13_), channel_id=1, source_target_pairs={{0,4},{1,5},{2,6},{3,7},{4,0},{5,1},{6,2},{7,3},{8,12},{9,13},{10,... | collective-permute-start | bytes 1572872 | tf_op jit(solution)/shard_map/ppermute | solution.py:97
  63.0 2.0 %copy-start = (bf16[8,512,512]{2,1,0:T(8,128)(2,1)}, bf16[8,512,512]{2,1,0:T(8,128)(2,1)S(1)}, u32[]{:S(2)}) copy-start(bf16[8,512,512]{2,1,0:T(8,128)(2,1)S(1)} %shard_map.37.centres) | copy-start | bytes 12582916
  65.0 2.2 %copy-start.1 = (bf16[8,512,512]{2,1,0:T(8,128)(2,1)S(1)}, bf16[8,512,512]{2,1,0:T(8,128)(2,1)}, u32[]{:S(2)}) copy-start(bf16[8,512,512]{2,1,0:T(8,128)(2,1)} %copy-done) | copy-start | bytes 12582916
  67.2 0.8 copy-start.2
  68.5 0.7 collective-permute-start.15
  69.8 0.7 collective-permute-start.16
  71.0 0.7 collective-permute-start.17
  72.2 0.7 collective-permute-start.18
  72.9 58.3 %slice-start = ((s8[9437184]{0:T(1024)(128)(4,1)}), s8[4194304]{0:T(1024)(128)(4,1)S(1)}, s32[]{:S(2)}) async-start(s8[9437184]{0:T(1024)(128)(4,1)} %bitcast.102), calls=%async_computation.2 | async-start | bytes 8388608
  73.5 0.8 collective-permute-start.19
  74.3 57.0 %slice-start.1 = ((s8[9437184]{0:T(1024)(128)(4,1)}), s8[4194304]{0:T(1024)(128)(4,1)S(1)}, s32[]{:S(2)}) async-start(s8[9437184]{0:T(1024)(128)(4,1)} %bitcast.102), calls=%async_computation.3 | async-start | bytes 8388608
  74.9 0.8 collective-permute-start.20
  75.7 55.6 %slice-start.2 = ((s8[9437184]{0:T(1024)(128)(4,1)}), s8[1048576]{0:T(1024)(128)(4,1)S(1)}, s32[]{:S(2)}) async-start(s8[9437184]{0:T(1024)(128)(4,1)} %bitcast.102), calls=%async_computation.4 | async-start | bytes 2097152
  76.3 40.4 %collective-permute-start.21 = (f32[16,512]{1,0:T(8,128)S(1)}, f32[16,512]{1,0:T(8,128)S(1)}, u32[]{:S(2)}, u32[]{:S(2)}) collective-permute-start(f32[16,512]{1,0:T(8,128)S(1)} %get-tuple-element.32), channel_id=1, source_target_pairs={{192,224},{196,228},{200,232},{204,236},{208,240},{212,244},{216,2... | collective-permute-start | bytes 98312 | tf_op jit(solution)/shard_map/ppermute | solution.py:150
  119.2 12.1 %copy-start.5 = (f32[8,4,4,512]{3,0,2,1:T(8,128)S(1)}, f32[8,4,4,512]{3,0,2,1:T(8,128)}, u32[]{:S(2)}) copy-start(f32[8,4,4,512]{3,0,2,1:T(8,128)} %copy-done.4) | copy-start | bytes 786436

commit v2 on v0

v2 whole, which is shorter than its diff:
```python
import functools

import jax
import jax.numpy as jnp
from jax import lax
from jax.experimental import pallas as pl
from jax.experimental.pallas import tpu as pltpu
from jax.sharding import PartitionSpec as P

step_size = 0.25
GROUP = 8
PAD = 8
FLIPS = (0, 5, 0, 5, 4, 1, 4, 1)
SIDE = 4
IMAGES = 8
LANES = 128
MIB = 1 << 20

VMEM = pl.BlockSpec(memory_space=pltpu.VMEM)
ANY = pl.BlockSpec(memory_space=pl.ANY)
HBM = pl.BlockSpec(memory_space=pltpu.HBM)


def call(kernel, out_shape, operands, scratch=(), limit=8, flops=0, aliases=None, specs=None, out_specs=None):
    single = not isinstance(out_shape, (tuple, list))
    results = (out_shape,) if single else out_shape
    return pl.pallas_call(
        kernel,
        out_shape=out_shape,
        in_specs=specs or [VMEM] * len(operands),
        out_specs=out_specs or (VMEM if single else [VMEM for _ in out_shape]),
        scratch_shapes=list(scratch),
        input_output_aliases=aliases or {},
        compiler_params=pltpu.CompilerParams(vmem_limit_bytes=limit * MIB),
        cost_estimate=pl.CostEstimate(flops=0, bytes_accessed=0, transcendentals=0),
    )(*operands)


def f32(*shape):
    return jax.ShapeDtypeStruct(shape, jnp.float32)


def spread(field, columns):
    channels = field.shape[-1]
    cells = [field[IMAGES * at : IMAGES * (at + 1)] for at in range(SIDE * SIDE)]
    nothing = jnp.zeros_like(cells[0])
    for tap in range(9):
        down, right = tap // 3 - 1, tap % 3 - 1
        pieces = []
        for row in range(SIDE):
            for col in range(SIDE):
                inside = 0 <= row + down < SIDE and 0 <= col + right < SIDE
                pieces.append(cells[(row + down) * SIDE + col + right] if inside else nothing)
        columns[:, tap * channels : (tap + 1) * channels] = jnp.concatenate(pieces, axis=0).astype(
            jnp.bfloat16
        )


def fine(field, weights, biases, layer, columns):
    spread(field, columns)
    mixed = jnp.dot(columns[...], weights[layer], preferred_element_type=jnp.float32)
    return field + step_size * jnp.tanh(mixed + biases[layer : layer + 1])


def coarse(field, centre, bias):
    mixed = jnp.dot(field.astype(jnp.bfloat16), centre, preferred_element_type=jnp.float32)
    return field + 2.0 * step_size * jnp.tanh(mixed + bias)


def flip_of(position):
    group = lax.div(position, GROUP)
    other_x = lax.bitwise_and(lax.bitwise_xor(group, lax.div(group, 4)), 1)
    return lax.bitwise_or(4 * other_x, lax.bitwise_and(group, 1))


def centre_kernel(weights, biases, whole, landing, sem):
    channels = whole.shape[1]
    copy = pltpu.make_async_copy(weights.at[0, pl.ds(4 * channels, channels)], landing, sem)
    copy.start()
    whole[channels:] = jnp.broadcast_to(biases[0:1], (PAD, channels))
    copy.wait()
    whole[:channels] = landing[...].astype(jnp.float32)


def guess_kernel(initial, weights, biases, guessed, columns):
    first = fine(initial[...], weights, biases, 0, columns)
    guessed[...] = fine(first, weights, biases, 1, columns)


def force_kernel(incoming, initial, weights, biases, packed, columns):
    position = lax.axis_index("layer")
    rows, channels = packed.shape[1:]
    begin = jnp.where(position == 0, initial[...], incoming[...])
    relaxed = fine(begin, weights, biases, 0, columns)
    after = fine(relaxed, weights, biases, 1, columns)
    forcing = after - coarse(
        begin, weights[0, 4 * channels : 5 * channels], biases[0:1]
    )
    flip = flip_of(position)
    for lane in range(GROUP):
        spot = lax.bitwise_xor(flip, lane)
        packed[spot] = forcing[lane * rows : (lane + 1) * rows]


def hold_kernel(*refs):
    del refs


def lower_kernel(begin, count, *refs):
    centres, offsets = refs[-2:]
    channels = centres.shape[1]
    for n in range(count):
        centres[begin + n] = refs[n][:channels].astype(jnp.bfloat16)
        offsets[begin + n] = refs[n][channels:]


def chain_kernel(turn, state, near, near_bias, far, far_bias, extras, *refs):
    starts, end = refs[-2:]
    rows = end.shape[0]
    position = lax.axis_index("layer")
    mine = lax.rem(position, GROUP)

    def walk(order):
        if turn:
            current = state[...]
        else:
            current = state[pl.ds(pl.multiple_of(mine * rows, rows), rows)]
        for at in range(GROUP):
            starts[at] = current
            centres, offsets = order[at // 4]
            slot = lax.bitwise_and(lax.bitwise_xor(mine, at), 3)
            current = coarse(current, centres[slot], offsets[slot, 0:1]) + extras[at]
        end[...] = current

    first, second = (near, near_bias), (far, far_bias)
    here = lax.div(position, GROUP) == turn
    pl.when(here & (mine < 4))(lambda: walk((first, second)))
    pl.when(here & (mine >= 4))(lambda: walk((second, first)))


def finish_kernel(arrived, packed, weights, biases, states, columns, whole):
    position = lax.axis_index("layer")
    channels = arrived.shape[2]
    flip = flip_of(position)
    begin = jnp.concatenate([arrived[lax.bitwise_xor(flip, lane)] for lane in range(GROUP)], axis=0)
    forcing = jnp.concatenate(
        [packed[lax.bitwise_xor(flip, lane)] for lane in range(GROUP)], axis=0
    )
    solved = coarse(begin, weights[0, 4 * channels : 5 * channels], biases[0:1]) + forcing
    finished = fine(begin, weights, biases, 0, columns)
    for layer, value in ((1, solved), (0, finished)):
        for band in range(channels // LANES):
            across = slice(band * LANES, (band + 1) * LANES)
            whole[layer, band] = value[:, across]
            for image in range(IMAGES):
                for row in range(SIDE):
                    states[layer, image, row, :, across] = whole[
                        layer, band, pl.ds(row * SIDE * IMAGES + image, SIDE, stride=IMAGES), :
                    ]


def solution(mesh):
    blocks = mesh.shape["layer"]
    parts = mesh.shape["batch"]
    groups = blocks // GROUP
    both = ("layer", "batch")

    def route(step):
        pairs = []
        for block in range(blocks):
            for part in range(parts):
                there, other = step(block, part)
                pairs.append((block * parts + part, there * parts + other))
        return pairs

    def over(block, part):
        return block ^ 2, (part + ((block >> 1) & 1) - (block & 1)) % parts

    behind = route(over)
    beside = route(lambda block, part: (block ^ 4, part))
    twin = route(lambda block, part: (block ^ 1, part))

    def shards(images, weights, biases):
        channels = images.shape[-1]
        cells = IMAGES * SIDE * SIDE
        rows = cells // GROUP
        columns = pltpu.VMEM((cells, 9 * channels), jnp.bfloat16)
        conv = 2 * cells * 9 * channels * channels

        own = call(
            centre_kernel,
            pltpu.VMEM((channels + PAD, channels), jnp.float32),
            (pltpu.with_memory_space_constraint(weights, pltpu.HBM), biases),
            scratch=[pltpu.VMEM((channels, channels), jnp.bfloat16), pltpu.SemaphoreType.DMA],
            specs=[HBM, VMEM],
        )
        beside_x = lax.ppermute(own, both, beside)
        behind_z = lax.ppermute(own, both, behind)

        initial = images.astype(jnp.float32).reshape(IMAGES, SIDE * SIDE, channels)
        initial = jnp.transpose(initial, (1, 0, 2)).reshape(cells, channels)
        guessed = call(
            guess_kernel, f32(cells, channels), (initial, weights, biases), [columns], flops=2 * conv
        )
        incoming = lax.ppermute(guessed, "layer", [(i, i + 1) for i in range(blocks - 1)])
        packed = call(
            force_kernel,
            f32(GROUP, rows, channels),
            (incoming, initial, weights, biases),
            [columns],
            flops=2 * conv,
        )
        teams = [[g * GROUP + i for i in range(GROUP)] for g in range(groups)]
        extras = lax.all_to_all(packed, "layer", 0, 0, axis_index_groups=teams)

        def hold(each, *after):
            return call(
                hold_kernel,
                f32(*each.shape),
                (each, *after),
                specs=[ANY] * (1 + len(after)),
                out_specs=ANY,
                aliases={0: 0},
            )

        def lowered(begin, pieces, held=()):
            return call(
                functools.partial(lower_kernel, begin, len(pieces)),
                (
                    pltpu.VMEM((4, channels, channels), jnp.bfloat16),
                    pltpu.VMEM((4, PAD, channels), jnp.float32),
                ),
                (*pieces, *held),
                aliases={len(pieces) + n: n for n in range(len(held))},
            )

        behind_z = hold(behind_z, packed)
        beside_x = hold(beside_x, packed)
        held = hold(own, extras)
        corner = lax.ppermute(beside_x, both, behind)
        own_twin = lax.ppermute(held, both, twin)
        behind_twin = lax.ppermute(behind_z, both, twin)
        beside_twin = lax.ppermute(beside_x, both, twin)
        near = lowered(0, (held, own_twin, behind_z, behind_twin))
        far = lowered(0, (beside_x, beside_twin))
        corner = hold(corner, near[1])
        far = lowered(2, (corner, lax.ppermute(corner, both, twin)), far)

        state = initial
        starts = None
        for turn in range(groups):
            operands = (state, *near, *far, extras)
            if turn:
                pairs = [
                    (
                        (turn - 1) * GROUP + (lane ^ FLIPS[turn - 1]),
                        turn * GROUP + (lane ^ FLIPS[turn]),
                    )
                    for lane in range(GROUP)
                ]
                state = lax.ppermute(state, "layer", pairs)
                operands = (state, *near, *far, extras, starts)
            starts, state = call(
                functools.partial(chain_kernel, turn),
                (f32(GROUP, rows, channels), f32(rows, channels)),
                operands,
                aliases={6: 0} if turn else None,
            )

        arrived = lax.all_to_all(starts, "layer", 0, 0, axis_index_groups=teams)
        return call(
            finish_kernel,
            f32(2, IMAGES, SIDE, SIDE, channels),
            (arrived, packed, weights, biases),
            [columns, pltpu.VMEM((2, channels // LANES, cells, LANES), jnp.float32)],
            flops=conv,
        )

    return jax.shard_map(
        shards,
        mesh=mesh,
        in_specs=(P("batch", None, None, None), P("layer", None, None), P("layer", None)),
        out_specs=P("layer", "batch", None, None, None),
        check_vma=False,
    )
```

time: 745 us -> 105 us (0.14)
  the two profiles are of different devices: /device:TPU:16 before, /device:TPU:92 now
where the time goes in v2:
time: 105 us
  waiting for transfers between devices  61.6 us (59%)
  blocking collectives  21.5 us (20%)
  starting transfers between devices  11.4 us (11%)
  Pallas kernels  9 us (9%)
    ppermute x7, waiting for transfers between devices, shards(): state = lax.ppermute(state, 'layer', pairs)  34.4 us
    ppermute x1, waiting for transfers between devices, shards(): corner = lax.ppermute(beside_x, both, behind)  11.1 us
    all_to_all x1, blocking collectives, shards(): extras = lax.all_to_all(packed, 'layer', 0, 0, axis_index_groups=teams)  10.9 us
    all_to_all x1, blocking collectives, shards(): arrived = lax.all_to_all(starts, 'layer', 0, 0, axis_index_groups=teams)  10.6 us
    ppermute x1, waiting for transfers between devices, shards(): lax.ppermute(guessed, 'layer', [(i, i + 1) for i in range(blocks - 1)])  10.4 us
    pallas_call x19, Pallas kernels, call(): pl.pallas_call(kernel, out_shape=out_shape, in_specs=specs or [VMEM] * le...  9 us
    ppermute x7, starting transfers between devices, shards(): state = lax.ppermute(state, 'layer', pairs)  5.27 us
    ppermute x1, waiting for transfers between devices, shards(): far = lowered(2, (corner, lax.ppermute(corner, both, twin)), far)  2.57 us
  transfers between devices with their start and end apart: 15, of which 6 were waited for; matrix products, arithmetic and copies ran while one was open for 0% of the time, Pallas kernels for 3%

profile of v2, /device:TPU:92, one launch (start us, length us, event | category | flops | bytes accessed | tf_op | source)
XLA Modules:
  0.0 104.5 jit_solution(1836021179097304939)
XLA Ops:
  0.0 0.0 copy-start.1
  0.0 0.7 copy-done.1
  0.7 0.0 copy-start.3
  0.7 1.3 %shard_map.37.refs_0_ = f32[520,512]{1,0:T(8,128)S(1)} custom-call(bf16[2,4608,512]{2,1,0:T(8,128)(2,1)} %weights.7, f32[2,512]{1,0:T(2,128)S(1)} %copy-done.1), custom_call_target="tpu_custom_call" | custom-call | tf_op jit(solution)/shard_map/pallas_call | solution.py:27
  2.0 1.3 %collective-permute-start.4 = (f32[520,512]{1,0:T(8,128)S(1)}, f32[520,512]{1,0:T(8,128)S(1)}, u32[]{:S(2)}, u32[]{:S(2)}) collective-permute-start(f32[520,512]{1,0:T(8,128)S(1)} %shard_map.37.refs_0_), channel_id=1, source_target_pairs={{0,16},{1,17},{2,18},{3,19},{4,20},{5,21},{6,22},{7,23},{8,24},{9,... | collective-permute-start | bytes 3194888 | tf_op jit(solution)/shard_map/ppermute | solution.py:197
  3.3 1.9 %collective-permute-start.2 = (f32[520,512]{1,0:T(8,128)S(1)}, f32[520,512]{1,0:T(8,128)S(1)}, u32[]{:S(2)}, u32[]{:S(2)}) collective-permute-start(f32[520,512]{1,0:T(8,128)S(1)} %shard_map.37.refs_0_), channel_id=1, source_target_pairs={{0,8},{1,9},{2,10},{3,11},{4,15},{5,12},{6,13},{7,14},{8,1},{9,2},... | collective-permute-start | bytes 3194888 | tf_op jit(solution)/shard_map/ppermute | solution.py:198
  5.2 0.0 copy-done.3
  5.2 0.1 copy.18
  5.3 0.0 copy-done
  5.3 0.0 copy-done.2
  5.3 1.5 %shard_map.38 = f32[128,512]{1,0:T(8,128)S(1)} custom-call(f32[128,512]{1,0:T(8,128)S(1)} %bitcast.5, bf16[2,4608,512]{2,1,0:T(8,128)(2,1)S(1)} %copy-done, f32[2,512]{1,0:T(2,128)S(1)} %copy-done.2), custom_call_target="tpu_custom_call" | custom-call | tf_op jit(solution)/shard_map/pallas_call | solution.py:27
  6.8 1.9 %collective-permute-start = (f32[128,512]{1,0:T(8,128)S(1)}, f32[128,512]{1,0:T(8,128)S(1)}, u32[]{:S(2)}, u32[]{:S(2)}) collective-permute-start(f32[128,512]{1,0:T(8,128)S(1)} %shard_map.38), channel_id=1, source_target_pairs={{0,4},{4,8},{8,12},{12,16},{16,20},{20,24},{24,28},{28,32},{32,36}... | collective-permute-start | bytes 786440 | tf_op jit(solution)/shard_map/ppermute | solution.py:205
  8.8 10.4 %collective-permute-done.incoming = f32[128,512]{1,0:T(8,128)S(1)} collective-permute-done((f32[128,512]{1,0:T(8,128)S(1)}, f32[128,512]{1,0:T(8,128)S(1)}, u32[]{:S(2)}, u32[]{:S(2)}) %collective-permute-start) | collective-permute-done | bytes 262176 | tf_op jit(solution)/shard_map/ppermute | solution.py:205
  19.1 1.6 %shard_map.39.refs_1_.packed = f32[8,16,512]{2,1,0:T(8,128)S(1)} custom-call(f32[128,512]{1,0:T(8,128)S(1)} %collective-permute-done.incoming, f32[128,512]{1,0:T(8,128)S(1)} %bitcast.6, bf16[2,4608,512]{2,1,0:T(8,128)(2,1)S(1)} %copy-done, f32[2,512]{1,0:T(2,128)S(1)} %copy-done.2), custom_call_target="tpu_custom_call" | custom-call | tf_op jit(solution)/shard_map/pallas_call | solution.py:27
  20.7 10.9 %all_to_all.10.refs_1_.extras = f32[8,16,512]{2,1,0:T(8,128)S(1)} all-to-all(f32[8,16,512]{2,1,0:T(8,128)S(1)} %shard_map.39.refs_1_.packed), channel_id=1, replica_groups={{0,4,8,12,16,20,24,28},{32,36,40,44,48,52,56,60},{64,68,72,76,80,84,88,..., dimensions={0} | all-to-all | bytes 524288 | tf_op jit(solution)/shard_map/all_to_all | solution.py:214
  31.6 0.0 collective-permute-done.4.refs_0_
  31.6 0.0 collective-permute-done.2.refs_0_
  31.6 0.0 collective-permute-start.1
  31.7 0.5 collective-permute-start.3
  32.2 0.5 collective-permute-start.5
  32.6 0.0 collective-permute-start.7
  32.6 1.7 %collective-permute-done.1.refs_1_ = f32[520,512]{1,0:T(8,128)S(1)} collective-permute-done((f32[520,512]{1,0:T(8,128)S(1)}, f32[520,512]{1,0:T(8,128)S(1)}, u32[]{:S(2)}, u32[]{:S(2)}) %collective-permute-start.1) | collective-permute-done | bytes 1064992 | tf_op jit(solution)/shard_map/ppermute | solution.py:241
  34.3 1.5 %collective-permute-done.3.refs_3_ = f32[520,512]{1,0:T(8,128)S(1)} collective-permute-done((f32[520,512]{1,0:T(8,128)S(1)}, f32[520,512]{1,0:T(8,128)S(1)}, u32[]{:S(2)}, u32[]{:S(2)}) %collective-permute-start.3) | collective-permute-done | bytes 1064992 | tf_op jit(solution)/shard_map/ppermute | solution.py:242
  35.9 0.2 shard_map.42
  36.1 11.1 %collective-permute-done.5.refs_0_ = f32[520,512]{1,0:T(8,128)S(1)} collective-permute-done((f32[520,512]{1,0:T(8,128)S(1)}, f32[520,512]{1,0:T(8,128)S(1)}, u32[]{:S(2)}, u32[]{:S(2)}) %collective-permute-start.5) | collective-permute-done | bytes 1064992 | tf_op jit(solution)/shard_map/ppermute | solution.py:240
  47.1 0.0 collective-permute-start.6
  47.1 0.0 collective-permute-done.7.refs_1_
  47.1 0.1 shard_map.45
  47.3 2.6 %collective-permute-done.6.refs_1_ = f32[520,512]{1,0:T(8,128)S(1)} collective-permute-done((f32[520,512]{1,0:T(8,128)S(1)}, f32[520,512]{1,0:T(8,128)S(1)}, u32[]{:S(2)}, u32[]{:S(2)}) %collective-permute-start.6) | collective-permute-done | bytes 1064992 | tf_op jit(solution)/shard_map/ppermute | solution.py:247
  49.8 0.1 shard_map.46
  50.0 0.7 collective-permute-start.8
  50.6 0.0 collective-permute-done.8.state
  50.7 0.7 collective-permute-start.9
  51.4 0.0 collective-permute-done.9.state
  51.4 0.7 collective-permute-start.10
  52.1 0.0 collective-permute-done.10.state
  52.1 0.7 collective-permute-start.11
  52.8 0.0 collective-permute-done.11.state
  52.8 0.2 shard_map.51
  53.0 0.7 collective-permute-start.12
  53.7 0.0 collective-permute-done.12.state
  53.7 0.7 collective-permute-start.13
  54.4 0.0 collective-permute-done.13.state
  54.4 1.3 %collective-permute-start.14 = (f32[16,512]{1,0:T(8,128)S(1)}, f32[16,512]{1,0:T(8,128)S(1)}, u32[]{:S(2)}, u32[]{:S(2)}) collective-permute-start(f32[16,512]{1,0:T(8,128)S(1)} %get-tuple-element.44), channel_id=1, source_target_pairs={{208,228},{212,224},{216,236},{220,232},{192,244},{196,240},{200,2... | collective-permute-start | bytes 98312 | tf_op jit(solution)/shard_map/ppermute | solution.py:261
  55.7 34.4 %collective-permute-done.14.state = f32[16,512]{1,0:T(8,128)S(1)} collective-permute-done((f32[16,512]{1,0:T(8,128)S(1)}, f32[16,512]{1,0:T(8,128)S(1)}, u32[]{:S(2)}, u32[]{:S(2)}) %collective-permute-start.14) | collective-permute-done | bytes 32800 | tf_op jit(solution)/shard_map/ppermute | solution.py:261
  90.2 1.9 %shard_map.54 = (f32[8,16,512]{2,1,0:T(8,128)S(1)}, f32[16,512]{1,0:T(8,128)}) custom-call(f32[16,512]{1,0:T(8,128)S(1)} %collective-permute-done.14.state, bf16[4,512,512]{2,1,0:T(8,128)(2,1)S(1)} %get-tuple-element.26.near, f32[4,8,512]{2,1,0:T(8,128)S(1)} %get-tuple-element.27.refs_1_.near_bias, ...), custom_call_target="tpu_custom_call", output_to_operand_aliasing={{0}: (6, {})} | custom-call | tf_op jit(solution)/shard_map/pallas_call | solution.py:27
  92.1 10.6 %all_to_all.11.arrived = f32[8,16,512]{2,1,0:T(8,128)S(1)} all-to-all(f32[8,16,512]{2,1,0:T(8,128)S(1)} %get-tuple-element.46), channel_id=1, replica_groups={{0,4,8,12,16,20,24,28},{32,36,40,44,48,52,56,60},{64,68,72,76,80,84,88,..., dimensions={0} | all-to-all | bytes 524288 | tf_op jit(solution)/shard_map/all_to_all | solution.py:270
  102.7 1.8 %shard_map.55 = f32[2,8,4,4,512]{4,3,2,1,0:T(4,128)} custom-call(f32[8,16,512]{2,1,0:T(8,128)S(1)} %all_to_all.11.arrived, f32[8,16,512]{2,1,0:T(8,128)S(1)} %shard_map.39.refs_1_.packed, bf16[2,4608,512]{2,1,0:T(8,128)(2,1)S(1)} %copy-done, f32[2,512]{1,0:T(2,128)S(1)} %copy-done.2), custom_call_target="tpu_custom_call" | custom-call | tf_op jit(solution)/shard_map/pallas_call | solution.py:27
  (12 shorter events, 0.2 us)
Async XLA Ops:
  0.0 0.7 copy-start.1
  0.7 4.5 %copy-start.3 = (bf16[8,4,4,512]{3,2,1,0:T(4,128)(2,1)S(1)}, bf16[8,4,4,512]{3,2,1,0:T(4,128)(2,1)}, u32[]{:S(2)}) copy-start(bf16[8,4,4,512]{3,2,1,0:T(4,128)(2,1)} %param.3) | copy-start | bytes 393220
  0.7 4.6 %copy-start = (bf16[2,4608,512]{2,1,0:T(8,128)(2,1)S(1)}, bf16[2,4608,512]{2,1,0:T(8,128)(2,1)}, u32[]{:S(2)}) copy-start(bf16[2,4608,512]{2,1,0:T(8,128)(2,1)} %weights.7) | copy-start | bytes 28311556
  0.7 4.6 %copy-start.2 = (f32[2,512]{1,0:T(2,128)S(1)}, f32[2,512]{1,0:T(2,128)}, u32[]{:S(2)}) copy-start(f32[2,512]{1,0:T(2,128)} %biases.7) | copy-start | bytes 12292
  2.0 29.7 %collective-permute-start.4 = (f32[520,512]{1,0:T(8,128)S(1)}, f32[520,512]{1,0:T(8,128)S(1)}, u32[]{:S(2)}, u32[]{:S(2)}) collective-permute-start(f32[520,512]{1,0:T(8,128)S(1)} %shard_map.37.refs_0_), channel_id=1, source_target_pairs={{0,16},{1,17},{2,18},{3,19},{4,20},{5,21},{6,22},{7,23},{8,24},{9,... | collective-permute-start | bytes 3194888 | tf_op jit(solution)/shard_map/ppermute | solution.py:197
  3.3 28.4 %collective-permute-start.2 = (f32[520,512]{1,0:T(8,128)S(1)}, f32[520,512]{1,0:T(8,128)S(1)}, u32[]{:S(2)}, u32[]{:S(2)}) collective-permute-start(f32[520,512]{1,0:T(8,128)S(1)} %shard_map.37.refs_0_), channel_id=1, source_target_pairs={{0,8},{1,9},{2,10},{3,11},{4,15},{5,12},{6,13},{7,14},{8,1},{9,2},... | collective-permute-start | bytes 3194888 | tf_op jit(solution)/shard_map/ppermute | solution.py:198
  6.8 12.3 %collective-permute-start = (f32[128,512]{1,0:T(8,128)S(1)}, f32[128,512]{1,0:T(8,128)S(1)}, u32[]{:S(2)}, u32[]{:S(2)}) collective-permute-start(f32[128,512]{1,0:T(8,128)S(1)} %shard_map.38), channel_id=1, source_target_pairs={{0,4},{4,8},{8,12},{12,16},{16,20},{20,24},{24,28},{28,32},{32,36}... | collective-permute-start | bytes 786440 | tf_op jit(solution)/shard_map/ppermute | solution.py:205
  31.6 2.7 %collective-permute-start.1 = (f32[520,512]{1,0:T(8,128)S(1)}, f32[520,512]{1,0:T(8,128)S(1)}, u32[]{:S(2)}, u32[]{:S(2)}) collective-permute-start(f32[520,512]{1,0:T(8,128)S(1)} %shard_map.40.refs_0_), channel_id=1, source_target_pairs={{0,4},{1,5},{2,6},{3,7},{4,0},{5,1},{6,2},{7,3},{8,12},{9,13},{10,... | collective-permute-start | bytes 3194888 | tf_op jit(solution)/shard_map/ppermute | solution.py:241
  31.7 4.2 %collective-permute-start.3 = (f32[520,512]{1,0:T(8,128)S(1)}, f32[520,512]{1,0:T(8,128)S(1)}, u32[]{:S(2)}, u32[]{:S(2)}) collective-permute-start(f32[520,512]{1,0:T(8,128)S(1)} %shard_map.41.refs_2_), channel_id=1, source_target_pairs={{0,4},{1,5},{2,6},{3,7},{4,0},{5,1},{6,2},{7,3},{8,12},{9,13},{10,... | collective-permute-start | bytes 3194888 | tf_op jit(solution)/shard_map/ppermute | solution.py:242
  32.2 15.0 %collective-permute-start.5 = (f32[520,512]{1,0:T(8,128)S(1)}, f32[520,512]{1,0:T(8,128)S(1)}, u32[]{:S(2)}, u32[]{:S(2)}) collective-permute-start(f32[520,512]{1,0:T(8,128)S(1)} %shard_map.43.refs_0_), channel_id=1, source_target_pairs={{0,8},{1,9},{2,10},{3,11},{4,15},{5,12},{6,13},{7,14},{8,1},{9,2},... | collective-permute-start | bytes 3194888 | tf_op jit(solution)/shard_map/ppermute | solution.py:240
  32.6 14.5 %collective-permute-start.7 = (f32[520,512]{1,0:T(8,128)S(1)}, f32[520,512]{1,0:T(8,128)S(1)}, u32[]{:S(2)}, u32[]{:S(2)}) collective-permute-start(f32[520,512]{1,0:T(8,128)S(1)} %shard_map.43.refs_0_), channel_id=1, source_target_pairs={{0,4},{1,5},{2,6},{3,7},{4,0},{5,1},{6,2},{7,3},{8,12},{9,13},{10,... | collective-permute-start | bytes 3194888 | tf_op jit(solution)/shard_map/ppermute | solution.py:243
  47.1 2.7 %collective-permute-start.6 = (f32[520,512]{1,0:T(8,128)S(1)}, f32[520,512]{1,0:T(8,128)S(1)}, u32[]{:S(2)}, u32[]{:S(2)}) collective-permute-start(f32[520,512]{1,0:T(8,128)S(1)} %shard_map.44.refs_0_), channel_id=1, source_target_pairs={{0,4},{1,5},{2,6},{3,7},{4,0},{5,1},{6,2},{7,3},{8,12},{9,13},{10,... | collective-permute-start | bytes 3194888 | tf_op jit(solution)/shard_map/ppermute | solution.py:247
  50.0 0.7 collective-permute-start.8
  50.7 0.7 collective-permute-start.9
  51.4 0.7 collective-permute-start.10
  52.1 0.7 collective-permute-start.11
  53.0 0.7 collective-permute-start.12
  53.7 0.7 collective-permute-start.13
  54.4 35.7 %collective-permute-start.14 = (f32[16,512]{1,0:T(8,128)S(1)}, f32[16,512]{1,0:T(8,128)S(1)}, u32[]{:S(2)}, u32[]{:S(2)}) collective-permute-start(f32[16,512]{1,0:T(8,128)S(1)} %get-tuple-element.44), channel_id=1, source_target_pairs={{208,228},{212,224},{216,236},{220,232},{192,244},{196,240},{200,2... | collective-permute-start | bytes 98312 | tf_op jit(solution)/shard_map/ppermute | solution.py:261

commit v3 on v2

--- a/solution.py
+++ b/solution.py
@@ -73,11 +73,16 @@
     return lax.bitwise_or(4 * other_x, lax.bitwise_and(group, 1))
 
 
-def centre_kernel(weights, biases, whole, landing, sem):
+def centre_kernel(weights, biases, whole, landing, offsets, sems):
     channels = whole.shape[1]
-    copy = pltpu.make_async_copy(weights.at[0, pl.ds(4 * channels, channels)], landing, sem)
+    copy = pltpu.make_async_copy(
+        weights.at[0, pl.ds(4 * channels, channels)], landing, sems.at[0]
+    )
+    offset_copy = pltpu.make_async_copy(biases, offsets, sems.at[1])
     copy.start()
-    whole[channels:] = jnp.broadcast_to(biases[0:1], (PAD, channels))
+    offset_copy.start()
+    offset_copy.wait()
+    whole[channels:] = jnp.broadcast_to(offsets[0:1], (PAD, channels))
     copy.wait()
     whole[:channels] = landing[...].astype(jnp.float32)
 
@@ -114,9 +119,9 @@
         offsets[begin + n] = refs[n][channels:]
 
 
-def chain_kernel(turn, state, near, near_bias, far, far_bias, extras, *refs):
-    starts, end = refs[-2:]
-    rows = end.shape[0]
+def chain_kernel(turn, last, state, near, near_bias, far, far_bias, extras, *refs):
+    starts, end = (refs[-1], None) if last else refs[-2:]
+    rows = starts.shape[1]
     position = lax.axis_index("layer")
     mine = lax.rem(position, GROUP)
 
@@ -130,7 +135,8 @@
             centres, offsets = order[at // 4]
             slot = lax.bitwise_and(lax.bitwise_xor(mine, at), 3)
             current = coarse(current, centres[slot], offsets[slot, 0:1]) + extras[at]
-        end[...] = current
+        if not last:
+            end[...] = current
 
     first, second = (near, near_bias), (far, far_bias)
     here = lax.div(position, GROUP) == turn
@@ -190,9 +196,13 @@
         own = call(
             centre_kernel,
             pltpu.VMEM((channels + PAD, channels), jnp.float32),
-            (pltpu.with_memory_space_constraint(weights, pltpu.HBM), biases),
-            scratch=[pltpu.VMEM((channels, channels), jnp.bfloat16), pltpu.SemaphoreType.DMA],
-            specs=[HBM, VMEM],
+            [pltpu.with_memory_space_constraint(each, pltpu.HBM) for each in (weights, biases)],
+            scratch=[
+                pltpu.VMEM((channels, channels), jnp.bfloat16),
+                pltpu.VMEM(biases.shape, jnp.float32),
+                pltpu.SemaphoreType.DMA((2,)),
+            ],
+            specs=[HBM, HBM],
         )
         beside_x = lax.ppermute(own, both, beside)
         behind_z = lax.ppermute(own, both, behind)
@@ -246,10 +256,10 @@
         corner = hold(corner, near[1])
         far = lowered(2, (corner, lax.ppermute(corner, both, twin)), far)
 
-        state = initial
+        state = [initial]
         starts = None
         for turn in range(groups):
-            operands = (state, *near, *far, extras)
+            operands = (*state, *near, *far, extras)
             if turn:
                 pairs = [
                     (
@@ -258,11 +268,12 @@
                     )
                     for lane in range(GROUP)
                 ]
-                state = lax.ppermute(state, "layer", pairs)
-                operands = (state, *near, *far, extras, starts)
-            starts, state = call(
-                functools.partial(chain_kernel, turn),
-                (f32(GROUP, rows, channels), f32(rows, channels)),
+                state = [lax.ppermute(*state, "layer", pairs)]
+                operands = (*state, *near, *far, extras, starts)
+            last = turn == groups - 1
+            starts, *state = call(
+                functools.partial(chain_kernel, turn, last),
+                [f32(GROUP, rows, channels)] + [f32(rows, channels)] * (not last),
                 operands,
                 aliases={6: 0} if turn else None,
             )

time: 105 us -> 103 us (0.981)
  no operation moved by 1% of the time
where the time goes in v3:
time: 103 us
  waiting for transfers between devices  61.6 us (60%)
  blocking collectives  21.5 us (21%)
  starting transfers between devices  11.4 us (11%)
  Pallas kernels  8.24 us (8%)
    ppermute x7, waiting for transfers between devices, shards(): state = [lax.ppermute(*state, 'layer', pairs)]  34.4 us
    ppermute x1, waiting for transfers between devices, shards(): corner = lax.ppermute(beside_x, both, behind)  11.1 us
    all_to_all x1, blocking collectives, shards(): extras = lax.all_to_all(packed, 'layer', 0, 0, axis_index_groups=teams)  10.9 us
    all_to_all x1, blocking collectives, shards(): arrived = lax.all_to_all(starts, 'layer', 0, 0, axis_index_groups=teams)  10.6 us
    ppermute x1, waiting for transfers between devices, shards(): lax.ppermute(guessed, 'layer', [(i, i + 1) for i in range(blocks - 1)])  10.4 us
    pallas_call x19, Pallas kernels, call(): pl.pallas_call(kernel, out_shape=out_shape, in_specs=specs or [VMEM] * le...  8.24 us
    ppermute x7, starting transfers between devices, shards(): state = [lax.ppermute(*state, 'layer', pairs)]  5.27 us
    ppermute x1, waiting for transfers between devices, shards(): far = lowered(2, (corner, lax.ppermute(corner, both, twin)), far)  2.57 us
  transfers between devices with their start and end apart: 15, of which 6 were waited for; matrix products, arithmetic and copies ran while one was open for 0% of the time, Pallas kernels for 3%

profile of v3, /device:TPU:92, one launch (start us, length us, event | category | flops | bytes accessed | tf_op | source)
XLA Modules:
  0.0 103.1 jit_solution(10094476847319754667)
XLA Ops:
  0.0 0.0 copy-start.1
  0.0 0.0 copy-start.2
  0.0 0.0 copy-start
  0.0 1.3 %shard_map.37.refs_0_ = f32[520,512]{1,0:T(8,128)S(1)} custom-call(bf16[2,4608,512]{2,1,0:T(8,128)(2,1)} %weights.7, f32[2,512]{1,0:T(2,128)} %biases.7), custom_call_target="tpu_custom_call" | custom-call | tf_op jit(solution)/shard_map/pallas_call | solution.py:27
  1.3 1.3 %collective-permute-start.4 = (f32[520,512]{1,0:T(8,128)S(1)}, f32[520,512]{1,0:T(8,128)S(1)}, u32[]{:S(2)}, u32[]{:S(2)}) collective-permute-start(f32[520,512]{1,0:T(8,128)S(1)} %shard_map.37.refs_0_), channel_id=1, source_target_pairs={{0,16},{1,17},{2,18},{3,19},{4,20},{5,21},{6,22},{7,23},{8,24},{9,... | collective-permute-start | bytes 3194888 | tf_op jit(solution)/shard_map/ppermute | solution.py:207
  2.6 1.9 %collective-permute-start.2 = (f32[520,512]{1,0:T(8,128)S(1)}, f32[520,512]{1,0:T(8,128)S(1)}, u32[]{:S(2)}, u32[]{:S(2)}) collective-permute-start(f32[520,512]{1,0:T(8,128)S(1)} %shard_map.37.refs_0_), channel_id=1, source_target_pairs={{0,8},{1,9},{2,10},{3,11},{4,15},{5,12},{6,13},{7,14},{8,1},{9,2},... | collective-permute-start | bytes 3194888 | tf_op jit(solution)/shard_map/ppermute | solution.py:208
  4.5 0.0 copy-done.2
  4.5 0.1 copy.18
  4.6 0.0 copy-done.1
  4.6 0.0 copy-done
  4.6 1.5 %shard_map.38 = f32[128,512]{1,0:T(8,128)S(1)} custom-call(f32[128,512]{1,0:T(8,128)S(1)} %bitcast.5, bf16[2,4608,512]{2,1,0:T(8,128)(2,1)S(1)} %copy-done, f32[2,512]{1,0:T(2,128)S(1)} %copy-done.1), custom_call_target="tpu_custom_call" | custom-call | tf_op jit(solution)/shard_map/pallas_call | solution.py:27
  6.1 1.9 %collective-permute-start = (f32[128,512]{1,0:T(8,128)S(1)}, f32[128,512]{1,0:T(8,128)S(1)}, u32[]{:S(2)}, u32[]{:S(2)}) collective-permute-start(f32[128,512]{1,0:T(8,128)S(1)} %shard_map.38), channel_id=1, source_target_pairs={{0,4},{4,8},{8,12},{12,16},{16,20},{20,24},{24,28},{28,32},{32,36}... | collective-permute-start | bytes 786440 | tf_op jit(solution)/shard_map/ppermute | solution.py:215
  8.1 10.4 %collective-permute-done.incoming = f32[128,512]{1,0:T(8,128)S(1)} collective-permute-done((f32[128,512]{1,0:T(8,128)S(1)}, f32[128,512]{1,0:T(8,128)S(1)}, u32[]{:S(2)}, u32[]{:S(2)}) %collective-permute-start) | collective-permute-done | bytes 262176 | tf_op jit(solution)/shard_map/ppermute | solution.py:215
  18.4 1.6 %shard_map.39.refs_1_.packed = f32[8,16,512]{2,1,0:T(8,128)S(1)} custom-call(f32[128,512]{1,0:T(8,128)S(1)} %collective-permute-done.incoming, f32[128,512]{1,0:T(8,128)S(1)} %bitcast.6, bf16[2,4608,512]{2,1,0:T(8,128)(2,1)S(1)} %copy-done, f32[2,512]{1,0:T(2,128)S(1)} %copy-done.1), custom_call_target="tpu_custom_call" | custom-call | tf_op jit(solution)/shard_map/pallas_call | solution.py:27
  20.1 10.9 %all_to_all.10.refs_1_.extras = f32[8,16,512]{2,1,0:T(8,128)S(1)} all-to-all(f32[8,16,512]{2,1,0:T(8,128)S(1)} %shard_map.39.refs_1_.packed), channel_id=1, replica_groups={{0,4,8,12,16,20,24,28},{32,36,40,44,48,52,56,60},{64,68,72,76,80,84,88,..., dimensions={0} | all-to-all | bytes 524288 | tf_op jit(solution)/shard_map/all_to_all | solution.py:224
  31.0 0.0 collective-permute-done.4.refs_0_
  31.0 0.0 collective-permute-done.2.refs_0_
  31.0 0.0 collective-permute-start.1
  31.0 0.5 collective-permute-start.3
  31.5 0.5 collective-permute-start.5
  32.0 0.0 collective-permute-start.7
  32.0 1.7 %collective-permute-done.1.refs_1_ = f32[520,512]{1,0:T(8,128)S(1)} collective-permute-done((f32[520,512]{1,0:T(8,128)S(1)}, f32[520,512]{1,0:T(8,128)S(1)}, u32[]{:S(2)}, u32[]{:S(2)}) %collective-permute-start.1) | collective-permute-done | bytes 1064992 | tf_op jit(solution)/shard_map/ppermute | solution.py:251
  33.7 1.5 %collective-permute-done.3.refs_3_ = f32[520,512]{1,0:T(8,128)S(1)} collective-permute-done((f32[520,512]{1,0:T(8,128)S(1)}, f32[520,512]{1,0:T(8,128)S(1)}, u32[]{:S(2)}, u32[]{:S(2)}) %collective-permute-start.3) | collective-permute-done | bytes 1064992 | tf_op jit(solution)/shard_map/ppermute | solution.py:252
  35.2 0.2 shard_map.42
  35.4 11.1 %collective-permute-done.5.refs_0_ = f32[520,512]{1,0:T(8,128)S(1)} collective-permute-done((f32[520,512]{1,0:T(8,128)S(1)}, f32[520,512]{1,0:T(8,128)S(1)}, u32[]{:S(2)}, u32[]{:S(2)}) %collective-permute-start.5) | collective-permute-done | bytes 1064992 | tf_op jit(solution)/shard_map/ppermute | solution.py:250
  46.5 0.0 collective-permute-start.6
  46.5 0.0 collective-permute-done.7.refs_1_
  46.5 0.1 shard_map.45
  46.6 2.6 %collective-permute-done.6.refs_1_ = f32[520,512]{1,0:T(8,128)S(1)} collective-permute-done((f32[520,512]{1,0:T(8,128)S(1)}, f32[520,512]{1,0:T(8,128)S(1)}, u32[]{:S(2)}, u32[]{:S(2)}) %collective-permute-start.6) | collective-permute-done | bytes 1064992 | tf_op jit(solution)/shard_map/ppermute | solution.py:257
  49.1 0.1 shard_map.46
  49.3 0.7 collective-permute-start.8
  50.0 0.0 collective-permute-done.8.state
  50.0 0.7 collective-permute-start.9
  50.7 0.0 collective-permute-done.9.state
  50.7 0.7 collective-permute-start.10
  51.4 0.0 collective-permute-done.10.state
  51.4 0.7 collective-permute-start.11
  52.1 0.0 collective-permute-done.11.state
  52.1 0.2 shard_map.51
  52.3 0.7 collective-permute-start.12
  53.0 0.0 collective-permute-done.12.state
  53.1 0.7 collective-permute-start.13
  53.7 0.0 collective-permute-done.13.state
  53.8 1.3 %collective-permute-start.14 = (f32[16,512]{1,0:T(8,128)S(1)}, f32[16,512]{1,0:T(8,128)S(1)}, u32[]{:S(2)}, u32[]{:S(2)}) collective-permute-start(f32[16,512]{1,0:T(8,128)S(1)} %get-tuple-element.43), channel_id=1, source_target_pairs={{208,228},{212,224},{216,236},{220,232},{192,244},{196,240},{200,2... | collective-permute-start | bytes 98312 | tf_op jit(solution)/shard_map/ppermute | solution.py:271
  55.1 34.4 %collective-permute-done.14.state = f32[16,512]{1,0:T(8,128)S(1)} collective-permute-done((f32[16,512]{1,0:T(8,128)S(1)}, f32[16,512]{1,0:T(8,128)S(1)}, u32[]{:S(2)}, u32[]{:S(2)}) %collective-permute-start.14) | collective-permute-done | bytes 32800 | tf_op jit(solution)/shard_map/ppermute | solution.py:271
  89.5 1.2 %shard_map.54 = f32[8,16,512]{2,1,0:T(8,128)S(1)} custom-call(f32[16,512]{1,0:T(8,128)S(1)} %collective-permute-done.14.state, bf16[4,512,512]{2,1,0:T(8,128)(2,1)S(1)} %get-tuple-element.25.near, f32[4,8,512]{2,1,0:T(8,128)S(1)} %get-tuple-element.26.refs_1_.near_bias, ...), custom_call_target="tpu_custom_call", output_to_operand_aliasing={{}: (6, {})} | custom-call | tf_op jit(solution)/shard_map/pallas_call | solution.py:27
  90.7 10.6 %all_to_all.11.arrived = f32[8,16,512]{2,1,0:T(8,128)S(1)} all-to-all(f32[8,16,512]{2,1,0:T(8,128)S(1)} %shard_map.54), channel_id=1, replica_groups={{0,4,8,12,16,20,24,28},{32,36,40,44,48,52,56,60},{64,68,72,76,80,84,88,..., dimensions={0} | all-to-all | bytes 524288 | tf_op jit(solution)/shard_map/all_to_all | solution.py:281
  101.2 1.9 %shard_map.55 = f32[2,8,4,4,512]{4,3,2,1,0:T(4,128)} custom-call(f32[8,16,512]{2,1,0:T(8,128)S(1)} %all_to_all.11.arrived, f32[8,16,512]{2,1,0:T(8,128)S(1)} %shard_map.39.refs_1_.packed, bf16[2,4608,512]{2,1,0:T(8,128)(2,1)S(1)} %copy-done, f32[2,512]{1,0:T(2,128)S(1)} %copy-done.1), custom_call_target="tpu_custom_call" | custom-call | tf_op jit(solution)/shard_map/pallas_call | solution.py:27
  (10 shorter events, 0.2 us)
Async XLA Ops:
  0.0 4.6 %copy-start.1 = (f32[2,512]{1,0:T(2,128)S(1)}, f32[2,512]{1,0:T(2,128)}, u32[]{:S(2)}) copy-start(f32[2,512]{1,0:T(2,128)} %biases.7) | copy-start | bytes 12292
  0.0 4.5 %copy-start.2 = (bf16[8,4,4,512]{3,2,1,0:T(4,128)(2,1)S(1)}, bf16[8,4,4,512]{3,2,1,0:T(4,128)(2,1)}, u32[]{:S(2)}) copy-start(bf16[8,4,4,512]{3,2,1,0:T(4,128)(2,1)} %param.3) | copy-start | bytes 393220
  0.0 4.6 %copy-start = (bf16[2,4608,512]{2,1,0:T(8,128)(2,1)S(1)}, bf16[2,4608,512]{2,1,0:T(8,128)(2,1)}, u32[]{:S(2)}) copy-start(bf16[2,4608,512]{2,1,0:T(8,128)(2,1)} %weights.7) | copy-start | bytes 28311556
  1.3 29.7 %collective-permute-start.4 = (f32[520,512]{1,0:T(8,128)S(1)}, f32[520,512]{1,0:T(8,128)S(1)}, u32[]{:S(2)}, u32[]{:S(2)}) collective-permute-start(f32[520,512]{1,0:T(8,128)S(1)} %shard_map.37.refs_0_), channel_id=1, source_target_pairs={{0,16},{1,17},{2,18},{3,19},{4,20},{5,21},{6,22},{7,23},{8,24},{9,... | collective-permute-start | bytes 3194888 | tf_op jit(solution)/shard_map/ppermute | solution.py:207
  2.6 28.4 %collective-permute-start.2 = (f32[520,512]{1,0:T(8,128)S(1)}, f32[520,512]{1,0:T(8,128)S(1)}, u32[]{:S(2)}, u32[]{:S(2)}) collective-permute-start(f32[520,512]{1,0:T(8,128)S(1)} %shard_map.37.refs_0_), channel_id=1, source_target_pairs={{0,8},{1,9},{2,10},{3,11},{4,15},{5,12},{6,13},{7,14},{8,1},{9,2},... | collective-permute-start | bytes 3194888 | tf_op jit(solution)/shard_map/ppermute | solution.py:208
  6.1 12.3 %collective-permute-start = (f32[128,512]{1,0:T(8,128)S(1)}, f32[128,512]{1,0:T(8,128)S(1)}, u32[]{:S(2)}, u32[]{:S(2)}) collective-permute-start(f32[128,512]{1,0:T(8,128)S(1)} %shard_map.38), channel_id=1, source_target_pairs={{0,4},{4,8},{8,12},{12,16},{16,20},{20,24},{24,28},{28,32},{32,36}... | collective-permute-start | bytes 786440 | tf_op jit(solution)/shard_map/ppermute | solution.py:215
  31.0 2.7 %collective-permute-start.1 = (f32[520,512]{1,0:T(8,128)S(1)}, f32[520,512]{1,0:T(8,128)S(1)}, u32[]{:S(2)}, u32[]{:S(2)}) collective-permute-start(f32[520,512]{1,0:T(8,128)S(1)} %shard_map.40.refs_0_), channel_id=1, source_target_pairs={{0,4},{1,5},{2,6},{3,7},{4,0},{5,1},{6,2},{7,3},{8,12},{9,13},{10,... | collective-permute-start | bytes 3194888 | tf_op jit(solution)/shard_map/ppermute | solution.py:251
  31.0 4.2 %collective-permute-start.3 = (f32[520,512]{1,0:T(8,128)S(1)}, f32[520,512]{1,0:T(8,128)S(1)}, u32[]{:S(2)}, u32[]{:S(2)}) collective-permute-start(f32[520,512]{1,0:T(8,128)S(1)} %shard_map.41.refs_2_), channel_id=1, source_target_pairs={{0,4},{1,5},{2,6},{3,7},{4,0},{5,1},{6,2},{7,3},{8,12},{9,13},{10,... | collective-permute-start | bytes 3194888 | tf_op jit(solution)/shard_map/ppermute | solution.py:252
  31.5 15.0 %collective-permute-start.5 = (f32[520,512]{1,0:T(8,128)S(1)}, f32[520,512]{1,0:T(8,128)S(1)}, u32[]{:S(2)}, u32[]{:S(2)}) collective-permute-start(f32[520,512]{1,0:T(8,128)S(1)} %shard_map.43.refs_0_), channel_id=1, source_target_pairs={{0,8},{1,9},{2,10},{3,11},{4,15},{5,12},{6,13},{7,14},{8,1},{9,2},... | collective-permute-start | bytes 3194888 | tf_op jit(solution)/shard_map/ppermute | solution.py:250
  32.0 14.5 %collective-permute-start.7 = (f32[520,512]{1,0:T(8,128)S(1)}, f32[520,512]{1,0:T(8,128)S(1)}, u32[]{:S(2)}, u32[]{:S(2)}) collective-permute-start(f32[520,512]{1,0:T(8,128)S(1)} %shard_map.43.refs_0_), channel_id=1, source_target_pairs={{0,4},{1,5},{2,6},{3,7},{4,0},{5,1},{6,2},{7,3},{8,12},{9,13},{10,... | collective-permute-start | bytes 3194888 | tf_op jit(solution)/shard_map/ppermute | solution.py:253
  46.5 2.7 %collective-permute-start.6 = (f32[520,512]{1,0:T(8,128)S(1)}, f32[520,512]{1,0:T(8,128)S(1)}, u32[]{:S(2)}, u32[]{:S(2)}) collective-permute-start(f32[520,512]{1,0:T(8,128)S(1)} %shard_map.44.refs_0_), channel_id=1, source_target_pairs={{0,4},{1,5},{2,6},{3,7},{4,0},{5,1},{6,2},{7,3},{8,12},{9,13},{10,... | collective-permute-start | bytes 3194888 | tf_op jit(solution)/shard_map/ppermute | solution.py:257
  49.3 0.7 collective-permute-start.8
  50.0 0.7 collective-permute-start.9
  50.7 0.7 collective-permute-start.10
  51.4 0.7 collective-permute-start.11
  52.3 0.7 collective-permute-start.12
  53.1 0.7 collective-permute-start.13
  53.8 35.7 %collective-permute-start.14 = (f32[16,512]{1,0:T(8,128)S(1)}, f32[16,512]{1,0:T(8,128)S(1)}, u32[]{:S(2)}, u32[]{:S(2)}) collective-permute-start(f32[16,512]{1,0:T(8,128)S(1)} %get-tuple-element.43), channel_id=1, source_target_pairs={{208,228},{212,224},{216,236},{220,232},{192,244},{196,240},{200,2... | collective-permute-start | bytes 98312 | tf_op jit(solution)/shard_map/ppermute | solution.py:271

commit v4 on v3

--- a/solution.py
+++ b/solution.py
@@ -10,6 +10,7 @@
 step_size = 0.25
 GROUP = 8
 PAD = 8
+CUT = 344
 FLIPS = (0, 5, 0, 5, 4, 1, 4, 1)
 SIDE = 4
 IMAGES = 8
@@ -111,12 +112,23 @@
     del refs
 
 
-def lower_kernel(begin, count, *refs):
+def part_kernel(begin, whole, after, part):
+    del after
+    part[...] = whole[begin : begin + part.shape[0]]
+
+
+def lower_kernel(begin, counts, *refs):
     centres, offsets = refs[-2:]
     channels = centres.shape[1]
-    for n in range(count):
-        centres[begin + n] = refs[n][:channels].astype(jnp.bfloat16)
-        offsets[begin + n] = refs[n][channels:]
+    at = 0
+    for n, count in enumerate(counts):
+        spot = 0
+        for ref in refs[at : at + count]:
+            rows = min(ref.shape[0], channels - spot)
+            centres[begin + n, spot : spot + rows] = ref[:rows].astype(jnp.bfloat16)
+            spot += rows
+        offsets[begin + n] = ref[rows:]
+        at += count
 
 
 def chain_kernel(turn, last, state, near, near_bias, far, far_bias, extras, *refs):
@@ -233,9 +245,10 @@
                 aliases={0: 0},
             )
 
-        def lowered(begin, pieces, held=()):
+        def lowered(begin, slots, held=()):
+            pieces = [each for slot in slots for each in slot]
             return call(
-                functools.partial(lower_kernel, begin, len(pieces)),
+                functools.partial(lower_kernel, begin, [len(slot) for slot in slots]),
                 (
                     pltpu.VMEM((4, channels, channels), jnp.bfloat16),
                     pltpu.VMEM((4, PAD, channels), jnp.float32),
@@ -244,17 +257,29 @@
                 aliases={len(pieces) + n: n for n in range(len(held))},
             )
 
+        def part(whole, begin, end, after):
+            return call(
+                functools.partial(part_kernel, begin),
+                pltpu.VMEM((end - begin, channels), jnp.float32),
+                (whole, after),
+                specs=[VMEM, ANY],
+            )
+
         behind_z = hold(behind_z, packed)
         beside_x = hold(beside_x, packed)
         held = hold(own, extras)
-        corner = lax.ppermute(beside_x, both, behind)
+        corner = [
+            lax.ppermute(part(beside_x, 0, CUT, extras), both, behind),
+            lax.ppermute(part(behind_z, CUT, channels + PAD, extras), both, beside),
+        ]
         own_twin = lax.ppermute(held, both, twin)
         behind_twin = lax.ppermute(behind_z, both, twin)
         beside_twin = lax.ppermute(beside_x, both, twin)
-        near = lowered(0, (held, own_twin, behind_z, behind_twin))
-        far = lowered(0, (beside_x, beside_twin))
-        corner = hold(corner, near[1])
-        far = lowered(2, (corner, lax.ppermute(corner, both, twin)), far)
+        near = lowered(0, ([held], [own_twin], [behind_z], [behind_twin]))
+        far = lowered(0, ([beside_x], [beside_twin]))
+        corner = [hold(each, near[1]) for each in corner]
+        corner_twin = [lax.ppermute(each, both, twin) for each in corner]
+        far = lowered(2, (corner, corner_twin), far)
 
         state = [initial]
         starts = None

time: 103 us -> 101 us (0.981)
  waiting for transfers between devices: 61.6 us -> 55.4 us
  starting transfers between devices: 11.4 us -> 13.8 us
  blocking collectives: 21.5 us -> 22.8 us
    ppermute x2 -> x4, waiting for transfers between devices: 13.6 us -> 9.9 us  [the longest x1 7.33 us: shards(): lax.ppermute(part(beside_x, 0, CUT, extras), both, behind)]
    ppermute x2 -> x4, starting transfers between devices: 0.47 us -> 2.94 us  [the longest x1 2.38 us: shards(): lax.ppermute(part(behind_z, CUT, channels + PAD, extras), both, beside)]
    ppermute x1, waiting for transfers between devices: 1.7 us -> 0.01 us  [shards(): own_twin = lax.ppermute(held, both, twin)]
    all_to_all x1, blocking collectives: 10.6 us -> 11.9 us  [shards(): arrived = lax.all_to_all(starts, 'layer', 0, 0, axis_index_groups=teams)]
    pallas_call x19 -> x22, Pallas kernels: 8.24 us -> 8.31 us  [call(): pl.pallas_call(kernel, out_shape=out_shape, in_specs=specs or [VMEM] * le...]
  transfers between devices with their start and end apart: 15 -> 17, of which waited for: 6 -> 6; matrix products, arithmetic and copies ran while one was open for 0% -> 0% of each run, Pallas kernels for 3% -> 4%
where the time goes in v4:
time: 101 us
  waiting for transfers between devices  55.4 us (55%)
  blocking collectives  22.8 us (23%)
  starting transfers between devices  13.8 us (14%)
  Pallas kernels  8.31 us (8%)
    ppermute x7, waiting for transfers between devices, shards(): state = [lax.ppermute(*state, 'layer', pairs)]  34.4 us
    all_to_all x1, blocking collectives, shards(): arrived = lax.all_to_all(starts, 'layer', 0, 0, axis_index_groups=teams)  11.9 us
    all_to_all x1, blocking collectives, shards(): extras = lax.all_to_all(packed, 'layer', 0, 0, axis_index_groups=teams)  10.9 us
    ppermute x1, waiting for transfers between devices, shards(): lax.ppermute(guessed, 'layer', [(i, i + 1) for i in range(blocks - 1)])  10.4 us
    pallas_call x22, Pallas kernels, call(): pl.pallas_call(kernel, out_shape=out_shape, in_specs=specs or [VMEM] * le...  8.31 us
    ppermute x1, waiting for transfers between devices, shards(): lax.ppermute(part(beside_x, 0, CUT, extras), both, behind)  7.33 us
    ppermute x7, starting transfers between devices, shards(): state = [lax.ppermute(*state, 'layer', pairs)]  5.27 us
    ppermute x1, starting transfers between devices, shards(): lax.ppermute(part(behind_z, CUT, channels + PAD, extras), both, beside)  2.38 us
  transfers between devices with their start and end apart: 17, of which 6 were waited for; matrix products, arithmetic and copies ran while one was open for 0% of the time, Pallas kernels for 4%

profile of v4, /device:TPU:92, one launch (start us, length us, event | category | flops | bytes accessed | tf_op | source)
XLA Modules:
  0.0 100.7 jit_solution(5758441929764550882)
XLA Ops:
  0.0 1.3 %shard_map.37.refs_0_ = f32[520,512]{1,0:T(8,128)S(1)} custom-call(bf16[2,4608,512]{2,1,0:T(8,128)(2,1)} %weights.7, f32[2,512]{1,0:T(2,128)} %biases.7), custom_call_target="tpu_custom_call" | custom-call | tf_op jit(solution)/shard_map/pallas_call | solution.py:28
  1.3 1.3 %collective-permute-start.4 = (f32[520,512]{1,0:T(8,128)S(1)}, f32[520,512]{1,0:T(8,128)S(1)}, u32[]{:S(2)}, u32[]{:S(2)}) collective-permute-start(f32[520,512]{1,0:T(8,128)S(1)} %shard_map.37.refs_0_), channel_id=1, source_target_pairs={{0,16},{1,17},{2,18},{3,19},{4,20},{5,21},{6,22},{7,23},{8,24},{9,... | collective-permute-start | bytes 3194888 | tf_op jit(solution)/shard_map/ppermute | solution.py:219
  2.6 1.9 %collective-permute-start.2 = (f32[520,512]{1,0:T(8,128)S(1)}, f32[520,512]{1,0:T(8,128)S(1)}, u32[]{:S(2)}, u32[]{:S(2)}) collective-permute-start(f32[520,512]{1,0:T(8,128)S(1)} %shard_map.37.refs_0_), channel_id=1, source_target_pairs={{0,8},{1,9},{2,10},{3,11},{4,15},{5,12},{6,13},{7,14},{8,1},{9,2},... | collective-permute-start | bytes 3194888 | tf_op jit(solution)/shard_map/ppermute | solution.py:220
  4.5 0.0 copy-done.2
  4.5 0.1 copy.19
  4.6 0.0 copy-done.1
  4.6 1.5 %shard_map.38 = f32[128,512]{1,0:T(8,128)S(1)} custom-call(f32[128,512]{1,0:T(8,128)S(1)} %bitcast.5, bf16[2,4608,512]{2,1,0:T(8,128)(2,1)S(1)} %copy-done, f32[2,512]{1,0:T(2,128)S(1)} %copy-done.1), custom_call_target="tpu_custom_call" | custom-call | tf_op jit(solution)/shard_map/pallas_call | solution.py:28
  6.1 1.9 %collective-permute-start = (f32[128,512]{1,0:T(8,128)S(1)}, f32[128,512]{1,0:T(8,128)S(1)}, u32[]{:S(2)}, u32[]{:S(2)}) collective-permute-start(f32[128,512]{1,0:T(8,128)S(1)} %shard_map.38), channel_id=1, source_target_pairs={{0,4},{4,8},{8,12},{12,16},{16,20},{20,24},{24,28},{28,32},{32,36}... | collective-permute-start | bytes 786440 | tf_op jit(solution)/shard_map/ppermute | solution.py:227
  8.1 10.4 %collective-permute-done.incoming = f32[128,512]{1,0:T(8,128)S(1)} collective-permute-done((f32[128,512]{1,0:T(8,128)S(1)}, f32[128,512]{1,0:T(8,128)S(1)}, u32[]{:S(2)}, u32[]{:S(2)}) %collective-permute-start) | collective-permute-done | bytes 262176 | tf_op jit(solution)/shard_map/ppermute | solution.py:227
  18.4 1.6 %shard_map.39.refs_1_.packed = f32[8,16,512]{2,1,0:T(8,128)S(1)} custom-call(f32[128,512]{1,0:T(8,128)S(1)} %collective-permute-done.incoming, f32[128,512]{1,0:T(8,128)S(1)} %bitcast.6, bf16[2,4608,512]{2,1,0:T(8,128)(2,1)S(1)} %copy-done, f32[2,512]{1,0:T(2,128)S(1)} %copy-done.1), custom_call_target="tpu_custom_call" | custom-call | tf_op jit(solution)/shard_map/pallas_call | solution.py:28
  20.1 10.9 %all_to_all.10.refs_1_.after.extras = f32[8,16,512]{2,1,0:T(8,128)S(1)} all-to-all(f32[8,16,512]{2,1,0:T(8,128)S(1)} %shard_map.39.refs_1_.packed), channel_id=1, replica_groups={{0,4,8,12,16,20,24,28},{32,36,40,44,48,52,56,60},{64,68,72,76,80,84,88,..., dimensions={0} | all-to-all | bytes 524288 | tf_op jit(solution)/shard_map/all_to_all | solution.py:236
  31.0 0.0 collective-permute-done.4.refs_0_
  31.0 0.0 collective-permute-done.2.refs_0_
  31.0 0.0 collective-permute-start.1
  31.0 0.5 collective-permute-start.3
  31.5 0.5 collective-permute-start.5
  32.1 0.0 collective-permute-start.9
  32.1 2.4 %collective-permute-start.6 = (f32[176,512]{1,0:T(8,128)S(1)}, f32[176,512]{1,0:T(8,128)S(1)}, u32[]{:S(2)}, u32[]{:S(2)}) collective-permute-start(f32[176,512]{1,0:T(8,128)S(1)} %shard_map.46), channel_id=1, source_target_pairs={{0,16},{1,17},{2,18},{3,19},{4,20},{5,21},{6,22},{7,23},{8,24},{9,... | collective-permute-start | bytes 1081352 | tf_op jit(solution)/shard_map/ppermute | solution.py:273
  34.5 0.0 collective-permute-done.1.refs_1_
  34.5 0.7 collective-permute-done.3.refs_3_
  35.2 0.2 shard_map.42
  35.4 7.3 %collective-permute-done.5.refs_0_ = f32[344,512]{1,0:T(8,128)S(1)} collective-permute-done((f32[344,512]{1,0:T(8,128)S(1)}, f32[344,512]{1,0:T(8,128)S(1)}, u32[]{:S(2)}, u32[]{:S(2)}) %collective-permute-start.5) | collective-permute-done | bytes 704544 | tf_op jit(solution)/shard_map/ppermute | solution.py:272
  42.7 0.0 collective-permute-start.7
  42.7 0.7 collective-permute-done.6.refs_0_
  43.5 0.0 collective-permute-start.8
  43.5 0.0 collective-permute-done.9.refs_1_
  43.5 0.1 shard_map.48
  43.6 1.8 %collective-permute-done.8.refs_3_ = f32[176,512]{1,0:T(8,128)S(1)} collective-permute-done((f32[176,512]{1,0:T(8,128)S(1)}, f32[176,512]{1,0:T(8,128)S(1)}, u32[]{:S(2)}, u32[]{:S(2)}) %collective-permute-start.8) | collective-permute-done | bytes 360480 | tf_op jit(solution)/shard_map/ppermute | solution.py:281
  45.4 0.0 collective-permute-done.7.refs_2_
  45.4 0.1 shard_map.49
  45.6 0.7 collective-permute-start.10
  46.2 0.0 collective-permute-done.10.state
  46.3 0.7 collective-permute-start.11
  47.0 0.0 collective-permute-done.11.state
  47.0 0.7 collective-permute-start.12
  47.7 0.0 collective-permute-done.12.state
  47.7 0.2 shard_map.53
  47.9 0.7 collective-permute-start.13
  48.6 0.0 collective-permute-done.13.state
  48.6 0.7 collective-permute-start.14
  49.3 0.0 collective-permute-done.14.state
  49.3 0.7 collective-permute-start.15
  50.0 0.0 collective-permute-done.15.state
  50.0 1.3 %collective-permute-start.16 = (f32[16,512]{1,0:T(8,128)S(1)}, f32[16,512]{1,0:T(8,128)S(1)}, u32[]{:S(2)}, u32[]{:S(2)}) collective-permute-start(f32[16,512]{1,0:T(8,128)S(1)} %get-tuple-element.43), channel_id=1, source_target_pairs={{208,228},{212,224},{216,236},{220,232},{192,244},{196,240},{200,2... | collective-permute-start | bytes 98312 | tf_op jit(solution)/shard_map/ppermute | solution.py:296
  51.3 34.4 %collective-permute-done.16.state = f32[16,512]{1,0:T(8,128)S(1)} collective-permute-done((f32[16,512]{1,0:T(8,128)S(1)}, f32[16,512]{1,0:T(8,128)S(1)}, u32[]{:S(2)}, u32[]{:S(2)}) %collective-permute-start.16) | collective-permute-done | bytes 32800 | tf_op jit(solution)/shard_map/ppermute | solution.py:296
  85.8 1.2 %shard_map.57 = f32[8,16,512]{2,1,0:T(8,128)S(1)} custom-call(f32[16,512]{1,0:T(8,128)S(1)} %collective-permute-done.16.state, bf16[4,512,512]{2,1,0:T(8,128)(2,1)S(1)} %get-tuple-element.25.near, f32[4,8,512]{2,1,0:T(8,128)S(1)} %get-tuple-element.26.refs_1_.near_bias, ...), custom_call_target="tpu_custom_call", output_to_operand_aliasing={{}: (6, {})} | custom-call | tf_op jit(solution)/shard_map/pallas_call | solution.py:28
  86.9 11.9 %all_to_all.11.arrived = f32[8,16,512]{2,1,0:T(8,128)S(1)} all-to-all(f32[8,16,512]{2,1,0:T(8,128)S(1)} %shard_map.57), channel_id=1, replica_groups={{0,4,8,12,16,20,24,28},{32,36,40,44,48,52,56,60},{64,68,72,76,80,84,88,..., dimensions={0} | all-to-all | bytes 524288 | tf_op jit(solution)/shard_map/all_to_all | solution.py:306
  98.8 1.8 %shard_map.58 = f32[2,8,4,4,512]{4,3,2,1,0:T(4,128)} custom-call(f32[8,16,512]{2,1,0:T(8,128)S(1)} %all_to_all.11.arrived, f32[8,16,512]{2,1,0:T(8,128)S(1)} %shard_map.39.refs_1_.packed, bf16[2,4608,512]{2,1,0:T(8,128)(2,1)S(1)} %copy-done, f32[2,512]{1,0:T(2,128)S(1)} %copy-done.1), custom_call_target="tpu_custom_call" | custom-call | tf_op jit(solution)/shard_map/pallas_call | solution.py:28
  (17 shorter events, 0.2 us)
Async XLA Ops:
  0.0 4.6 %copy-start.1 = (f32[2,512]{1,0:T(2,128)S(1)}, f32[2,512]{1,0:T(2,128)}, u32[]{:S(2)}) copy-start(f32[2,512]{1,0:T(2,128)} %biases.7) | copy-start | bytes 12292
  0.0 4.5 %copy-start.2 = (bf16[8,4,4,512]{3,2,1,0:T(4,128)(2,1)S(1)}, bf16[8,4,4,512]{3,2,1,0:T(4,128)(2,1)}, u32[]{:S(2)}) copy-start(bf16[8,4,4,512]{3,2,1,0:T(4,128)(2,1)} %param.3) | copy-start | bytes 393220
  0.0 4.6 %copy-start = (bf16[2,4608,512]{2,1,0:T(8,128)(2,1)S(1)}, bf16[2,4608,512]{2,1,0:T(8,128)(2,1)}, u32[]{:S(2)}) copy-start(bf16[2,4608,512]{2,1,0:T(8,128)(2,1)} %weights.7) | copy-start | bytes 28311556
  1.3 29.7 %collective-permute-start.4 = (f32[520,512]{1,0:T(8,128)S(1)}, f32[520,512]{1,0:T(8,128)S(1)}, u32[]{:S(2)}, u32[]{:S(2)}) collective-permute-start(f32[520,512]{1,0:T(8,128)S(1)} %shard_map.37.refs_0_), channel_id=1, source_target_pairs={{0,16},{1,17},{2,18},{3,19},{4,20},{5,21},{6,22},{7,23},{8,24},{9,... | collective-permute-start | bytes 3194888 | tf_op jit(solution)/shard_map/ppermute | solution.py:219
  2.6 28.4 %collective-permute-start.2 = (f32[520,512]{1,0:T(8,128)S(1)}, f32[520,512]{1,0:T(8,128)S(1)}, u32[]{:S(2)}, u32[]{:S(2)}) collective-permute-start(f32[520,512]{1,0:T(8,128)S(1)} %shard_map.37.refs_0_), channel_id=1, source_target_pairs={{0,8},{1,9},{2,10},{3,11},{4,15},{5,12},{6,13},{7,14},{8,1},{9,2},... | collective-permute-start | bytes 3194888 | tf_op jit(solution)/shard_map/ppermute | solution.py:220
  6.1 12.3 %collective-permute-start = (f32[128,512]{1,0:T(8,128)S(1)}, f32[128,512]{1,0:T(8,128)S(1)}, u32[]{:S(2)}, u32[]{:S(2)}) collective-permute-start(f32[128,512]{1,0:T(8,128)S(1)} %shard_map.38), channel_id=1, source_target_pairs={{0,4},{4,8},{8,12},{12,16},{16,20},{20,24},{24,28},{28,32},{32,36}... | collective-permute-start | bytes 786440 | tf_op jit(solution)/shard_map/ppermute | solution.py:227
  31.0 3.5 %collective-permute-start.1 = (f32[520,512]{1,0:T(8,128)S(1)}, f32[520,512]{1,0:T(8,128)S(1)}, u32[]{:S(2)}, u32[]{:S(2)}) collective-permute-start(f32[520,512]{1,0:T(8,128)S(1)} %shard_map.40.refs_0_), channel_id=1, source_target_pairs={{0,4},{1,5},{2,6},{3,7},{4,0},{5,1},{6,2},{7,3},{8,12},{9,13},{10,... | collective-permute-start | bytes 3194888 | tf_op jit(solution)/shard_map/ppermute | solution.py:275
  31.0 4.2 %collective-permute-start.3 = (f32[520,512]{1,0:T(8,128)S(1)}, f32[520,512]{1,0:T(8,128)S(1)}, u32[]{:S(2)}, u32[]{:S(2)}) collective-permute-start(f32[520,512]{1,0:T(8,128)S(1)} %shard_map.41.refs_2_.whole), channel_id=1, source_target_pairs={{0,4},{1,5},{2,6},{3,7},{4,0},{5,1},{6,2},{7,3},{8,12},{9,13},{10,... | collective-permute-start | bytes 3194888 | tf_op jit(solution)/shard_map/ppermute | solution.py:276
  31.5 11.2 %collective-permute-start.5 = (f32[344,512]{1,0:T(8,128)S(1)}, f32[344,512]{1,0:T(8,128)S(1)}, u32[]{:S(2)}, u32[]{:S(2)}) collective-permute-start(f32[344,512]{1,0:T(8,128)S(1)} %shard_map.44), channel_id=1, source_target_pairs={{0,8},{1,9},{2,10},{3,11},{4,15},{5,12},{6,13},{7,14},{8,1},{9,2},... | collective-permute-start | bytes 2113544 | tf_op jit(solution)/shard_map/ppermute | solution.py:272
  32.1 11.4 %collective-permute-start.9 = (f32[520,512]{1,0:T(8,128)S(1)}, f32[520,512]{1,0:T(8,128)S(1)}, u32[]{:S(2)}, u32[]{:S(2)}) collective-permute-start(f32[520,512]{1,0:T(8,128)S(1)} %shard_map.43.whole.refs_0_), channel_id=1, source_target_pairs={{0,4},{1,5},{2,6},{3,7},{4,0},{5,1},{6,2},{7,3},{8,12},{9,13},{10,... | collective-permute-start | bytes 3194888 | tf_op jit(solution)/shard_map/ppermute | solution.py:277
  32.1 11.4 %collective-permute-start.6 = (f32[176,512]{1,0:T(8,128)S(1)}, f32[176,512]{1,0:T(8,128)S(1)}, u32[]{:S(2)}, u32[]{:S(2)}) collective-permute-start(f32[176,512]{1,0:T(8,128)S(1)} %shard_map.46), channel_id=1, source_target_pairs={{0,16},{1,17},{2,18},{3,19},{4,20},{5,21},{6,22},{7,23},{8,24},{9,... | collective-permute-start | bytes 1081352 | tf_op jit(solution)/shard_map/ppermute | solution.py:273
  42.7 2.7 %collective-permute-start.7 = (f32[344,512]{1,0:T(8,128)S(1)}, f32[344,512]{1,0:T(8,128)S(1)}, u32[]{:S(2)}, u32[]{:S(2)}) collective-permute-start(f32[344,512]{1,0:T(8,128)S(1)} %shard_map.45.refs_0_), channel_id=1, source_target_pairs={{0,4},{1,5},{2,6},{3,7},{4,0},{5,1},{6,2},{7,3},{8,12},{9,13},{10,... | collective-permute-start | bytes 2113544 | tf_op jit(solution)/shard_map/ppermute | solution.py:281
  43.5 1.9 %collective-permute-start.8 = (f32[176,512]{1,0:T(8,128)S(1)}, f32[176,512]{1,0:T(8,128)S(1)}, u32[]{:S(2)}, u32[]{:S(2)}) collective-permute-start(f32[176,512]{1,0:T(8,128)S(1)} %shard_map.47.refs_1_), channel_id=1, source_target_pairs={{0,4},{1,5},{2,6},{3,7},{4,0},{5,1},{6,2},{7,3},{8,12},{9,13},{10,... | collective-permute-start | bytes 1081352 | tf_op jit(solution)/shard_map/ppermute | solution.py:281
  45.6 0.7 collective-permute-start.10
  46.3 0.7 collective-permute-start.11
  47.0 0.7 collective-permute-start.12
  47.9 0.7 collective-permute-start.13
  48.6 0.7 collective-permute-start.14
  49.3 0.7 collective-permute-start.15
  50.0 35.7 %collective-permute-start.16 = (f32[16,512]{1,0:T(8,128)S(1)}, f32[16,512]{1,0:T(8,128)S(1)}, u32[]{:S(2)}, u32[]{:S(2)}) collective-permute-start(f32[16,512]{1,0:T(8,128)S(1)} %get-tuple-element.43), channel_id=1, source_target_pairs={{208,228},{212,224},{216,236},{220,232},{192,244},{196,240},{200,2... | collective-permute-start | bytes 98312 | tf_op jit(solution)/shard_map/ppermute | solution.py:296

commit v5 on v4

--- a/solution.py
+++ b/solution.py
@@ -267,15 +267,14 @@
 
         behind_z = hold(behind_z, packed)
         beside_x = hold(beside_x, packed)
-        held = hold(own, extras)
         corner = [
             lax.ppermute(part(beside_x, 0, CUT, extras), both, behind),
             lax.ppermute(part(behind_z, CUT, channels + PAD, extras), both, beside),
         ]
-        own_twin = lax.ppermute(held, both, twin)
+        own_twin = lax.ppermute(own, both, twin)
         behind_twin = lax.ppermute(behind_z, both, twin)
         beside_twin = lax.ppermute(beside_x, both, twin)
-        near = lowered(0, ([held], [own_twin], [behind_z], [behind_twin]))
+        near = lowered(0, ([own], [own_twin], [behind_z], [behind_twin]))
         far = lowered(0, ([beside_x], [beside_twin]))
         corner = [hold(each, near[1]) for each in corner]
         corner_twin = [lax.ppermute(each, both, twin) for each in corner]

time: 101 us -> 104 us (1.030); the launches traced: 101 us -> 102 us
  blocking collectives: 22.8 us -> 11.9 us
  waiting for transfers between devices: 55.4 us -> 59.7 us
  starting transfers between devices: 13.8 us -> 17.6 us
  Pallas kernels: 8.31 us -> 11.5 us
    all_to_all x1 -> x0, blocking collectives: 10.9 us -> none  [shards(): extras = lax.all_to_all(packed, 'layer', 0, 0, axis_index_groups=teams)]
    ppermute x1, waiting for transfers between devices: 0.01 us -> 5.84 us  [shards(): beside_x = lax.ppermute(own, both, beside)]
    all_to_all x0 -> x1, starting transfers between devices: none -> 3.41 us  [shards(): extras = lax.all_to_all(packed, 'layer', 0, 0, axis_index_groups=teams)]
    pallas_call x22 -> x21, Pallas kernels: 8.31 us -> 11.5 us  [call(): pl.pallas_call(kernel, out_shape=out_shape, in_specs=specs or [VMEM] * le...]
  transfers between devices with their start and end apart: 17 -> 18, of which waited for: 6 -> 7; matrix products, arithmetic and copies ran while one was open for 0% -> 0% of each run, Pallas kernels for 4% -> 6%
where the time goes in v5:
time: 104 us; the launch traced here: 102 us
  waiting for transfers between devices  59.7 us (57%)
  starting transfers between devices  17.6 us (17%)
  blocking collectives  11.9 us (11%)
  Pallas kernels  11.5 us (11%)
    ppermute x7, waiting for transfers between devices, shards(): state = [lax.ppermute(*state, 'layer', pairs)]  33.7 us
    all_to_all x1, blocking collectives, shards(): arrived = lax.all_to_all(starts, 'layer', 0, 0, axis_index_groups=teams)  11.9 us
    pallas_call x21, Pallas kernels, call(): pl.pallas_call(kernel, out_shape=out_shape, in_specs=specs or [VMEM] * le...  11.5 us
    ppermute x1, waiting for transfers between devices, shards(): lax.ppermute(guessed, 'layer', [(i, i + 1) for i in range(blocks - 1)])  10.1 us
    ppermute x1, waiting for transfers between devices, shards(): lax.ppermute(part(beside_x, 0, CUT, extras), both, behind)  6.73 us
    ppermute x1, waiting for transfers between devices, shards(): beside_x = lax.ppermute(own, both, beside)  5.84 us
    ppermute x7, starting transfers between devices, shards(): state = [lax.ppermute(*state, 'layer', pairs)]  5.79 us
    all_to_all x1, starting transfers between devices, shards(): extras = lax.all_to_all(packed, 'layer', 0, 0, axis_index_groups=teams)  3.41 us
  transfers between devices with their start and end apart: 18, of which 7 were waited for; matrix products, arithmetic and copies ran while one was open for 0% of the time, Pallas kernels for 6%

profile of v5, /device:TPU:92, one launch (start us, length us, event | category | flops | bytes accessed | tf_op | source)
XLA Modules:
  0.0 101.9 jit_solution(15598481181740456306)
XLA Ops:
  0.0 1.3 %shard_map.37.refs_0_ = f32[520,512]{1,0:T(8,128)S(1)} custom-call(bf16[2,4608,512]{2,1,0:T(8,128)(2,1)} %weights.7, f32[2,512]{1,0:T(2,128)} %biases.7), custom_call_target="tpu_custom_call" | custom-call | tf_op jit(solution)/shard_map/pallas_call | solution.py:28
  1.3 2.0 %collective-permute-start.1 = (f32[520,512]{1,0:T(8,128)S(1)}, f32[520,512]{1,0:T(8,128)S(1)}, u32[]{:S(2)}, u32[]{:S(2)}) collective-permute-start(f32[520,512]{1,0:T(8,128)S(1)} %shard_map.37.refs_0_), channel_id=1, source_target_pairs={{0,8},{1,9},{2,10},{3,11},{4,15},{5,12},{6,13},{7,14},{8,1},{9,2},... | collective-permute-start | bytes 3194888 | tf_op jit(solution)/shard_map/ppermute | solution.py:220
  3.3 1.2 %collective-permute-start.4 = (f32[520,512]{1,0:T(8,128)S(1)}, f32[520,512]{1,0:T(8,128)S(1)}, u32[]{:S(2)}, u32[]{:S(2)}) collective-permute-start(f32[520,512]{1,0:T(8,128)S(1)} %shard_map.37.refs_0_), channel_id=1, source_target_pairs={{0,16},{1,17},{2,18},{3,19},{4,20},{5,21},{6,22},{7,23},{8,24},{9,... | collective-permute-start | bytes 3194888 | tf_op jit(solution)/shard_map/ppermute | solution.py:219
  4.5 0.1 copy.18
  4.6 0.0 copy-start.1
  4.6 1.5 %shard_map.38 = f32[128,512]{1,0:T(8,128)S(1)} custom-call(f32[128,512]{1,0:T(8,128)S(1)} %bitcast.7, bf16[2,4608,512]{2,1,0:T(8,128)(2,1)S(1)} %copy-done, f32[2,512]{1,0:T(2,128)S(1)} %copy-done.3), custom_call_target="tpu_custom_call" | custom-call | tf_op jit(solution)/shard_map/pallas_call | solution.py:28
  6.1 1.9 %collective-permute-start.2 = (f32[128,512]{1,0:T(8,128)S(1)}, f32[128,512]{1,0:T(8,128)S(1)}, u32[]{:S(2)}, u32[]{:S(2)}) collective-permute-start(f32[128,512]{1,0:T(8,128)S(1)} %shard_map.38), channel_id=1, source_target_pairs={{0,4},{4,8},{8,12},{12,16},{16,20},{20,24},{24,28},{28,32},{32,36}... | collective-permute-start | bytes 786440 | tf_op jit(solution)/shard_map/ppermute | solution.py:227
  8.1 10.1 %collective-permute-done.2.incoming = f32[128,512]{1,0:T(8,128)S(1)} collective-permute-done((f32[128,512]{1,0:T(8,128)S(1)}, f32[128,512]{1,0:T(8,128)S(1)}, u32[]{:S(2)}, u32[]{:S(2)}) %collective-permute-start.2) | collective-permute-done | bytes 262176 | tf_op jit(solution)/shard_map/ppermute | solution.py:227
  18.2 2.3 %shard_map.39.refs_1_.packed = f32[8,16,512]{2,1,0:T(8,128)} custom-call(f32[128,512]{1,0:T(8,128)S(1)} %collective-permute-done.2.incoming, f32[128,512]{1,0:T(8,128)S(1)} %bitcast.8, bf16[2,4608,512]{2,1,0:T(8,128)(2,1)S(1)} %copy-done, f32[2,512]{1,0:T(2,128)S(1)} %copy-done.3), custom_call_target="tpu_custom_call" | custom-call | tf_op jit(solution)/shard_map/pallas_call | solution.py:28
  20.5 3.4 %all-to-all-start = ((f32[8,16,512]{2,1,0:T(8,128)}), f32[8,16,512]{2,1,0:T(8,128)S(1)}, u32[]{:S(2)}, u32[]{:S(2)}) async-start(f32[8,16,512]{2,1,0:T(8,128)} %shard_map.39.refs_1_.packed), calls=%async_computation | async-start | bytes 524288 | tf_op jit(solution)/shard_map/all_to_all | solution.py:236
  23.9 0.4 collective-permute-start
  24.3 0.0 collective-permute-done.1.refs_0_
  24.3 0.2 collective-permute-start.3
  24.5 5.8 %collective-permute-done.4.refs_0_ = f32[520,512]{1,0:T(8,128)S(1)} collective-permute-done((f32[520,512]{1,0:T(8,128)S(1)}, f32[520,512]{1,0:T(8,128)S(1)}, u32[]{:S(2)}, u32[]{:S(2)}) %collective-permute-start.4) | collective-permute-done | bytes 1064992 | tf_op jit(solution)/shard_map/ppermute | solution.py:219
  30.4 0.8 all-to-all-done.after.extras
  31.2 0.4 collective-permute-start.5
  31.6 0.0 collective-permute-start.9
  31.6 2.3 %collective-permute-start.6 = (f32[176,512]{1,0:T(8,128)S(1)}, f32[176,512]{1,0:T(8,128)S(1)}, u32[]{:S(2)}, u32[]{:S(2)}) collective-permute-start(f32[176,512]{1,0:T(8,128)S(1)} %shard_map.45), channel_id=1, source_target_pairs={{0,16},{1,17},{2,18},{3,19},{4,20},{5,21},{6,22},{7,23},{8,24},{9,... | collective-permute-start | bytes 1081352 | tf_op jit(solution)/shard_map/ppermute | solution.py:272
  33.9 0.0 collective-permute-done.refs_1_
  33.9 0.0 collective-permute-done.3.refs_3_
  33.9 1.8 %shard_map.41 = (bf16[4,512,512]{2,1,0:T(8,128)(2,1)S(1)}, f32[4,8,512]{2,1,0:T(8,128)S(1)}) custom-call(f32[520,512]{1,0:T(8,128)S(1)} %shard_map.37.refs_0_, f32[520,512]{1,0:T(8,128)} %collective-permute-done.refs_1_, f32[520,512]{1,0:T(8,128)S(1)} %shard_map.40.refs_2_.whole, f32[520,512]{1,0:T(8,128)} %collective-permute-done.3.refs_3_), custom_call_target="tpu_custom_call" | custom-call | tf_op jit(solution)/shard_map/pallas_call | solution.py:28
  35.7 6.7 %collective-permute-done.5.refs_0_ = f32[344,512]{1,0:T(8,128)S(1)} collective-permute-done((f32[344,512]{1,0:T(8,128)S(1)}, f32[344,512]{1,0:T(8,128)S(1)}, u32[]{:S(2)}, u32[]{:S(2)}) %collective-permute-start.5) | collective-permute-done | bytes 704544 | tf_op jit(solution)/shard_map/ppermute | solution.py:271
  42.4 0.0 collective-permute-start.7
  42.4 0.6 collective-permute-done.6.refs_0_
  43.0 0.1 shard_map.47
  43.1 2.0 %collective-permute-done.8.refs_3_ = f32[176,512]{1,0:T(8,128)S(1)} collective-permute-done((f32[176,512]{1,0:T(8,128)S(1)}, f32[176,512]{1,0:T(8,128)S(1)}, u32[]{:S(2)}, u32[]{:S(2)}) %collective-permute-start.8) | collective-permute-done | bytes 360480 | tf_op jit(solution)/shard_map/ppermute | solution.py:280
  45.1 0.0 collective-permute-done.7.refs_2_
  45.1 0.1 shard_map.48
  45.2 0.8 copy-done.2
  46.0 0.7 collective-permute-start.10
  46.7 0.0 collective-permute-done.10.state
  46.7 0.7 collective-permute-start.11
  47.4 0.0 collective-permute-done.11.state
  47.5 0.7 collective-permute-start.12
  48.1 0.0 collective-permute-done.12.state
  48.1 0.2 shard_map.52
  48.4 0.7 collective-permute-start.13
  49.0 0.0 slice-start
  49.1 0.8 collective-permute-start.14
  49.9 0.0 slice-start.1
  50.0 0.8 collective-permute-start.15
  50.8 0.0 collective-permute-done.15.state
  50.8 0.0 slice-start.2
  50.8 1.6 %collective-permute-start.16 = (f32[16,512]{1,0:T(8,128)S(1)}, f32[16,512]{1,0:T(8,128)S(1)}, u32[]{:S(2)}, u32[]{:S(2)}) collective-permute-start(f32[16,512]{1,0:T(8,128)S(1)} %get-tuple-element.43), channel_id=1, source_target_pairs={{208,228},{212,224},{216,236},{220,232},{192,244},{196,240},{200,2... | collective-permute-start | bytes 98312 | tf_op jit(solution)/shard_map/ppermute | solution.py:295
  52.4 33.7 %collective-permute-done.16.state = f32[16,512]{1,0:T(8,128)S(1)} collective-permute-done((f32[16,512]{1,0:T(8,128)S(1)}, f32[16,512]{1,0:T(8,128)S(1)}, u32[]{:S(2)}, u32[]{:S(2)}) %collective-permute-start.16) | collective-permute-done | bytes 32800 | tf_op jit(solution)/shard_map/ppermute | solution.py:295
  86.0 1.2 %shard_map.56 = f32[8,16,512]{2,1,0:T(8,128)S(1)} custom-call(f32[16,512]{1,0:T(8,128)S(1)} %collective-permute-done.16.state, bf16[4,512,512]{2,1,0:T(8,128)(2,1)S(1)} %get-tuple-element.25.near, f32[4,8,512]{2,1,0:T(8,128)S(1)} %get-tuple-element.26.refs_1_.near_bias, ...), custom_call_target="tpu_custom_call", output_to_operand_aliasing={{}: (6, {})} | custom-call | tf_op jit(solution)/shard_map/pallas_call | solution.py:28
  87.2 11.9 %all_to_all.10.arrived = f32[8,16,512]{2,1,0:T(8,128)S(1)} all-to-all(f32[8,16,512]{2,1,0:T(8,128)S(1)} %shard_map.56), channel_id=1, replica_groups={{0,4,8,12,16,20,24,28},{32,36,40,44,48,52,56,60},{64,68,72,76,80,84,88,..., dimensions={0} | all-to-all | bytes 524288 | tf_op jit(solution)/shard_map/all_to_all | solution.py:305
  99.1 2.8 %shard_map.57 = f32[2,8,4,4,512]{4,3,2,1,0:T(4,128)} custom-call(f32[8,16,512]{2,1,0:T(8,128)S(1)} %all_to_all.10.arrived, f32[8,16,512]{2,1,0:T(8,128)} %shard_map.39.refs_1_.packed, bf16[2,4608,512]{2,1,0:T(8,128)(2,1)S(1)} %bitcast.6, f32[2,512]{1,0:T(2,128)S(1)} %copy-done.3), custom_call_target="tpu_custom_call" | custom-call | tf_op jit(solution)/shard_map/pallas_call | solution.py:28
  (28 shorter events, 0.2 us)
Async XLA Ops:
  0.0 4.6 %copy-start.3 = (f32[2,512]{1,0:T(2,128)S(1)}, f32[2,512]{1,0:T(2,128)}, u32[]{:S(2)}) copy-start(f32[2,512]{1,0:T(2,128)} %biases.7) | copy-start | bytes 12292
  0.0 4.5 %copy-start.4 = (bf16[8,4,4,512]{3,2,1,0:T(4,128)(2,1)S(1)}, bf16[8,4,4,512]{3,2,1,0:T(4,128)(2,1)}, u32[]{:S(2)}) copy-start(bf16[8,4,4,512]{3,2,1,0:T(4,128)(2,1)} %param.3) | copy-start | bytes 393220
  0.0 4.6 %copy-start = (bf16[2,4608,512]{2,1,0:T(8,128)(2,1)S(1)}, bf16[2,4608,512]{2,1,0:T(8,128)(2,1)}, u32[]{:S(2)}) copy-start(bf16[2,4608,512]{2,1,0:T(8,128)(2,1)} %weights.7) | copy-start | bytes 28311556
  1.3 23.0 %collective-permute-start.1 = (f32[520,512]{1,0:T(8,128)S(1)}, f32[520,512]{1,0:T(8,128)S(1)}, u32[]{:S(2)}, u32[]{:S(2)}) collective-permute-start(f32[520,512]{1,0:T(8,128)S(1)} %shard_map.37.refs_0_), channel_id=1, source_target_pairs={{0,8},{1,9},{2,10},{3,11},{4,15},{5,12},{6,13},{7,14},{8,1},{9,2},... | collective-permute-start | bytes 3194888 | tf_op jit(solution)/shard_map/ppermute | solution.py:220
  3.3 27.1 %collective-permute-start.4 = (f32[520,512]{1,0:T(8,128)S(1)}, f32[520,512]{1,0:T(8,128)S(1)}, u32[]{:S(2)}, u32[]{:S(2)}) collective-permute-start(f32[520,512]{1,0:T(8,128)S(1)} %shard_map.37.refs_0_), channel_id=1, source_target_pairs={{0,16},{1,17},{2,18},{3,19},{4,20},{5,21},{6,22},{7,23},{8,24},{9,... | collective-permute-start | bytes 3194888 | tf_op jit(solution)/shard_map/ppermute | solution.py:219
  4.6 13.6 %copy-start.1 = (f32[8,4,4,512]{3,0,2,1:T(8,128)}, f32[8,4,4,512]{3,0,2,1:T(8,128)S(1)}, u32[]{:S(2)}) copy-start(f32[8,4,4,512]{3,0,2,1:T(8,128)S(1)} %copy.18) | copy-start | bytes 786436
  6.1 12.0 %collective-permute-start.2 = (f32[128,512]{1,0:T(8,128)S(1)}, f32[128,512]{1,0:T(8,128)S(1)}, u32[]{:S(2)}, u32[]{:S(2)}) collective-permute-start(f32[128,512]{1,0:T(8,128)S(1)} %shard_map.38), channel_id=1, source_target_pairs={{0,4},{4,8},{8,12},{12,16},{16,20},{20,24},{24,28},{28,32},{32,36}... | collective-permute-start | bytes 786440 | tf_op jit(solution)/shard_map/ppermute | solution.py:227
  20.5 10.7 %all-to-all-start = ((f32[8,16,512]{2,1,0:T(8,128)}), f32[8,16,512]{2,1,0:T(8,128)S(1)}, u32[]{:S(2)}, u32[]{:S(2)}) async-start(f32[8,16,512]{2,1,0:T(8,128)} %shard_map.39.refs_1_.packed), calls=%async_computation | async-start | bytes 524288 | tf_op jit(solution)/shard_map/all_to_all | solution.py:236
  23.9 10.0 %collective-permute-start = (f32[520,512]{1,0:T(8,128)S(1)}, f32[520,512]{1,0:T(8,128)}, u32[]{:S(2)}, u32[]{:S(2)}) collective-permute-start(f32[520,512]{1,0:T(8,128)S(1)} %shard_map.37.refs_0_), channel_id=1, source_target_pairs={{0,4},{1,5},{2,6},{3,7},{4,0},{5,1},{6,2},{7,3},{8,12},{9,13},{10,... | collective-permute-start | bytes 3194888 | tf_op jit(solution)/shard_map/ppermute | solution.py:274
  24.3 9.6 %collective-permute-start.3 = (f32[520,512]{1,0:T(8,128)S(1)}, f32[520,512]{1,0:T(8,128)}, u32[]{:S(2)}, u32[]{:S(2)}) collective-permute-start(f32[520,512]{1,0:T(8,128)S(1)} %shard_map.40.refs_2_.whole), channel_id=1, source_target_pairs={{0,4},{1,5},{2,6},{3,7},{4,0},{5,1},{6,2},{7,3},{8,12},{9,13},{10,... | collective-permute-start | bytes 3194888 | tf_op jit(solution)/shard_map/ppermute | solution.py:275
  31.2 11.2 %collective-permute-start.5 = (f32[344,512]{1,0:T(8,128)S(1)}, f32[344,512]{1,0:T(8,128)S(1)}, u32[]{:S(2)}, u32[]{:S(2)}) collective-permute-start(f32[344,512]{1,0:T(8,128)S(1)} %shard_map.43), channel_id=1, source_target_pairs={{0,8},{1,9},{2,10},{3,11},{4,15},{5,12},{6,13},{7,14},{8,1},{9,2},... | collective-permute-start | bytes 2113544 | tf_op jit(solution)/shard_map/ppermute | solution.py:271
  31.6 11.4 %collective-permute-start.9 = (f32[520,512]{1,0:T(8,128)S(1)}, f32[520,512]{1,0:T(8,128)S(1)}, u32[]{:S(2)}, u32[]{:S(2)}) collective-permute-start(f32[520,512]{1,0:T(8,128)S(1)} %shard_map.42.whole.refs_0_), channel_id=1, source_target_pairs={{0,4},{1,5},{2,6},{3,7},{4,0},{5,1},{6,2},{7,3},{8,12},{9,13},{10,... | collective-permute-start | bytes 3194888 | tf_op jit(solution)/shard_map/ppermute | solution.py:276
  31.6 11.4 %collective-permute-start.6 = (f32[176,512]{1,0:T(8,128)S(1)}, f32[176,512]{1,0:T(8,128)S(1)}, u32[]{:S(2)}, u32[]{:S(2)}) collective-permute-start(f32[176,512]{1,0:T(8,128)S(1)} %shard_map.45), channel_id=1, source_target_pairs={{0,16},{1,17},{2,18},{3,19},{4,20},{5,21},{6,22},{7,23},{8,24},{9,... | collective-permute-start | bytes 1081352 | tf_op jit(solution)/shard_map/ppermute | solution.py:272
  42.4 2.7 %collective-permute-start.7 = (f32[344,512]{1,0:T(8,128)S(1)}, f32[344,512]{1,0:T(8,128)S(1)}, u32[]{:S(2)}, u32[]{:S(2)}) collective-permute-start(f32[344,512]{1,0:T(8,128)S(1)} %shard_map.44.refs_0_), channel_id=1, source_target_pairs={{0,4},{1,5},{2,6},{3,7},{4,0},{5,1},{6,2},{7,3},{8,12},{9,13},{10,... | collective-permute-start | bytes 2113544 | tf_op jit(solution)/shard_map/ppermute | solution.py:280
  43.0 2.1 %collective-permute-start.8 = (f32[176,512]{1,0:T(8,128)S(1)}, f32[176,512]{1,0:T(8,128)S(1)}, u32[]{:S(2)}, u32[]{:S(2)}) collective-permute-start(f32[176,512]{1,0:T(8,128)S(1)} %shard_map.46.refs_1_), channel_id=1, source_target_pairs={{0,4},{1,5},{2,6},{3,7},{4,0},{5,1},{6,2},{7,3},{8,12},{9,13},{10,... | collective-permute-start | bytes 1081352 | tf_op jit(solution)/shard_map/ppermute | solution.py:280
  45.1 1.0 copy-start.2
  46.0 0.7 collective-permute-start.10
  46.7 0.7 collective-permute-start.11
  47.5 0.7 collective-permute-start.12
  48.4 0.7 collective-permute-start.13
  49.0 50.1 %slice-start = ((s8[9437184]{0:T(1024)(128)(4,1)}), s8[4194304]{0:T(1024)(128)(4,1)S(1)}, s32[]{:S(2)}) async-start(s8[9437184]{0:T(1024)(128)(4,1)} %bitcast.5), calls=%async_computation.2 | async-start | bytes 8388608
  49.1 0.8 collective-permute-start.14
  49.9 49.2 %slice-start.1 = ((s8[9437184]{0:T(1024)(128)(4,1)}), s8[4194304]{0:T(1024)(128)(4,1)S(1)}, s32[]{:S(2)}) async-start(s8[9437184]{0:T(1024)(128)(4,1)} %bitcast.5), calls=%async_computation.3 | async-start | bytes 8388608
  50.0 0.8 collective-permute-start.15
  50.8 48.3 %slice-start.2 = ((s8[9437184]{0:T(1024)(128)(4,1)}), s8[1048576]{0:T(1024)(128)(4,1)S(1)}, s32[]{:S(2)}) async-start(s8[9437184]{0:T(1024)(128)(4,1)} %bitcast.5), calls=%async_computation.4 | async-start | bytes 2097152
  50.8 35.2 %collective-permute-start.16 = (f32[16,512]{1,0:T(8,128)S(1)}, f32[16,512]{1,0:T(8,128)S(1)}, u32[]{:S(2)}, u32[]{:S(2)}) collective-permute-start(f32[16,512]{1,0:T(8,128)S(1)} %get-tuple-element.43), channel_id=1, source_target_pairs={{208,228},{212,224},{216,236},{220,232},{192,244},{196,240},{200,2... | collective-permute-start | bytes 98312 | tf_op jit(solution)/shard_map/ppermute | solution.py:295

commit v6 on v4

--- a/solution.py
+++ b/solution.py
@@ -10,7 +10,7 @@
 step_size = 0.25
 GROUP = 8
 PAD = 8
-CUT = 344
+CUT = 352
 FLIPS = (0, 5, 0, 5, 4, 1, 4, 1)
 SIDE = 4
 IMAGES = 8

time: 101 us -> 109 us (1.079)
  waiting for transfers between devices: 55.4 us -> 64.8 us
  blocking collectives: 22.8 us -> 21.5 us
    ppermute x1, waiting for transfers between devices: 0.75 us -> 8.73 us  [shards(): lax.ppermute(part(behind_z, CUT, channels + PAD, extras), both, beside)]
    ppermute x1, waiting for transfers between devices: 0.01 us -> 1.57 us  [shards(): own_twin = lax.ppermute(held, both, twin)]
    all_to_all x1, blocking collectives: 11.9 us -> 10.6 us  [shards(): arrived = lax.all_to_all(starts, 'layer', 0, 0, axis_index_groups=teams)]
  transfers between devices with their start and end apart: 17 -> 17, of which waited for: 6 -> 7; matrix products, arithmetic and copies ran while one was open for 0% -> 0% of each run, Pallas kernels for 4% -> 3%
where the time goes in v6:
time: 109 us
  waiting for transfers between devices  64.8 us (59%)
  blocking collectives  21.5 us (20%)
  starting transfers between devices  14.1 us (13%)
  Pallas kernels  8.31 us (8%)
    ppermute x7, waiting for transfers between devices, shards(): state = [lax.ppermute(*state, 'layer', pairs)]  33.6 us
    all_to_all x1, blocking collectives, shards(): extras = lax.all_to_all(packed, 'layer', 0, 0, axis_index_groups=teams)  10.9 us
    all_to_all x1, blocking collectives, shards(): arrived = lax.all_to_all(starts, 'layer', 0, 0, axis_index_groups=teams)  10.6 us
    ppermute x1, waiting for transfers between devices, shards(): lax.ppermute(guessed, 'layer', [(i, i + 1) for i in range(blocks - 1)])  10.4 us
    ppermute x1, waiting for transfers between devices, shards(): lax.ppermute(part(behind_z, CUT, channels + PAD, extras), both, beside)  8.73 us
    pallas_call x22, Pallas kernels, call(): pl.pallas_call(kernel, out_shape=out_shape, in_specs=specs or [VMEM] * le...  8.31 us
    ppermute x1, waiting for transfers between devices, shards(): lax.ppermute(part(beside_x, 0, CUT, extras), both, behind)  7.51 us
    ppermute x7, starting transfers between devices, shards(): state = [lax.ppermute(*state, 'layer', pairs)]  5.27 us
  transfers between devices with their start and end apart: 17, of which 7 were waited for; matrix products, arithmetic and copies ran while one was open for 0% of the time, Pallas kernels for 3%

profile of v6, /device:TPU:92, one launch (start us, length us, event | category | flops | bytes accessed | tf_op | source)
XLA Modules:
  0.0 109.1 jit_solution(15140220894381052151)
XLA Ops:
  0.0 1.3 %shard_map.37.refs_0_ = f32[520,512]{1,0:T(8,128)S(1)} custom-call(bf16[2,4608,512]{2,1,0:T(8,128)(2,1)} %weights.7, f32[2,512]{1,0:T(2,128)} %biases.7), custom_call_target="tpu_custom_call" | custom-call | tf_op jit(solution)/shard_map/pallas_call | solution.py:28
  1.3 1.3 %collective-permute-start.4 = (f32[520,512]{1,0:T(8,128)S(1)}, f32[520,512]{1,0:T(8,128)S(1)}, u32[]{:S(2)}, u32[]{:S(2)}) collective-permute-start(f32[520,512]{1,0:T(8,128)S(1)} %shard_map.37.refs_0_), channel_id=1, source_target_pairs={{0,16},{1,17},{2,18},{3,19},{4,20},{5,21},{6,22},{7,23},{8,24},{9,... | collective-permute-start | bytes 3194888 | tf_op jit(solution)/shard_map/ppermute | solution.py:219
  2.6 1.9 %collective-permute-start.2 = (f32[520,512]{1,0:T(8,128)S(1)}, f32[520,512]{1,0:T(8,128)S(1)}, u32[]{:S(2)}, u32[]{:S(2)}) collective-permute-start(f32[520,512]{1,0:T(8,128)S(1)} %shard_map.37.refs_0_), channel_id=1, source_target_pairs={{0,8},{1,9},{2,10},{3,11},{4,15},{5,12},{6,13},{7,14},{8,1},{9,2},... | collective-permute-start | bytes 3194888 | tf_op jit(solution)/shard_map/ppermute | solution.py:220
  4.5 0.1 copy.19
  4.6 0.0 copy-done.1
  4.6 0.0 copy-done
  4.6 1.5 %shard_map.38 = f32[128,512]{1,0:T(8,128)S(1)} custom-call(f32[128,512]{1,0:T(8,128)S(1)} %bitcast.5, bf16[2,4608,512]{2,1,0:T(8,128)(2,1)S(1)} %copy-done, f32[2,512]{1,0:T(2,128)S(1)} %copy-done.1), custom_call_target="tpu_custom_call" | custom-call | tf_op jit(solution)/shard_map/pallas_call | solution.py:28
  6.1 1.9 %collective-permute-start = (f32[128,512]{1,0:T(8,128)S(1)}, f32[128,512]{1,0:T(8,128)S(1)}, u32[]{:S(2)}, u32[]{:S(2)}) collective-permute-start(f32[128,512]{1,0:T(8,128)S(1)} %shard_map.38), channel_id=1, source_target_pairs={{0,4},{4,8},{8,12},{12,16},{16,20},{20,24},{24,28},{28,32},{32,36}... | collective-permute-start | bytes 786440 | tf_op jit(solution)/shard_map/ppermute | solution.py:227
  8.1 10.4 %collective-permute-done.incoming = f32[128,512]{1,0:T(8,128)S(1)} collective-permute-done((f32[128,512]{1,0:T(8,128)S(1)}, f32[128,512]{1,0:T(8,128)S(1)}, u32[]{:S(2)}, u32[]{:S(2)}) %collective-permute-start) | collective-permute-done | bytes 262176 | tf_op jit(solution)/shard_map/ppermute | solution.py:227
  18.4 1.6 %shard_map.39.refs_1_.packed = f32[8,16,512]{2,1,0:T(8,128)S(1)} custom-call(f32[128,512]{1,0:T(8,128)S(1)} %collective-permute-done.incoming, f32[128,512]{1,0:T(8,128)S(1)} %bitcast.6, bf16[2,4608,512]{2,1,0:T(8,128)(2,1)S(1)} %copy-done, f32[2,512]{1,0:T(2,128)S(1)} %copy-done.1), custom_call_target="tpu_custom_call" | custom-call | tf_op jit(solution)/shard_map/pallas_call | solution.py:28
  20.1 10.9 %all_to_all.10.refs_1_.after.extras = f32[8,16,512]{2,1,0:T(8,128)S(1)} all-to-all(f32[8,16,512]{2,1,0:T(8,128)S(1)} %shard_map.39.refs_1_.packed), channel_id=1, replica_groups={{0,4,8,12,16,20,24,28},{32,36,40,44,48,52,56,60},{64,68,72,76,80,84,88,..., dimensions={0} | all-to-all | bytes 524288 | tf_op jit(solution)/shard_map/all_to_all | solution.py:236
  31.0 0.0 collective-permute-done.4.refs_0_
  31.0 0.0 collective-permute-done.2.refs_0_
  31.0 0.0 collective-permute-start.1
  31.0 0.5 collective-permute-start.3
  31.5 0.5 collective-permute-start.5
  32.1 0.0 collective-permute-start.9
  32.1 1.6 %collective-permute-done.1.refs_1_ = f32[520,512]{1,0:T(8,128)S(1)} collective-permute-done((f32[520,512]{1,0:T(8,128)S(1)}, f32[520,512]{1,0:T(8,128)S(1)}, u32[]{:S(2)}, u32[]{:S(2)}) %collective-permute-start.1) | collective-permute-done | bytes 1064992 | tf_op jit(solution)/shard_map/ppermute | solution.py:275
  33.7 1.5 %collective-permute-done.3.refs_3_ = f32[520,512]{1,0:T(8,128)S(1)} collective-permute-done((f32[520,512]{1,0:T(8,128)S(1)}, f32[520,512]{1,0:T(8,128)S(1)}, u32[]{:S(2)}, u32[]{:S(2)}) %collective-permute-start.3) | collective-permute-done | bytes 1064992 | tf_op jit(solution)/shard_map/ppermute | solution.py:276
  35.2 0.2 shard_map.42
  35.4 7.5 %collective-permute-done.5.refs_0_ = f32[352,512]{1,0:T(8,128)S(1)} collective-permute-done((f32[352,512]{1,0:T(8,128)S(1)}, f32[352,512]{1,0:T(8,128)S(1)}, u32[]{:S(2)}, u32[]{:S(2)}) %collective-permute-start.5) | collective-permute-done | bytes 720928 | tf_op jit(solution)/shard_map/ppermute | solution.py:272
  42.9 0.0 collective-permute-start.7
  42.9 2.6 %collective-permute-start.6 = (f32[168,512]{1,0:T(8,128)S(1)}, f32[168,512]{1,0:T(8,128)S(1)}, u32[]{:S(2)}, u32[]{:S(2)}) collective-permute-start(f32[168,512]{1,0:T(8,128)S(1)} %shard_map.46), channel_id=1, source_target_pairs={{0,16},{1,17},{2,18},{3,19},{4,20},{5,21},{6,22},{7,23},{8,24},{9,... | collective-permute-start | bytes 1032200 | tf_op jit(solution)/shard_map/ppermute | solution.py:273
  45.6 8.7 %collective-permute-done.6.refs_0_ = f32[168,512]{1,0:T(8,128)S(1)} collective-permute-done((f32[168,512]{1,0:T(8,128)S(1)}, f32[168,512]{1,0:T(8,128)S(1)}, u32[]{:S(2)}, u32[]{:S(2)}) %collective-permute-start.6) | collective-permute-done | bytes 344096 | tf_op jit(solution)/shard_map/ppermute | solution.py:273
  54.3 0.0 collective-permute-start.8
  54.3 0.0 collective-permute-done.9.refs_1_
  54.3 0.1 shard_map.48
  54.4 1.5 %collective-permute-done.8.refs_3_ = f32[168,512]{1,0:T(8,128)S(1)} collective-permute-done((f32[168,512]{1,0:T(8,128)S(1)}, f32[168,512]{1,0:T(8,128)S(1)}, u32[]{:S(2)}, u32[]{:S(2)}) %collective-permute-start.8) | collective-permute-done | bytes 344096 | tf_op jit(solution)/shard_map/ppermute | solution.py:281
  56.0 0.0 collective-permute-done.7.refs_2_
  56.0 0.1 shard_map.49
  56.1 0.7 collective-permute-start.10
  56.8 0.0 collective-permute-done.10.state
  56.8 0.7 collective-permute-start.11
  57.5 0.0 collective-permute-done.11.state
  57.6 0.7 collective-permute-start.12
  58.2 0.0 collective-permute-done.12.state
  58.2 0.2 shard_map.53
  58.5 0.7 collective-permute-start.13
  59.1 0.0 collective-permute-done.13.state
  59.2 0.7 collective-permute-start.14
  59.8 0.0 collective-permute-done.14.state
  59.9 0.7 collective-permute-start.15
  60.6 0.0 collective-permute-done.15.state
  60.6 1.3 %collective-permute-start.16 = (f32[16,512]{1,0:T(8,128)S(1)}, f32[16,512]{1,0:T(8,128)S(1)}, u32[]{:S(2)}, u32[]{:S(2)}) collective-permute-start(f32[16,512]{1,0:T(8,128)S(1)} %get-tuple-element.43), channel_id=1, source_target_pairs={{208,228},{212,224},{216,236},{220,232},{192,244},{196,240},{200,2... | collective-permute-start | bytes 98312 | tf_op jit(solution)/shard_map/ppermute | solution.py:296
  61.9 33.6 %collective-permute-done.16.state = f32[16,512]{1,0:T(8,128)S(1)} collective-permute-done((f32[16,512]{1,0:T(8,128)S(1)}, f32[16,512]{1,0:T(8,128)S(1)}, u32[]{:S(2)}, u32[]{:S(2)}) %collective-permute-start.16) | collective-permute-done | bytes 32800 | tf_op jit(solution)/shard_map/ppermute | solution.py:296
  95.5 1.2 %shard_map.57 = f32[8,16,512]{2,1,0:T(8,128)S(1)} custom-call(f32[16,512]{1,0:T(8,128)S(1)} %collective-permute-done.16.state, bf16[4,512,512]{2,1,0:T(8,128)(2,1)S(1)} %get-tuple-element.25.near, f32[4,8,512]{2,1,0:T(8,128)S(1)} %get-tuple-element.26.refs_1_.near_bias, ...), custom_call_target="tpu_custom_call", output_to_operand_aliasing={{}: (6, {})} | custom-call | tf_op jit(solution)/shard_map/pallas_call | solution.py:28
  96.7 10.6 %all_to_all.11.arrived = f32[8,16,512]{2,1,0:T(8,128)S(1)} all-to-all(f32[8,16,512]{2,1,0:T(8,128)S(1)} %shard_map.57), channel_id=1, replica_groups={{0,4,8,12,16,20,24,28},{32,36,40,44,48,52,56,60},{64,68,72,76,80,84,88,..., dimensions={0} | all-to-all | bytes 524288 | tf_op jit(solution)/shard_map/all_to_all | solution.py:306
  107.2 1.8 %shard_map.58 = f32[2,8,4,4,512]{4,3,2,1,0:T(4,128)} custom-call(f32[8,16,512]{2,1,0:T(8,128)S(1)} %all_to_all.11.arrived, f32[8,16,512]{2,1,0:T(8,128)S(1)} %shard_map.39.refs_1_.packed, bf16[2,4608,512]{2,1,0:T(8,128)(2,1)S(1)} %copy-done, f32[2,512]{1,0:T(2,128)S(1)} %copy-done.1), custom_call_target="tpu_custom_call" | custom-call | tf_op jit(solution)/shard_map/pallas_call | solution.py:28
  (17 shorter events, 0.2 us)
Async XLA Ops:
  0.0 4.6 %copy-start.1 = (f32[2,512]{1,0:T(2,128)S(1)}, f32[2,512]{1,0:T(2,128)}, u32[]{:S(2)}) copy-start(f32[2,512]{1,0:T(2,128)} %biases.7) | copy-start | bytes 12292
  0.0 4.5 %copy-start.2 = (bf16[8,4,4,512]{3,2,1,0:T(4,128)(2,1)S(1)}, bf16[8,4,4,512]{3,2,1,0:T(4,128)(2,1)}, u32[]{:S(2)}) copy-start(bf16[8,4,4,512]{3,2,1,0:T(4,128)(2,1)} %param.3) | copy-start | bytes 393220
  0.0 4.6 %copy-start = (bf16[2,4608,512]{2,1,0:T(8,128)(2,1)S(1)}, bf16[2,4608,512]{2,1,0:T(8,128)(2,1)}, u32[]{:S(2)}) copy-start(bf16[2,4608,512]{2,1,0:T(8,128)(2,1)} %weights.7) | copy-start | bytes 28311556
  1.3 29.7 %collective-permute-start.4 = (f32[520,512]{1,0:T(8,128)S(1)}, f32[520,512]{1,0:T(8,128)S(1)}, u32[]{:S(2)}, u32[]{:S(2)}) collective-permute-start(f32[520,512]{1,0:T(8,128)S(1)} %shard_map.37.refs_0_), channel_id=1, source_target_pairs={{0,16},{1,17},{2,18},{3,19},{4,20},{5,21},{6,22},{7,23},{8,24},{9,... | collective-permute-start | bytes 3194888 | tf_op jit(solution)/shard_map/ppermute | solution.py:219
  2.6 28.4 %collective-permute-start.2 = (f32[520,512]{1,0:T(8,128)S(1)}, f32[520,512]{1,0:T(8,128)S(1)}, u32[]{:S(2)}, u32[]{:S(2)}) collective-permute-start(f32[520,512]{1,0:T(8,128)S(1)} %shard_map.37.refs_0_), channel_id=1, source_target_pairs={{0,8},{1,9},{2,10},{3,11},{4,15},{5,12},{6,13},{7,14},{8,1},{9,2},... | collective-permute-start | bytes 3194888 | tf_op jit(solution)/shard_map/ppermute | solution.py:220
  6.1 12.3 %collective-permute-start = (f32[128,512]{1,0:T(8,128)S(1)}, f32[128,512]{1,0:T(8,128)S(1)}, u32[]{:S(2)}, u32[]{:S(2)}) collective-permute-start(f32[128,512]{1,0:T(8,128)S(1)} %shard_map.38), channel_id=1, source_target_pairs={{0,4},{4,8},{8,12},{12,16},{16,20},{20,24},{24,28},{28,32},{32,36}... | collective-permute-start | bytes 786440 | tf_op jit(solution)/shard_map/ppermute | solution.py:227
  31.0 2.7 %collective-permute-start.1 = (f32[520,512]{1,0:T(8,128)S(1)}, f32[520,512]{1,0:T(8,128)S(1)}, u32[]{:S(2)}, u32[]{:S(2)}) collective-permute-start(f32[520,512]{1,0:T(8,128)S(1)} %shard_map.40.refs_0_), channel_id=1, source_target_pairs={{0,4},{1,5},{2,6},{3,7},{4,0},{5,1},{6,2},{7,3},{8,12},{9,13},{10,... | collective-permute-start | bytes 3194888 | tf_op jit(solution)/shard_map/ppermute | solution.py:275
  31.0 4.2 %collective-permute-start.3 = (f32[520,512]{1,0:T(8,128)S(1)}, f32[520,512]{1,0:T(8,128)S(1)}, u32[]{:S(2)}, u32[]{:S(2)}) collective-permute-start(f32[520,512]{1,0:T(8,128)S(1)} %shard_map.41.refs_2_.whole), channel_id=1, source_target_pairs={{0,4},{1,5},{2,6},{3,7},{4,0},{5,1},{6,2},{7,3},{8,12},{9,13},{10,... | collective-permute-start | bytes 3194888 | tf_op jit(solution)/shard_map/ppermute | solution.py:276
  31.5 11.4 %collective-permute-start.5 = (f32[352,512]{1,0:T(8,128)S(1)}, f32[352,512]{1,0:T(8,128)S(1)}, u32[]{:S(2)}, u32[]{:S(2)}) collective-permute-start(f32[352,512]{1,0:T(8,128)S(1)} %shard_map.44), channel_id=1, source_target_pairs={{0,8},{1,9},{2,10},{3,11},{4,15},{5,12},{6,13},{7,14},{8,1},{9,2},... | collective-permute-start | bytes 2162696 | tf_op jit(solution)/shard_map/ppermute | solution.py:272
  32.1 22.2 %collective-permute-start.9 = (f32[520,512]{1,0:T(8,128)S(1)}, f32[520,512]{1,0:T(8,128)S(1)}, u32[]{:S(2)}, u32[]{:S(2)}) collective-permute-start(f32[520,512]{1,0:T(8,128)S(1)} %shard_map.43.whole.refs_0_), channel_id=1, source_target_pairs={{0,4},{1,5},{2,6},{3,7},{4,0},{5,1},{6,2},{7,3},{8,12},{9,13},{10,... | collective-permute-start | bytes 3194888 | tf_op jit(solution)/shard_map/ppermute | solution.py:277
  42.9 13.1 %collective-permute-start.7 = (f32[352,512]{1,0:T(8,128)S(1)}, f32[352,512]{1,0:T(8,128)S(1)}, u32[]{:S(2)}, u32[]{:S(2)}) collective-permute-start(f32[352,512]{1,0:T(8,128)S(1)} %shard_map.45.refs_0_), channel_id=1, source_target_pairs={{0,4},{1,5},{2,6},{3,7},{4,0},{5,1},{6,2},{7,3},{8,12},{9,13},{10,... | collective-permute-start | bytes 2162696 | tf_op jit(solution)/shard_map/ppermute | solution.py:281
  42.9 11.4 %collective-permute-start.6 = (f32[168,512]{1,0:T(8,128)S(1)}, f32[168,512]{1,0:T(8,128)S(1)}, u32[]{:S(2)}, u32[]{:S(2)}) collective-permute-start(f32[168,512]{1,0:T(8,128)S(1)} %shard_map.46), channel_id=1, source_target_pairs={{0,16},{1,17},{2,18},{3,19},{4,20},{5,21},{6,22},{7,23},{8,24},{9,... | collective-permute-start | bytes 1032200 | tf_op jit(solution)/shard_map/ppermute | solution.py:273
  54.3 1.7 %collective-permute-start.8 = (f32[168,512]{1,0:T(8,128)S(1)}, f32[168,512]{1,0:T(8,128)S(1)}, u32[]{:S(2)}, u32[]{:S(2)}) collective-permute-start(f32[168,512]{1,0:T(8,128)S(1)} %shard_map.47.refs_1_), channel_id=1, source_target_pairs={{0,4},{1,5},{2,6},{3,7},{4,0},{5,1},{6,2},{7,3},{8,12},{9,13},{10,... | collective-permute-start | bytes 1032200 | tf_op jit(solution)/shard_map/ppermute | solution.py:281
  56.1 0.7 collective-permute-start.10
  56.8 0.7 collective-permute-start.11
  57.6 0.7 collective-permute-start.12
  58.5 0.7 collective-permute-start.13
  59.2 0.7 collective-permute-start.14
  59.9 0.7 collective-permute-start.15
  60.6 34.9 %collective-permute-start.16 = (f32[16,512]{1,0:T(8,128)S(1)}, f32[16,512]{1,0:T(8,128)S(1)}, u32[]{:S(2)}, u32[]{:S(2)}) collective-permute-start(f32[16,512]{1,0:T(8,128)S(1)} %get-tuple-element.43), channel_id=1, source_target_pairs={{208,228},{212,224},{216,236},{220,232},{192,244},{196,240},{200,2... | collective-permute-start | bytes 98312 | tf_op jit(solution)/shard_map/ppermute | solution.py:296
